TPU v7x, 32 devices: a whole 2x2x4 slice. The times are simulated.
32 devices in a mesh: grp: 2 (over x), slc: 16 (over z, y, core).
Axes of the slice: x: 2, y: 2, z: 4, core: 2. Of those that a mesh axis runs over, the one named last changes fastest.
Arguments:
- potential: float32 [32, 512, 512], P(('grp', 'slc')), parts along dimension 0, may hold values from -6 to 6
- thickness: int32 [32], P(('grp', 'slc')), parts along dimension 0, may hold values from 1 to 3
- propagator_phase: float32 [128], replicated, may hold values from -3.140625 to 3.140625
- probe: bfloat16 [4, 12, 128, 128], P('grp'), parts along dimension 0, may hold values from -1.1953125 to 1.1953125
- offsets: int32 [2, 2], P('grp'), parts along dimension 0, may hold values from 0 to 384
- measured: float32 [2, 128, 128], P('grp'), parts along dimension 0, may hold values from 0 to 2
Outputs:
- gradient: float32 [32, 512, 512], P(('grp', 'slc')), parts along dimension 0
There are 2 independent parts, one for each index of `grp`. A program takes and returns all parts, laid end to end along the dimension named above; an argument that names none is the same for every part. Nothing has to cross between parts.
Inputs may be any that keep to these rules, and one draw needn't show every extreme that they name: `thickness`: slice thicknesses are whole numbers of base steps. `offsets`: each panel lies inside the object field.
All inputs are finite; a program needn't handle non-finite values.
Results may differ from a plain program's by a relative error of at most 0.0003.
Values sent between devices are 32-bit elements; how exact they have to be, the bound alone decides.
No kernel may reach another device: no remote copies, remote signals or barrier semaphores. Data moves between devices by JAX's collectives and lax.ppermute only.
A program may use at most 64 MiB of HBM per device.

v0:
```python
import math

import jax
import jax.numpy as jnp
from jax import lax
from jax.sharding import PartitionSpec as P

HIGH = lax.Precision.HIGHEST


def shifted(block, axis, distance):
    devices = range(lax.axis_size(axis))
    route = [(i - distance, i) for i in devices if i - distance in devices]
    return lax.ppermute(block, axis, route)


def dft_tables(table_size):
    indices = jnp.arange(table_size, dtype=jnp.int32)
    products = indices[:, None] * indices[None, :] % table_size
    angle_grid = products.astype(jnp.float32) * (2.0 * math.pi / table_size)
    return (jnp.cos(angle_grid), jnp.sin(angle_grid))


def propagator(phase_table, thickness_value, cos_grid, sin_grid):
    table_size = phase_table.shape[0]
    argument = thickness_value.astype(jnp.float32) * phase_table
    filter_real = jnp.cos(argument)
    filter_imag = jnp.sin(argument)
    mixed_real = cos_grid * filter_real[None, :] - sin_grid * filter_imag[None, :]
    mixed_imag = cos_grid * filter_imag[None, :] + sin_grid * filter_real[None, :]
    kernel_real = (
        jnp.dot(mixed_real, cos_grid, precision=HIGH)
        + jnp.dot(mixed_imag, sin_grid, precision=HIGH)
    ) / table_size
    kernel_imag = (
        jnp.dot(mixed_imag, cos_grid, precision=HIGH)
        - jnp.dot(mixed_real, sin_grid, precision=HIGH)
    ) / table_size
    return (kernel_real, kernel_imag)


def product(pattern, left_operand, right_operand):
    return jnp.einsum(
        pattern, left_operand, right_operand, precision=HIGH, preferred_element_type=jnp.float32
    )


def left_apply(pattern, matrix_real, matrix_imag, current):
    real_part = product(pattern, matrix_real, current[0]) - product(
        pattern, matrix_imag, current[1]
    )
    imag_part = product(pattern, matrix_real, current[1]) + product(
        pattern, matrix_imag, current[0]
    )
    return jnp.stack([real_part, imag_part])


def right_apply(pattern, current, matrix_real, matrix_imag):
    real_part = product(pattern, current[0], matrix_real) - product(
        pattern, current[1], matrix_imag
    )
    imag_part = product(pattern, current[1], matrix_real) + product(
        pattern, current[0], matrix_imag
    )
    return jnp.stack([real_part, imag_part])


def propagate(kernel, current):
    half_way = left_apply("ab,mbc->mac", kernel[0], kernel[1], current)
    return right_apply("mab,cb->mac", half_way, kernel[0], kernel[1])


def back_propagate(kernel, current):
    half_way = left_apply("ba,mbc->mac", kernel[0], -kernel[1], current)
    return right_apply("mab,bc->mac", half_way, kernel[0], -kernel[1])


def transmit(patch, current):
    cosine = jnp.cos(patch)
    sine_part = jnp.sin(patch)
    real_part = cosine * current[0] - sine_part * current[1]
    imag_part = cosine * current[1] + sine_part * current[0]
    return jnp.stack([real_part, imag_part])


def untransmit(patch, pulled):
    cosine = jnp.cos(patch)
    sine_part = jnp.sin(patch)
    real_part = cosine * pulled[0] + sine_part * pulled[1]
    imag_part = cosine * pulled[1] - sine_part * pulled[0]
    return jnp.stack([real_part, imag_part])


def sensitivity(pulled, transmitted):
    return jnp.sum(pulled[1] * transmitted[0] - pulled[0] * transmitted[1], axis=0)


def far_field_of(exit_wave, fourier):
    half_way = left_apply("ab,mbc->mac", fourier[0], fourier[1], exit_wave)
    return right_apply("mab,cb->mac", half_way, fourier[0], fourier[1])


def back_from_detector(far_field, misfit, fourier):
    weighted = far_field * misfit[None, None]
    half_back = left_apply("ba,mbc->mac", fourier[0], -fourier[1], weighted)
    return right_apply("mab,bc->mac", half_back, fourier[0], -fourier[1])


def detector(exit_wave, panel_data, fourier):
    far_field = far_field_of(exit_wave, fourier)
    intensity = jnp.sum(far_field[0] * far_field[0] + far_field[1] * far_field[1], axis=0)
    return back_from_detector(far_field, intensity - panel_data, fourier)


def local(potential, thickness, propagator_phase, probe, offsets, measured):
    local_slices = potential.shape[0]
    mode_count = probe.shape[1]
    panel_size = probe.shape[2]
    position_count = offsets.shape[0]
    chain_length = lax.axis_size("slc")
    chain_rank = lax.axis_index("slc")
    cos_grid, sin_grid = dft_tables(panel_size)
    norm_scale = 1.0 / math.sqrt(panel_size)
    fourier = (cos_grid * norm_scale, -sin_grid * norm_scale)
    anchor = jnp.zeros((), jnp.int32)
    probe_wave = probe.astype(jnp.float32)
    block_size = 1
    mode_groups = mode_count // block_size
    work_units = position_count * mode_groups
    kernels = [propagator(propagator_phase, thickness[0], cos_grid, sin_grid)]
    wave_zero = jnp.zeros((2, block_size, panel_size, panel_size), jnp.float32)

    def patches_for(work_unit):
        corner = lax.dynamic_index_in_dim(offsets, work_unit // mode_groups, 0, keepdims=False)
        patches = lax.dynamic_slice(
            potential, (anchor, corner[0], corner[1]), (local_slices, panel_size, panel_size)
        )
        return (patches, corner)

    def forward_tick(step_index, carry):
        incoming, storage, exits = carry
        work_unit = step_index - chain_rank
        working_now = jnp.logical_and(work_unit >= 0, work_unit < work_units)
        bounded = jnp.clip(work_unit, 0, work_units - 1)
        leading = lax.dynamic_slice_in_dim(
            probe_wave, bounded % mode_groups * block_size, block_size, 1
        )
        entering = jnp.where(chain_rank == 0, leading, incoming)
        patches, _ = patches_for(bounded)

        def forward_working():
            current = entering
            stored = [current]
            current = propagate(kernels[0], transmit(patches[0], current))
            return (current, jnp.stack(stored))

        def forward_waiting():
            return (wave_zero, jnp.zeros((local_slices,) + wave_zero.shape, jnp.float32))

        leaving, stored = lax.cond(working_now, forward_working, forward_waiting)
        target = jnp.where(working_now, bounded, work_units)
        storage = lax.dynamic_update_index_in_dim(storage, stored, target, 0)
        exits = lax.dynamic_update_index_in_dim(exits, leaving, target, 0)
        incoming = shifted(leaving, "slc", 1)
        return (incoming, storage, exits)

    storage_empty = jnp.zeros((work_units + 1, local_slices) + wave_zero.shape, jnp.float32)
    exits_empty = jnp.zeros((work_units + 1,) + wave_zero.shape, jnp.float32)
    _, storage, exits = lax.fori_loop(
        0, work_units + chain_length - 1, forward_tick, (wave_zero, storage_empty, exits_empty)
    )

    def detect_all():
        arranged = exits[:work_units].reshape(
            position_count, mode_groups, 2, block_size, panel_size, panel_size
        )
        arranged = arranged.transpose(0, 2, 1, 3, 4, 5).reshape(
            position_count, 2, mode_count, panel_size, panel_size
        )
        adjoints = lax.map(
            lambda inputs: detector(inputs[0], inputs[1], fourier), (arranged, measured)
        )
        adjoints = adjoints.reshape(
            position_count, 2, mode_groups, block_size, panel_size, panel_size
        )
        return adjoints.transpose(0, 2, 1, 3, 4, 5).reshape((work_units,) + wave_zero.shape)

    def skip_all():
        return jnp.zeros((work_units,) + wave_zero.shape, jnp.float32)

    starts = lax.cond(chain_rank == chain_length - 1, detect_all, skip_all)

    def backward_tick(step_index, carry):
        incoming, gradient = carry
        work_unit = step_index - (chain_length - 1 - chain_rank)
        working_now = jnp.logical_and(work_unit >= 0, work_unit < work_units)
        bounded = jnp.clip(work_unit, 0, work_units - 1)
        from_detector = lax.dynamic_index_in_dim(starts, bounded, 0, keepdims=False)
        entering = jnp.where(chain_rank == chain_length - 1, from_detector, incoming)
        stored = lax.dynamic_index_in_dim(storage, bounded, 0, keepdims=False)
        patches, corner = patches_for(bounded)

        def backward_working():
            adjoint = entering
            updates = [None] * local_slices
            for index in reversed(range(local_slices)):
                transmitted = transmit(patches[index], stored[index])
                pulled = back_propagate(kernels[index], adjoint)
                updates[index] = sensitivity(pulled, transmitted)
                adjoint = untransmit(patches[index], pulled)
            return (adjoint, jnp.stack(updates))

        def backward_waiting():
            return (wave_zero, jnp.zeros((local_slices, panel_size, panel_size), jnp.float32))

        leaving, updates = lax.cond(working_now, backward_working, backward_waiting)
        window = lax.dynamic_slice(
            gradient, (anchor, corner[0], corner[1]), (local_slices, panel_size, panel_size)
        )
        gradient = lax.dynamic_update_slice(
            gradient, window + updates, (anchor, corner[0], corner[1])
        )
        incoming = shifted(leaving, "slc", -1)
        return (incoming, gradient)

    gradient_empty = jnp.zeros(potential.shape, jnp.float32)
    _, gradient = lax.fori_loop(
        0, work_units + chain_length - 1, backward_tick, (wave_zero, gradient_empty)
    )
    return gradient


def solution(mesh):
    placed = (
        P(("grp", "slc"), None, None),
        P(("grp", "slc")),
        P(),
        P("grp", None, None, None),
        P("grp", None),
        P("grp", None, None),
    )
    return jax.shard_map(
        local, mesh=mesh, in_specs=placed, out_specs=P(("grp", "slc"), None, None), check_vma=False
    )
```

profile of v0, /device:TPU:0, one launch (start us, length us, event | category | flops | bytes accessed | tf_op | source)
XLA Modules:
  0.0 581.5 jit_solution(11134887940822791852)
XLA Ops:
  11.8 259.9 %while.40 = (s32[]{:T(128)}, f32[2,1,128,128]{3,2,1,0:T(8,128)S(1)}, f32[13,1,2,1,128,128]{5,4,2,3,1,0:T(8,128)}, f32[13,2,1,128,128]{4,3,1,2,0:T(8,128)S(1)}, s...) while((s32[]{:T(128)}, ...), condition=%wide.region_3.4_spmd, body=%wide.region_0.3_spmd.sunk | while | flops 201588736 | bytes 4391856 | solution.py:169
  19.9 5.1 conditional.6
  28.2 5.1 conditional.6
  37.2 5.1 conditional.6
  48.6 5.1 conditional.6
  59.9 5.1 conditional.6
  71.3 5.1 conditional.6
  82.7 5.1 conditional.6
  105.5 5.1 conditional.6
  140.4 9.0 %collective-permute-start = (f32[2,1,128,128]{3,2,1,0:T(8,128)S(1)}, f32[2,1,128,128]{3,2,1,0:T(8,128)S(1)}, u32[]{:S(2)}, u32[]{:S(2)}) collective-permute-start(f32[2,1,128,128]{3,2,1,0:T(8,128)S(1)} %get-tuple-element.1047), channel_id=1, source_target_pairs={{0,1},{1,2},{2,3},{3,4},{4,5},{5,6},{6,7},{7,8},{8,9},{9,10},{10,1... | collective-permute-start | bytes 393224 | tf_op jit(solution)/shard_map/while/body/eval_jaxpr/ppermute | solution.py:14
  158.7 9.0 %collective-permute-start = (f32[2,1,128,128]{3,2,1,0:T(8,128)S(1)}, f32[2,1,128,128]{3,2,1,0:T(8,128)S(1)}, u32[]{:S(2)}, u32[]{:S(2)}) collective-permute-start(f32[2,1,128,128]{3,2,1,0:T(8,128)S(1)} %get-tuple-element.1047), channel_id=1, source_target_pairs={{0,1},{1,2},{2,3},{3,4},{4,5},{5,6},{6,7},{7,8},{8,9},{9,10},{10,1... | collective-permute-start | bytes 393224 | tf_op jit(solution)/shard_map/while/body/eval_jaxpr/ppermute | solution.py:14
  177.1 9.8 %collective-permute-start = (f32[2,1,128,128]{3,2,1,0:T(8,128)S(1)}, f32[2,1,128,128]{3,2,1,0:T(8,128)S(1)}, u32[]{:S(2)}, u32[]{:S(2)}) collective-permute-start(f32[2,1,128,128]{3,2,1,0:T(8,128)S(1)} %get-tuple-element.1047), channel_id=1, source_target_pairs={{0,1},{1,2},{2,3},{3,4},{4,5},{5,6},{6,7},{7,8},{8,9},{9,10},{10,1... | collective-permute-start | bytes 393224 | tf_op jit(solution)/shard_map/while/body/eval_jaxpr/ppermute | solution.py:14
  189.3 5.5 collective-permute-start
  197.2 9.9 %collective-permute-start = (f32[2,1,128,128]{3,2,1,0:T(8,128)S(1)}, f32[2,1,128,128]{3,2,1,0:T(8,128)S(1)}, u32[]{:S(2)}, u32[]{:S(2)}) collective-permute-start(f32[2,1,128,128]{3,2,1,0:T(8,128)S(1)} %get-tuple-element.1047), channel_id=1, source_target_pairs={{0,1},{1,2},{2,3},{3,4},{4,5},{5,6},{6,7},{7,8},{8,9},{9,10},{10,1... | collective-permute-start | bytes 393224 | tf_op jit(solution)/shard_map/while/body/eval_jaxpr/ppermute | solution.py:14
  209.4 5.5 collective-permute-start
  217.3 5.5 collective-permute-start
  225.2 5.5 collective-permute-start
  233.1 5.5 collective-permute-start
  240.9 5.5 collective-permute-start
  248.8 5.5 collective-permute-start
  256.7 5.5 collective-permute-start
  264.6 5.5 collective-permute-start
  273.5 307.0 %while.41 = (s32[]{:T(128)}, f32[2,1,128,128]{3,2,1,0:T(8,128)S(1)}, f32[1,512,512]{2,1,0:T(8,128)S(1)}, s32[]{:T(128)}, f32[1,128,128]{2,1,0:T(8,128)S(1)}, /*i...) while((s32[]{:T(128)}, ...), condition=%wide.region_10.11_spmd, body=%wide.region_7.10_spmd.sunk | while | flops 201785344 | bytes 4260184 | solution.py:227
  378.0 66.5 %collective-permute-done.1 = f32[2,1,128,128]{3,2,1,0:T(8,128)S(1)} collective-permute-done((f32[2,1,128,128]{3,2,1,0:T(8,128)S(1)}, f32[2,1,128,128]{3,2,1,0:T(8,128)S(1)}, u32[]{:S(2)}, u32[]{:S(2)}) %collective-permute-start.1) | collective-permute-done | bytes 131104 | tf_op jit(solution)/shard_map/while/body/eval_jaxpr/ppermute | solution.py:14
  (647 shorter events, 503.8 us)
Async XLA Ops:
  140.4 10.6 %collective-permute-start = (f32[2,1,128,128]{3,2,1,0:T(8,128)S(1)}, f32[2,1,128,128]{3,2,1,0:T(8,128)S(1)}, u32[]{:S(2)}, u32[]{:S(2)}) collective-permute-start(f32[2,1,128,128]{3,2,1,0:T(8,128)S(1)} %get-tuple-element.1047), channel_id=1, source_target_pairs={{0,1},{1,2},{2,3},{3,4},{4,5},{5,6},{6,7},{7,8},{8,9},{9,10},{10,1... | collective-permute-start | bytes 393224 | tf_op jit(solution)/shard_map/while/body/eval_jaxpr/ppermute | solution.py:14
  158.7 10.6 %collective-permute-start = (f32[2,1,128,128]{3,2,1,0:T(8,128)S(1)}, f32[2,1,128,128]{3,2,1,0:T(8,128)S(1)}, u32[]{:S(2)}, u32[]{:S(2)}) collective-permute-start(f32[2,1,128,128]{3,2,1,0:T(8,128)S(1)} %get-tuple-element.1047), channel_id=1, source_target_pairs={{0,1},{1,2},{2,3},{3,4},{4,5},{5,6},{6,7},{7,8},{8,9},{9,10},{10,1... | collective-permute-start | bytes 393224 | tf_op jit(solution)/shard_map/while/body/eval_jaxpr/ppermute | solution.py:14
  177.1 11.4 %collective-permute-start = (f32[2,1,128,128]{3,2,1,0:T(8,128)S(1)}, f32[2,1,128,128]{3,2,1,0:T(8,128)S(1)}, u32[]{:S(2)}, u32[]{:S(2)}) collective-permute-start(f32[2,1,128,128]{3,2,1,0:T(8,128)S(1)} %get-tuple-element.1047), channel_id=1, source_target_pairs={{0,1},{1,2},{2,3},{3,4},{4,5},{5,6},{6,7},{7,8},{8,9},{9,10},{10,1... | collective-permute-start | bytes 393224 | tf_op jit(solution)/shard_map/while/body/eval_jaxpr/ppermute | solution.py:14
  197.2 11.5 %collective-permute-start = (f32[2,1,128,128]{3,2,1,0:T(8,128)S(1)}, f32[2,1,128,128]{3,2,1,0:T(8,128)S(1)}, u32[]{:S(2)}, u32[]{:S(2)}) collective-permute-start(f32[2,1,128,128]{3,2,1,0:T(8,128)S(1)} %get-tuple-element.1047), channel_id=1, source_target_pairs={{0,1},{1,2},{2,3},{3,4},{4,5},{5,6},{6,7},{7,8},{8,9},{9,10},{10,1... | collective-permute-start | bytes 393224 | tf_op jit(solution)/shard_map/while/body/eval_jaxpr/ppermute | solution.py:14
  280.0 7.9 %collective-permute-start.1 = (f32[2,1,128,128]{3,2,1,0:T(8,128)S(1)}, f32[2,1,128,128]{3,2,1,0:T(8,128)S(1)}, u32[]{:S(2)}, u32[]{:S(2)}) collective-permute-start(f32[2,1,128,128]{3,2,1,0:T(8,128)S(1)} %get-tuple-element.1062), channel_id=1, source_target_pairs={{1,0},{2,1},{3,2},{4,3},{5,4},{6,5},{7,6},{8,7},{9,8},{10,9},{11,1... | collective-permute-start | bytes 393224 | tf_op jit(solution)/shard_map/while/body/eval_jaxpr/ppermute | solution.py:14
  294.3 7.9 %collective-permute-start.1 = (f32[2,1,128,128]{3,2,1,0:T(8,128)S(1)}, f32[2,1,128,128]{3,2,1,0:T(8,128)S(1)}, u32[]{:S(2)}, u32[]{:S(2)}) collective-permute-start(f32[2,1,128,128]{3,2,1,0:T(8,128)S(1)} %get-tuple-element.1062), channel_id=1, source_target_pairs={{1,0},{2,1},{3,2},{4,3},{5,4},{6,5},{7,6},{8,7},{9,8},{10,9},{11,1... | collective-permute-start | bytes 393224 | tf_op jit(solution)/shard_map/while/body/eval_jaxpr/ppermute | solution.py:14
  302.3 7.2 %collective-permute-start.1 = (f32[2,1,128,128]{3,2,1,0:T(8,128)S(1)}, f32[2,1,128,128]{3,2,1,0:T(8,128)S(1)}, u32[]{:S(2)}, u32[]{:S(2)}) collective-permute-start(f32[2,1,128,128]{3,2,1,0:T(8,128)S(1)} %get-tuple-element.1062), channel_id=1, source_target_pairs={{1,0},{2,1},{3,2},{4,3},{5,4},{6,5},{7,6},{8,7},{9,8},{10,9},{11,1... | collective-permute-start | bytes 393224 | tf_op jit(solution)/shard_map/while/body/eval_jaxpr/ppermute | solution.py:14
  309.5 7.2 %collective-permute-start.1 = (f32[2,1,128,128]{3,2,1,0:T(8,128)S(1)}, f32[2,1,128,128]{3,2,1,0:T(8,128)S(1)}, u32[]{:S(2)}, u32[]{:S(2)}) collective-permute-start(f32[2,1,128,128]{3,2,1,0:T(8,128)S(1)} %get-tuple-element.1062), channel_id=1, source_target_pairs={{1,0},{2,1},{3,2},{4,3},{5,4},{6,5},{7,6},{8,7},{9,8},{10,9},{11,1... | collective-permute-start | bytes 393224 | tf_op jit(solution)/shard_map/while/body/eval_jaxpr/ppermute | solution.py:14
  316.7 7.2 %collective-permute-start.1 = (f32[2,1,128,128]{3,2,1,0:T(8,128)S(1)}, f32[2,1,128,128]{3,2,1,0:T(8,128)S(1)}, u32[]{:S(2)}, u32[]{:S(2)}) collective-permute-start(f32[2,1,128,128]{3,2,1,0:T(8,128)S(1)} %get-tuple-element.1062), channel_id=1, source_target_pairs={{1,0},{2,1},{3,2},{4,3},{5,4},{6,5},{7,6},{8,7},{9,8},{10,9},{11,1... | collective-permute-start | bytes 393224 | tf_op jit(solution)/shard_map/while/body/eval_jaxpr/ppermute | solution.py:14
  323.9 7.2 %collective-permute-start.1 = (f32[2,1,128,128]{3,2,1,0:T(8,128)S(1)}, f32[2,1,128,128]{3,2,1,0:T(8,128)S(1)}, u32[]{:S(2)}, u32[]{:S(2)}) collective-permute-start(f32[2,1,128,128]{3,2,1,0:T(8,128)S(1)} %get-tuple-element.1062), channel_id=1, source_target_pairs={{1,0},{2,1},{3,2},{4,3},{5,4},{6,5},{7,6},{8,7},{9,8},{10,9},{11,1... | collective-permute-start | bytes 393224 | tf_op jit(solution)/shard_map/while/body/eval_jaxpr/ppermute | solution.py:14
  331.2 7.2 %collective-permute-start.1 = (f32[2,1,128,128]{3,2,1,0:T(8,128)S(1)}, f32[2,1,128,128]{3,2,1,0:T(8,128)S(1)}, u32[]{:S(2)}, u32[]{:S(2)}) collective-permute-start(f32[2,1,128,128]{3,2,1,0:T(8,128)S(1)} %get-tuple-element.1062), channel_id=1, source_target_pairs={{1,0},{2,1},{3,2},{4,3},{5,4},{6,5},{7,6},{8,7},{9,8},{10,9},{11,1... | collective-permute-start | bytes 393224 | tf_op jit(solution)/shard_map/while/body/eval_jaxpr/ppermute | solution.py:14
  338.4 7.2 %collective-permute-start.1 = (f32[2,1,128,128]{3,2,1,0:T(8,128)S(1)}, f32[2,1,128,128]{3,2,1,0:T(8,128)S(1)}, u32[]{:S(2)}, u32[]{:S(2)}) collective-permute-start(f32[2,1,128,128]{3,2,1,0:T(8,128)S(1)} %get-tuple-element.1062), channel_id=1, source_target_pairs={{1,0},{2,1},{3,2},{4,3},{5,4},{6,5},{7,6},{8,7},{9,8},{10,9},{11,1... | collective-permute-start | bytes 393224 | tf_op jit(solution)/shard_map/while/body/eval_jaxpr/ppermute | solution.py:14
  345.6 7.2 %collective-permute-start.1 = (f32[2,1,128,128]{3,2,1,0:T(8,128)S(1)}, f32[2,1,128,128]{3,2,1,0:T(8,128)S(1)}, u32[]{:S(2)}, u32[]{:S(2)}) collective-permute-start(f32[2,1,128,128]{3,2,1,0:T(8,128)S(1)} %get-tuple-element.1062), channel_id=1, source_target_pairs={{1,0},{2,1},{3,2},{4,3},{5,4},{6,5},{7,6},{8,7},{9,8},{10,9},{11,1... | collective-permute-start | bytes 393224 | tf_op jit(solution)/shard_map/while/body/eval_jaxpr/ppermute | solution.py:14
  352.8 7.2 %collective-permute-start.1 = (f32[2,1,128,128]{3,2,1,0:T(8,128)S(1)}, f32[2,1,128,128]{3,2,1,0:T(8,128)S(1)}, u32[]{:S(2)}, u32[]{:S(2)}) collective-permute-start(f32[2,1,128,128]{3,2,1,0:T(8,128)S(1)} %get-tuple-element.1062), channel_id=1, source_target_pairs={{1,0},{2,1},{3,2},{4,3},{5,4},{6,5},{7,6},{8,7},{9,8},{10,9},{11,1... | collective-permute-start | bytes 393224 | tf_op jit(solution)/shard_map/while/body/eval_jaxpr/ppermute | solution.py:14
  360.0 7.2 %collective-permute-start.1 = (f32[2,1,128,128]{3,2,1,0:T(8,128)S(1)}, f32[2,1,128,128]{3,2,1,0:T(8,128)S(1)}, u32[]{:S(2)}, u32[]{:S(2)}) collective-permute-start(f32[2,1,128,128]{3,2,1,0:T(8,128)S(1)} %get-tuple-element.1062), channel_id=1, source_target_pairs={{1,0},{2,1},{3,2},{4,3},{5,4},{6,5},{7,6},{8,7},{9,8},{10,9},{11,1... | collective-permute-start | bytes 393224 | tf_op jit(solution)/shard_map/while/body/eval_jaxpr/ppermute | solution.py:14
  367.3 7.2 %collective-permute-start.1 = (f32[2,1,128,128]{3,2,1,0:T(8,128)S(1)}, f32[2,1,128,128]{3,2,1,0:T(8,128)S(1)}, u32[]{:S(2)}, u32[]{:S(2)}) collective-permute-start(f32[2,1,128,128]{3,2,1,0:T(8,128)S(1)} %get-tuple-element.1062), channel_id=1, source_target_pairs={{1,0},{2,1},{3,2},{4,3},{5,4},{6,5},{7,6},{8,7},{9,8},{10,9},{11,1... | collective-permute-start | bytes 393224 | tf_op jit(solution)/shard_map/while/body/eval_jaxpr/ppermute | solution.py:14
  374.5 70.0 %collective-permute-start.1 = (f32[2,1,128,128]{3,2,1,0:T(8,128)S(1)}, f32[2,1,128,128]{3,2,1,0:T(8,128)S(1)}, u32[]{:S(2)}, u32[]{:S(2)}) collective-permute-start(f32[2,1,128,128]{3,2,1,0:T(8,128)S(1)} %get-tuple-element.1062), channel_id=1, source_target_pairs={{1,0},{2,1},{3,2},{4,3},{5,4},{6,5},{7,6},{8,7},{9,8},{10,9},{11,1... | collective-permute-start | bytes 393224 | tf_op jit(solution)/shard_map/while/body/eval_jaxpr/ppermute | solution.py:14
  448.9 7.2 %collective-permute-start.1 = (f32[2,1,128,128]{3,2,1,0:T(8,128)S(1)}, f32[2,1,128,128]{3,2,1,0:T(8,128)S(1)}, u32[]{:S(2)}, u32[]{:S(2)}) collective-permute-start(f32[2,1,128,128]{3,2,1,0:T(8,128)S(1)} %get-tuple-element.1062), channel_id=1, source_target_pairs={{1,0},{2,1},{3,2},{4,3},{5,4},{6,5},{7,6},{8,7},{9,8},{10,9},{11,1... | collective-permute-start | bytes 393224 | tf_op jit(solution)/shard_map/while/body/eval_jaxpr/ppermute | solution.py:14
  472.2 7.2 %collective-permute-start.1 = (f32[2,1,128,128]{3,2,1,0:T(8,128)S(1)}, f32[2,1,128,128]{3,2,1,0:T(8,128)S(1)}, u32[]{:S(2)}, u32[]{:S(2)}) collective-permute-start(f32[2,1,128,128]{3,2,1,0:T(8,128)S(1)} %get-tuple-element.1062), channel_id=1, source_target_pairs={{1,0},{2,1},{3,2},{4,3},{5,4},{6,5},{7,6},{8,7},{9,8},{10,9},{11,1... | collective-permute-start | bytes 393224 | tf_op jit(solution)/shard_map/while/body/eval_jaxpr/ppermute | solution.py:14
  507.2 7.2 %collective-permute-start.1 = (f32[2,1,128,128]{3,2,1,0:T(8,128)S(1)}, f32[2,1,128,128]{3,2,1,0:T(8,128)S(1)}, u32[]{:S(2)}, u32[]{:S(2)}) collective-permute-start(f32[2,1,128,128]{3,2,1,0:T(8,128)S(1)} %get-tuple-element.1062), channel_id=1, source_target_pairs={{1,0},{2,1},{3,2},{4,3},{5,4},{6,5},{7,6},{8,7},{9,8},{10,9},{11,1... | collective-permute-start | bytes 393224 | tf_op jit(solution)/shard_map/while/body/eval_jaxpr/ppermute | solution.py:14
  518.8 7.2 %collective-permute-start.1 = (f32[2,1,128,128]{3,2,1,0:T(8,128)S(1)}, f32[2,1,128,128]{3,2,1,0:T(8,128)S(1)}, u32[]{:S(2)}, u32[]{:S(2)}) collective-permute-start(f32[2,1,128,128]{3,2,1,0:T(8,128)S(1)} %get-tuple-element.1062), channel_id=1, source_target_pairs={{1,0},{2,1},{3,2},{4,3},{5,4},{6,5},{7,6},{8,7},{9,8},{10,9},{11,1... | collective-permute-start | bytes 393224 | tf_op jit(solution)/shard_map/while/body/eval_jaxpr/ppermute | solution.py:14
  542.1 7.2 %collective-permute-start.1 = (f32[2,1,128,128]{3,2,1,0:T(8,128)S(1)}, f32[2,1,128,128]{3,2,1,0:T(8,128)S(1)}, u32[]{:S(2)}, u32[]{:S(2)}) collective-permute-start(f32[2,1,128,128]{3,2,1,0:T(8,128)S(1)} %get-tuple-element.1062), channel_id=1, source_target_pairs={{1,0},{2,1},{3,2},{4,3},{5,4},{6,5},{7,6},{8,7},{9,8},{10,9},{11,1... | collective-permute-start | bytes 393224 | tf_op jit(solution)/shard_map/while/body/eval_jaxpr/ppermute | solution.py:14
  553.7 7.2 %collective-permute-start.1 = (f32[2,1,128,128]{3,2,1,0:T(8,128)S(1)}, f32[2,1,128,128]{3,2,1,0:T(8,128)S(1)}, u32[]{:S(2)}, u32[]{:S(2)}) collective-permute-start(f32[2,1,128,128]{3,2,1,0:T(8,128)S(1)} %get-tuple-element.1062), channel_id=1, source_target_pairs={{1,0},{2,1},{3,2},{4,3},{5,4},{6,5},{7,6},{8,7},{9,8},{10,9},{11,1... | collective-permute-start | bytes 393224 | tf_op jit(solution)/shard_map/while/body/eval_jaxpr/ppermute | solution.py:14
  565.4 7.2 %collective-permute-start.1 = (f32[2,1,128,128]{3,2,1,0:T(8,128)S(1)}, f32[2,1,128,128]{3,2,1,0:T(8,128)S(1)}, u32[]{:S(2)}, u32[]{:S(2)}) collective-permute-start(f32[2,1,128,128]{3,2,1,0:T(8,128)S(1)} %get-tuple-element.1062), channel_id=1, source_target_pairs={{1,0},{2,1},{3,2},{4,3},{5,4},{6,5},{7,6},{8,7},{9,8},{10,9},{11,1... | collective-permute-start | bytes 393224 | tf_op jit(solution)/shard_map/while/body/eval_jaxpr/ppermute | solution.py:14
  (34 other events, 462.7 us)
where the time goes:
time: 587 us; the launch traced here: 581 us
  starting transfers between devices  178 us (30%)
  waiting for transfers between devices  159 us (27%)
  local copies, waits for them, and re-layouts  131 us (22%)
  matrix products  56.7 us (10%)
  other arithmetic  46.2 us (8%)
    ppermute x54, starting transfers between devices, shifted(): return lax.ppermute(block, axis, route)  178 us
    ppermute x54, waiting for transfers between devices, shifted(): return lax.ppermute(block, axis, route)  159 us
    dynamic_update_slice x27, local copies, waits for them, and re-layouts, backward_tick(): lax.dynamic_update_slice(gradient, window + updates, (anchor, corner[0],...  55.3 us
    dot_general x192, matrix products, product(): jnp.einsum(pattern, left_operand, right_operand, precision=HIGH, preferre...  54.8 us
    dynamic_update_slice x27, local copies, waits for them, and re-layouts, forward_tick(): storage = lax.dynamic_update_index_in_dim(storage, stored, target, 0)  42.3 us
    select_n x12, other arithmetic, forward_tick(): entering = jnp.where(chain_rank == 0, leading, incoming)  19 us
  transfers between devices with their start and end apart: 54, of which 26 were waited for; matrix products, arithmetic and copies ran while one was open for 17% of the time, Pallas kernels for 0%

commit v1 on v0

v1 whole, which is shorter than its diff:
```python
import functools
import math

import jax
import jax.numpy as jnp
from jax import lax
from jax.experimental import pallas as pl
from jax.experimental.pallas import tpu as pltpu
from jax.sharding import PartitionSpec as P

F32 = jnp.float32
BF16 = jnp.bfloat16
CLUSTER = 4
LIMIT = 24 * 2**20
VMEM = pl.BlockSpec(memory_space=pltpu.VMEM)
SMEM = pl.BlockSpec(memory_space=pltpu.SMEM)
ANY = pl.BlockSpec(memory_space=pl.ANY)


def sincos(x):
    turns = jnp.floor(x * (2.0 / math.pi) + 0.5)
    r = x - turns * 1.5703125
    r = r - turns * 4.837512969970703125e-4
    r = r - turns * 7.549789948768648e-8
    r2 = r * r
    s = r + r * r2 * (-1.6666654611e-1 + r2 * (8.3321608736e-3 + r2 * -1.9515295891e-4))
    c = 1.0 - 0.5 * r2 + r2 * r2 * (
        4.166664568298827e-2 + r2 * (-1.388731625493765e-3 + r2 * 2.443315711809948e-5)
    )
    quadrant = turns.astype(jnp.int32)
    odd = (quadrant & 1) == 1
    sine = jnp.where(odd, c, s)
    cosine = jnp.where(odd, s, c)
    sine = jnp.where((quadrant & 2) == 2, -sine, sine)
    cosine = jnp.where(((quadrant + 1) & 2) == 2, -cosine, cosine)
    return cosine, sine


def split(x):
    high = x.astype(BF16)
    return high, (x - high.astype(F32)).astype(BF16)


def dot(a, b):
    return jnp.dot(a, b, preferred_element_type=F32)


def product(x, high, low):
    x_high, x_low = split(x)
    return dot(x_high, high) + dot(x_low, high) + dot(x_high, low)


def turned(x, size):
    return jnp.concatenate([x[:, :size].T, x[:, size:].T], axis=1)


def two_sided(x, high, low, size):
    return product(turned(product(x, high, low), size), high, low)


def window_of(offsets_ref, rows, columns, size):
    row, column = offsets_ref[0, 0], offsets_ref[0, 1]
    row_base = jnp.minimum(row // 8 * 8, rows - size - 8)
    column_base = jnp.minimum(column // 128 * 128, columns - 2 * size)
    return (
        pl.multiple_of(row_base, 8),
        pl.multiple_of(column_base, 128),
        row - row_base,
        column - column_base,
    )


def extract_kernel(offsets_ref, thickness_ref, potential_ref, out_ref, window, sem):
    size = out_ref.shape[1]
    row_base, column_base, down, across = window_of(
        offsets_ref, potential_ref.shape[1], potential_ref.shape[2], size
    )
    copy = pltpu.make_async_copy(
        potential_ref.at[0, pl.ds(row_base, size + 8), pl.ds(column_base, 2 * size)], window, sem
    )
    copy.start()
    out_ref[size:, :] = jnp.full((8, size), thickness_ref[0].astype(F32))
    copy.wait()
    part = pltpu.roll(window[...], lax.rem(size + 8 - down, size + 8), 0)[:size]
    shift = lax.rem(size - across, size)
    left = pltpu.roll(part[:, :size], shift, 1)
    right = pltpu.roll(part[:, size:], shift, 1)
    lane = lax.broadcasted_iota(jnp.int32, (size, size), 1)
    out_ref[:size, :] = jnp.where(lane < size - across, left, right)


def place_kernel(layer_ref, offsets_ref, own_ref, relayed_ref, other_ref, zeros_ref, out_ref, window, sem):
    del zeros_ref
    size = own_ref.shape[1]
    row_base, column_base, down, across = window_of(
        offsets_ref, out_ref.shape[1], out_ref.shape[2], size
    )
    first = jnp.where(layer_ref[0] == 0, own_ref[...], relayed_ref[...])
    update = jnp.concatenate([first + other_ref[...], jnp.zeros((8, size), F32)], axis=0)
    update = pltpu.roll(pltpu.roll(update, down, 0), lax.rem(across, size), 1)
    lane = lax.broadcasted_iota(jnp.int32, (size + 8, size), 1)
    window[:, :size] = jnp.where(lane < across, 0.0, update)
    window[:, size:] = jnp.where(lane < across, update, 0.0)
    copy = pltpu.make_async_copy(
        window, out_ref.at[0, pl.ds(row_base, size + 8), pl.ds(column_base, 2 * size)], sem
    )
    copy.start()
    copy.wait()


def table_kernel(phase_ref, forward_ref, backward_ref):
    size = phase_ref.shape[1]
    rows = lax.broadcasted_iota(jnp.int32, (size, size), 0)
    columns = lax.broadcasted_iota(jnp.int32, (size, size), 1)
    angle = ((rows * columns) % size).astype(F32) * (2.0 * math.pi / size)
    c, s = sincos(angle)
    whole = jnp.concatenate(
        [jnp.concatenate([c, s], axis=1), jnp.concatenate([-s, c], axis=1)], axis=0
    )

    def put(index, real, imag):
        real_turned, imag_turned = real.T, imag.T
        for ref, quarters in (
            (forward_ref, (real, imag, -imag, real)),
            (backward_ref, (real_turned, -imag_turned, imag_turned, real_turned)),
        ):
            for place, quarter in enumerate(quarters):
                r, k = place // 2 * size, place % 2 * size
                high, low = split(quarter)
                ref[index, 0, r : r + size, k : k + size] = high
                ref[index, 1, r : r + size, k : k + size] = low

    for steps in (1, 2, 3):
        h_real, h_imag = sincos(phase_ref[...] * float(steps))
        real = c * h_real + s * h_imag
        imag = c * h_imag - s * h_real
        put(2 + steps, real * (1.0 / math.sqrt(size)), imag * (1.0 / math.sqrt(size)))
        both = jnp.concatenate([real, imag], axis=1)
        k = jnp.dot(both, whole, precision=lax.Precision.HIGHEST, preferred_element_type=F32)
        put(steps - 1, k[:, :size] * (1.0 / size), k[:, size:] * (1.0 / size))


def steps_of(ref, index, size):
    steps = ref[index, size, 0].astype(jnp.int32)
    return jnp.clip(steps, 1, 3) - 1


def forward_kernel(last, place_ref, near_ref, far_ref, table_ref, wave_ref, *refs):
    if last:
        out_ref, sum_ref, stored_ref, cs_ref, patch = refs
    else:
        out_ref, stored_ref, cs_ref, patch = refs
    size = near_ref.shape[2]
    place = place_ref[0]
    patch[0] = near_ref[0]
    patch[2] = near_ref[1]
    patch[1] = far_ref[0]
    patch[3] = far_ref[1]
    modes = out_ref.shape[0]
    waves = [
        wave_ref[m]
        if wave_ref.dtype == F32
        else jnp.concatenate([wave_ref[0, m].astype(F32), wave_ref[1, m].astype(F32)], axis=1)
        for m in range(modes)
    ]
    for index in range(CLUSTER):
        at = index ^ place
        kind = steps_of(patch, at, size)
        if last and index == CLUSTER - 1:
            kind = kind + 3
        cosine, sine = sincos(patch[at, :size, :])
        if index % 2 == 1:
            cosine, sine = cosine.T, sine.T
        cs_ref[index, 0] = cosine
        cs_ref[index, 1] = sine
        slot = jnp.where(index // 2 == place // 2, (index ^ place) & 1, 2)
        high, low = table_ref[kind, 0], table_ref[kind, 1]
        after = []
        for m in range(modes):
            real, imag = waves[m][:, :size], waves[m][:, size:]
            u = jnp.concatenate([cosine * real - sine * imag, cosine * imag + sine * real], axis=1)
            stored_ref[slot, m] = u
            after.append(two_sided(u, high, low, size))
        waves = after
    total = None
    for m in range(modes):
        out_ref[m] = waves[m]
        if last:
            real, imag = waves[m][:, :size], waves[m][:, size:]
            power = real * real + imag * imag
            total = power if total is None else total + power
    if last:
        sum_ref[...] = total


def backward_kernel(last, place_ref, near_ref, far_ref, table_ref, stored_ref, cs_ref, wave_ref, *refs):
    if last:
        mine_ref, theirs_ref, measured_ref, out_ref, own_ref, other_ref, patch, update = refs
    else:
        out_ref, own_ref, other_ref, patch, update = refs
    size = near_ref.shape[2]
    place = place_ref[0]
    patch[0] = near_ref[0, size:, :]
    patch[2] = near_ref[1, size:, :]
    patch[1] = far_ref[0, size:, :]
    patch[3] = far_ref[1, size:, :]
    modes = out_ref.shape[0]
    waves = [wave_ref[m] for m in range(modes)]
    if last:
        misfit = mine_ref[...] + theirs_ref[...] - measured_ref[0]
        misfit = jnp.concatenate([misfit, misfit], axis=1)
        waves = [wave * misfit for wave in waves]
    for index in reversed(range(CLUSTER)):
        at = index ^ place
        kind = steps_of(patch, at, 0)
        if last and index == CLUSTER - 1:
            kind = kind + 3
        cosine, sine = cs_ref[index, 0], cs_ref[index, 1]
        slot = jnp.where(index // 2 == place // 2, (index ^ place) & 1, 2)
        high, low = table_ref[kind, 0], table_ref[kind, 1]
        after = []
        gradient = None
        for m in range(modes):
            mu = two_sided(waves[m], high, low, size)
            real, imag = mu[:, :size], mu[:, size:]
            u = stored_ref[slot, m]
            term = imag * u[:, :size] - real * u[:, size:]
            gradient = term if gradient is None else gradient + term
            after.append(
                jnp.concatenate([cosine * real + sine * imag, cosine * imag - sine * real], axis=1)
            )
        update[slot] = gradient.T if index % 2 == 1 else gradient
        waves = after
    for m in range(modes):
        out_ref[m] = waves[m]
    own_ref[...] = update[0]
    other_ref[...] = update[1]


def shaped(*shape, dtype=F32):
    return jax.ShapeDtypeStruct(shape, dtype)


def call(kernel, ins, outs, scratch=(), flops=0, **more):
    return pl.pallas_call(
        kernel,
        in_specs=ins,
        out_specs=[VMEM] * len(outs),
        out_shape=outs,
        scratch_shapes=list(scratch),
        compiler_params=pltpu.CompilerParams(vmem_limit_bytes=LIMIT),
        cost_estimate=pl.CostEstimate(flops=flops, bytes_accessed=2**20, transcendentals=0),
        **more,
    )


def local(potential, thickness, propagator_phase, probe, offsets, measured):
    size = probe.shape[2]
    modes = probe.shape[1] // 2
    length = lax.axis_size("slc")
    chunks = length // CLUSTER
    rank = lax.axis_index("slc")
    place = (rank % CLUSTER).reshape(1).astype(jnp.int32)
    layer = (rank // CLUSTER).reshape(1).astype(jnp.int32)
    wave = shaped(modes, size, 2 * size)

    def flipped(block, bit):
        return lax.ppermute(block, "slc", [(i, i ^ bit) for i in range(length)])

    def moved(block, layers):
        route = [(i, (i + CLUSTER * layers) % length) for i in range(length)]
        return lax.ppermute(block, "slc", route)

    message = pl.pallas_call(
        extract_kernel,
        in_specs=[SMEM, SMEM, ANY],
        out_specs=VMEM,
        out_shape=shaped(size + 8, size),
        scratch_shapes=[pltpu.VMEM((size + 8, 2 * size), F32), pltpu.SemaphoreType.DMA],
    )(offsets, thickness, potential)
    near = jnp.stack([message, flipped(message, 2)])
    forward_table, backward_table = call(
        table_kernel, [VMEM], [shaped(6, 2, 2 * size, 2 * size, dtype=BF16)] * 2, flops=10**9
    )(propagator_phase.reshape(1, size))
    waves = lax.dynamic_slice_in_dim(probe, (rank % 2) * modes, modes, 1)

    work = CLUSTER * modes * 2 * 3 * 2 * size * (2 * size) ** 2
    nears, fars, kept, tables = [], [], [], []
    power = None
    for chunk in range(chunks):
        last = chunk == chunks - 1
        if chunk > 0:
            near = moved(near, -1)
        far = flipped(near, 1)
        nears.append(near)
        fars.append(far)
        outs = [wave] + ([shaped(size, size)] if last else [])
        outs += [shaped(3, modes, size, 2 * size), shaped(CLUSTER, 2, size, size)]
        results = call(
            functools.partial(forward_kernel, last),
            [SMEM] + [VMEM] * 4,
            outs,
            [pltpu.VMEM((CLUSTER, size + 8, size), F32)],
            work,
        )(place, near, far, forward_table, waves)
        waves = results[0]
        if last:
            power = results[1]
        kept.append(results[-2:])
    extra = (power, flipped(power, 1), measured)
    travelling = None
    for chunk in reversed(range(chunks)):
        last = chunk == chunks - 1
        waves, own, other = call(
            functools.partial(backward_kernel, last),
            [SMEM] + [VMEM] * (9 if last else 6),
            [wave, shaped(size, size), shaped(size, size)],
            [pltpu.VMEM((CLUSTER, 8, size), F32), pltpu.VMEM((3, size, size), F32)],
            work,
        )(place, nears[chunk], fars[chunk], backward_table, *kept[chunk], waves, *(extra if last else ()))
        if chunk > 0:
            fresh = jnp.stack([own, other])
            if travelling is not None:
                fresh = jnp.where(layer[0] == 0, fresh, travelling)
            travelling = moved(fresh, 1)
    if travelling is None:
        travelling = jnp.stack([own, other])
    other = jnp.where(layer[0] == 0, other, travelling[1])
    other = flipped(other, 1)
    return pl.pallas_call(
        place_kernel,
        in_specs=[SMEM, SMEM, VMEM, VMEM, VMEM, ANY],
        out_specs=ANY,
        out_shape=shaped(*potential.shape),
        scratch_shapes=[pltpu.VMEM((size + 8, 2 * size), F32), pltpu.SemaphoreType.DMA],
        input_output_aliases={5: 0},
    )(layer, offsets, own, travelling[0], other, jnp.zeros(potential.shape, F32))


def solution(mesh):
    placed = (
        P(("grp", "slc"), None, None),
        P(("grp", "slc")),
        P(),
        P("grp", None, None, None),
        P("grp", None),
        P("grp", None, None),
    )
    return jax.shard_map(
        local, mesh=mesh, in_specs=placed, out_specs=P(("grp", "slc"), None, None), check_vma=False
    )
```

time: 587 us -> 79.1 us (0.13)
  starting transfers between devices: 178 us -> 15.6 us
  waiting for transfers between devices: 159 us -> 14.6 us
  local copies, waits for them, and re-layouts: 131 us -> 15.2 us
  matrix products: 56.7 us -> 0 us
  other arithmetic: 46.2 us -> 0.95 us
  Pallas kernels: 0 us -> 31.2 us
    ppermute x54 -> x13, starting transfers between devices: 178 us -> 15.6 us  [the longest x6 11.7 us: moved(): return lax.ppermute(block, 'slc', route)]
    ppermute x54 -> x13, waiting for transfers between devices: 159 us -> 14.6 us  [the longest x6 10.5 us: moved(): return lax.ppermute(block, 'slc', route)]
    dynamic_update_slice x81 -> x0, local copies, waits for them, and re-layouts: 97.9 us -> none  [the longest x27 55.3 us: backward_tick(): lax.dynamic_update_slice(gradient, window + updates, (anchor, corner[0],...]
    dot_general x196 -> x0, matrix products: 56.7 us -> none  [the longest x192 54.8 us: product(): jnp.einsum(pattern, left_operand, right_operand, precision=HIGH, preferre...]
    pallas_call x0 -> x11, Pallas kernels: none -> 31.2 us  [the longest x4 13.9 us: local(): call(functools.partial(backward_kernel, last), [SMEM] + [VMEM] * (9 if la...]
    select_n x24 -> x3, other arithmetic: 30 us -> 0.04 us  [the longest x2 0.03 us: local(): fresh = jnp.where(layer[0] == 0, fresh, travelling)]
    unnamed x8 -> x46, local copies, waits for them, and re-layouts: 0.98 us -> 13.5 us
    broadcast_in_dim x65 -> x1, local copies, waits for them, and re-layouts: 12.2 us -> 1.1 us  [local(): jnp.zeros(potential.shape, F32)]
  transfers between devices with their start and end apart: 54 -> 13, of which waited for: 26 -> 7; matrix products, arithmetic and copies ran while one was open for 17% -> 1% of each run, Pallas kernels for 0% -> 26%
where the time goes in v1:
time: 79.1 us; the launch traced here: 78.8 us
  Pallas kernels  31.2 us (39%)
  starting transfers between devices  15.6 us (20%)
  local copies, waits for them, and re-layouts  15.2 us (19%)
  waiting for transfers between devices  14.6 us (18%)
  between operations  1.16 us (1%)
  other arithmetic  0.95 us (1%)
    pallas_call x4, Pallas kernels, local(): call(functools.partial(backward_kernel, last), [SMEM] + [VMEM] * (9 if la...  13.9 us
    unnamed x46, local copies, waits for them, and re-layouts  13.5 us
    pallas_call x4, Pallas kernels, local(): call(functools.partial(forward_kernel, last), [SMEM] + [VMEM] * 4, outs,...  12.4 us
    ppermute x6, starting transfers between devices, moved(): return lax.ppermute(block, 'slc', route)  11.7 us
    ppermute x6, waiting for transfers between devices, moved(): return lax.ppermute(block, 'slc', route)  10.5 us
    ppermute x7, waiting for transfers between devices, flipped(): return lax.ppermute(block, 'slc', [(i, i ^ bit) for i in range(length)])  4.09 us
    ppermute x7, starting transfers between devices, flipped(): return lax.ppermute(block, 'slc', [(i, i ^ bit) for i in range(length)])  3.9 us
    pallas_call x1, Pallas kernels, local(): pl.pallas_call(extract_kernel, in_specs=[SMEM, SMEM, ANY], out_specs=VMEM...  2.35 us
  transfers between devices with their start and end apart: 13, of which 7 were waited for; matrix products, arithmetic and copies ran while one was open for 1% of the time, Pallas kernels for 26%

profile of v1, /device:TPU:0, one launch (start us, length us, event | category | flops | bytes accessed | tf_op | source)
XLA Modules:
  0.0 78.8 jit_solution(17389780489529615626)
XLA Ops:
  0.7 2.3 %shard_map.64 = f32[136,128]{1,0:T(8,128)} custom-call(s32[1,2]{1,0:T(1,128)} %offsets_ref.3, s32[1]{0:T(128)S(6)} %copy.9.thickness_ref, f32[1,512,512]{2,1,0:T(8,128)} %potential_ref.1), custom_call_target="tpu_custom_call" | custom-call | tf_op jit(solution)/shard_map/pallas_call | solution.py:274
  3.1 3.0 %collective-permute-start = (f32[136,128]{1,0:T(8,128)}, f32[136,128]{1,0:T(8,128)S(1)}, u32[]{:S(2)}, u32[]{:S(2)}) collective-permute-start(f32[136,128]{1,0:T(8,128)} %shard_map.64), channel_id=1, source_target_pairs={{0,2},{1,3},{2,0},{3,1},{4,6},{5,7},{6,4},{7,5},{8,10},{9,11},{10,... | collective-permute-start | bytes 208904 | tf_op jit(solution)/shard_map/ppermute | solution.py:268
  6.1 2.5 %collective-permute-done = f32[136,128]{1,0:T(8,128)S(1)} collective-permute-done((f32[136,128]{1,0:T(8,128)}, f32[136,128]{1,0:T(8,128)S(1)}, u32[]{:S(2)}, u32[]{:S(2)}) %collective-permute-start) | collective-permute-done | bytes 69664 | tf_op jit(solution)/shard_map/ppermute | solution.py:268
  9.6 4.2 %collective-permute-start.2 = (f32[2,136,128]{2,1,0:T(8,128)S(1)}, f32[2,136,128]{2,1,0:T(8,128)S(1)}, u32[]{:S(2)}, u32[]{:S(2)}) collective-permute-start(f32[2,136,128]{2,1,0:T(8,128)S(1)} %pad_maximum_fusion.near_ref), channel_id=1, source_target_pairs={{0,12},{1,13},{2,14},{3,15},{4,0},{5,1},{6,2},{7,3},{8,4},{9,5},{1... | collective-permute-start | bytes 417800 | tf_op jit(solution)/shard_map/ppermute | solution.py:272
  17.3 4.3 %collective-permute-start.4 = (f32[2,136,128]{2,1,0:T(8,128)S(1)}, f32[2,136,128]{2,1,0:T(8,128)S(1)}, u32[]{:S(2)}, u32[]{:S(2)}) collective-permute-start(f32[2,136,128]{2,1,0:T(8,128)S(1)} %collective-permute-done.2.near_ref), channel_id=1, source_target_pairs={{0,12},{1,13},{2,14},{3,15},{4,0},{5,1},{6,2},{7,3},{8,4},{9,5},{1... | collective-permute-start | bytes 417800 | tf_op jit(solution)/shard_map/ppermute | solution.py:272
  21.6 3.1 %shard_map.66 = (f32[6,128,256]{2,1,0:T(8,128)S(1)}, f32[3,6,128,256]{3,2,1,0:T(8,128)S(1)}, f32[4,2,128,128]{3,2,1,0:T(8,128)S(1)}) custom-call(s32[1]{0:T(128)} %bitcast.1.place_ref, f32[2,136,128]{2,1,0:T(8,128)S(1)} %pad_maximum_fusion.near_ref, f32[2,136,128]{2,1,0:T(8,128)S(1)} %collective-permute-done.1.far_ref, ...), custom_call_target="tpu_custom_call" | custom-call | flops 2415919104 | bytes 1048576 | tf_op jit(solution)/shard_map/pallas_call | solution.py:299
  24.7 1.4 %copy-done.6 = f32[3,6,128,256]{3,2,1,0:T(8,128)} copy-done((f32[3,6,128,256]{3,2,1,0:T(8,128)}, f32[3,6,128,256]{3,2,1,0:T(8,128)S(1)}, u32[]{:S(2)}) %copy-start.6) | copy-done | bytes 2359320
  26.3 3.1 %collective-permute-start.6 = (f32[2,136,128]{2,1,0:T(8,128)S(1)}, f32[2,136,128]{2,1,0:T(8,128)S(1)}, u32[]{:S(2)}, u32[]{:S(2)}) collective-permute-start(f32[2,136,128]{2,1,0:T(8,128)S(1)} %collective-permute-done.4.near_ref), channel_id=1, source_target_pairs={{0,12},{1,13},{2,14},{3,15},{4,0},{5,1},{6,2},{7,3},{8,4},{9,5},{1... | collective-permute-start | bytes 417800 | tf_op jit(solution)/shard_map/ppermute | solution.py:272
  29.5 3.1 %shard_map.67 = (f32[6,128,256]{2,1,0:T(8,128)S(1)}, f32[3,6,128,256]{3,2,1,0:T(8,128)S(1)}, f32[4,2,128,128]{3,2,1,0:T(8,128)S(1)}) custom-call(s32[1]{0:T(128)} %bitcast.1.place_ref, f32[2,136,128]{2,1,0:T(8,128)S(1)} %collective-permute-done.2.near_ref, f32[2,136,128]{2,1,0:T(8,128)S(1)} %collective-permute-done.3.far_ref, ...), custom_call_target="tpu_custom_call" | custom-call | flops 2415919104 | bytes 1048576 | tf_op jit(solution)/shard_map/pallas_call | solution.py:299
  32.6 1.4 %copy-done.8 = f32[3,6,128,256]{3,2,1,0:T(8,128)} copy-done((f32[3,6,128,256]{3,2,1,0:T(8,128)}, f32[3,6,128,256]{3,2,1,0:T(8,128)S(1)}, u32[]{:S(2)}) %copy-start.8) | copy-done | bytes 2359320
  34.2 3.1 %shard_map.68 = (f32[6,128,256]{2,1,0:T(8,128)S(1)}, f32[3,6,128,256]{3,2,1,0:T(8,128)S(1)}, f32[4,2,128,128]{3,2,1,0:T(8,128)S(1)}) custom-call(s32[1]{0:T(128)} %bitcast.1.place_ref, f32[2,136,128]{2,1,0:T(8,128)S(1)} %collective-permute-done.4.near_ref, f32[2,136,128]{2,1,0:T(8,128)S(1)} %collective-permute-done.5.far_ref, ...), custom_call_target="tpu_custom_call" | custom-call | flops 2415919104 | bytes 1048576 | tf_op jit(solution)/shard_map/pallas_call | solution.py:299
  37.4 1.4 %copy-done.10 = f32[3,6,128,256]{3,2,1,0:T(8,128)} copy-done((f32[3,6,128,256]{3,2,1,0:T(8,128)}, f32[3,6,128,256]{3,2,1,0:T(8,128)S(1)}, u32[]{:S(2)}) %copy-start.10) | copy-done | bytes 2359320
  39.6 1.4 %copy-done.15 = bf16[6,2,256,256]{3,2,1,0:T(8,128)(2,1)S(1)} copy-done((bf16[6,2,256,256]{3,2,1,0:T(8,128)(2,1)S(1)}, bf16[6,2,256,256]{3,2,1,0:T(8,128)(2,1)}, u32[]{:S(2)}) %copy-start.15) | copy-done | bytes 1572888
  41.0 3.1 %shard_map.69 = (f32[6,128,256]{2,1,0:T(8,128)S(1)}, f32[128,128]{1,0:T(8,128)S(1)}, f32[3,6,128,256]{3,2,1,0:T(8,128)S(1)}, f32[4,2,128,128]{3,2,1,0:T(8,128)S(1)}) custom-call(s32[1]{0:T(128)} %bitcast.1.place_ref, f32[2,136,128]{2,1,0:T(8,128)S(1)} %collective-permute-done.6.near_ref, f32[2,136,128]{2,1,0:T(8,128)S(1)} %collective-permute-done.7.far_ref, ...), custom_call_target="tpu_custom_call" | custom-call | flops 2415919104 | bytes 1048576 | tf_op jit(solution)/shard_map/pallas_call | solution.py:299
  44.1 1.4 %copy-done.4 = f32[3,6,128,256]{3,2,1,0:T(8,128)} copy-done((f32[3,6,128,256]{3,2,1,0:T(8,128)}, f32[3,6,128,256]{3,2,1,0:T(8,128)S(1)}, u32[]{:S(2)}) %copy-start.4) | copy-done | bytes 2359320
  46.8 1.7 %copy-done.5 = f32[3,6,128,256]{3,2,1,0:T(8,128)S(1)} copy-done((f32[3,6,128,256]{3,2,1,0:T(8,128)S(1)}, f32[3,6,128,256]{3,2,1,0:T(8,128)}, u32[]{:S(2)}) %copy-start.5) | copy-done | bytes 2359320
  49.9 3.4 %shard_map.70 = (f32[6,128,256]{2,1,0:T(8,128)S(1)}, f32[128,128]{1,0:T(8,128)S(1)}, f32[128,128]{1,0:T(8,128)S(1)}) custom-call(s32[1]{0:T(128)} %bitcast.1.place_ref, f32[2,136,128]{2,1,0:T(8,128)S(1)} %collective-permute-done.6.near_ref, f32[2,136,128]{2,1,0:T(8,128)S(1)} %collective-permute-done.7.far_ref, bf16[6,2,256,256]{3,2,1,0:T(8,128)(2,1)S(1)} %copy-done.13, ...), custom_call_target="tpu_custom_call" | custom-call | flops 2415919104 | bytes 1048576 | tf_op jit(solution)/shard_map/pallas_call | solution.py:314
  53.4 3.2 %shard_map.71 = (f32[6,128,256]{2,1,0:T(8,128)S(1)}, f32[128,128]{1,0:T(8,128)S(1)}, f32[128,128]{1,0:T(8,128)S(1)}) custom-call(s32[1]{0:T(128)} %bitcast.1.place_ref, f32[2,136,128]{2,1,0:T(8,128)S(1)} %collective-permute-done.4.near_ref, f32[2,136,128]{2,1,0:T(8,128)S(1)} %collective-permute-done.5.far_ref, bf16[6,2,256,256]{3,2,1,0:T(8,128)(2,1)S(1)} %copy-done.13, ...), custom_call_target="tpu_custom_call" | custom-call | flops 2415919104 | bytes 1048576 | tf_op jit(solution)/shard_map/pallas_call | solution.py:314
  56.6 4.2 %collective-permute-done.9 = f32[2,128,128]{2,1,0:T(8,128)S(1)} collective-permute-done((f32[2,128,128]{2,1,0:T(8,128)S(1)}, f32[2,128,128]{2,1,0:T(8,128)S(1)}, u32[]{:S(2)}, u32[]{:S(2)}) %collective-permute-start.9) | collective-permute-done | bytes 131104 | tf_op jit(solution)/shard_map/ppermute | solution.py:272
  60.9 3.2 %shard_map.72 = (f32[6,128,256]{2,1,0:T(8,128)S(1)}, f32[128,128]{1,0:T(8,128)S(1)}, f32[128,128]{1,0:T(8,128)S(1)}) custom-call(s32[1]{0:T(128)} %bitcast.1.place_ref, f32[2,136,128]{2,1,0:T(8,128)S(1)} %collective-permute-done.2.near_ref, f32[2,136,128]{2,1,0:T(8,128)S(1)} %collective-permute-done.3.far_ref, bf16[6,2,256,256]{3,2,1,0:T(8,128)(2,1)S(1)} %copy-done.13, ...), custom_call_target="tpu_custom_call" | custom-call | flops 2415919104 | bytes 1048576 | tf_op jit(solution)/shard_map/pallas_call | solution.py:314
  64.1 3.5 %collective-permute-done.10 = f32[2,128,128]{2,1,0:T(8,128)S(1)} collective-permute-done((f32[2,128,128]{2,1,0:T(8,128)S(1)}, f32[2,128,128]{2,1,0:T(8,128)S(1)}, u32[]{:S(2)}, u32[]{:S(2)}) %collective-permute-start.10) | collective-permute-done | bytes 131104 | tf_op jit(solution)/shard_map/ppermute | solution.py:272
  67.7 4.1 %shard_map.73 = (f32[6,128,256]{2,1,0:T(8,128)}, f32[128,128]{1,0:T(8,128)S(1)}, f32[128,128]{1,0:T(8,128)S(1)}) custom-call(s32[1]{0:T(128)} %bitcast.1.place_ref, f32[2,136,128]{2,1,0:T(8,128)S(1)} %pad_maximum_fusion.near_ref, f32[2,136,128]{2,1,0:T(8,128)S(1)} %collective-permute-done.1.far_ref, bf16[6,2,256,256]{3,2,1,0:T(8,128)(2,1)S(1)} %copy-done.13, ...), custom_call_target="tpu_custom_call" | custom-call | flops 2415919104 | bytes 1048576 | tf_op jit(solution)/shard_map/pallas_call | solution.py:314
  72.4 2.0 %collective-permute-done.11 = f32[2,128,128]{2,1,0:T(8,128)S(1)} collective-permute-done((f32[2,128,128]{2,1,0:T(8,128)S(1)}, f32[2,128,128]{2,1,0:T(8,128)S(1)}, u32[]{:S(2)}, u32[]{:S(2)}) %collective-permute-start.11) | collective-permute-done | bytes 131104 | tf_op jit(solution)/shard_map/ppermute | solution.py:272
  76.9 1.7 %shard_map.74 = f32[1,512,512]{2,1,0:T(8,128)} custom-call(s32[1]{0:T(128)} %bitcast.layer_ref, s32[1,2]{1,0:T(1,128)} %offsets_ref.3, f32[128,128]{1,0:T(8,128)} %copy-done.1, f32[128,128]{1,0:T(8,128)} %slice_bitcast_fusion.1.relayed_ref, f32[128,128]{1,0:T(8,128)} %copy-done.22, ...), custom_call_target="tpu_custom_call", output_to_operand_aliasing={{}: (5, {})} | custom-call | tf_op jit(solution)/shard_map/pallas_call | solution.py:330
  (67 shorter events, 11.7 us)
Async XLA Ops:
  0.0 16.5 %copy-start = (bf16[2,12,128,128]{3,2,1,0:T(8,128)(2,1)S(1)}, bf16[2,12,128,128]{3,2,1,0:T(8,128)(2,1)}, u32[]{:S(2)}) copy-start(bf16[2,12,128,128]{3,2,1,0:T(8,128)(2,1)} %param.9) | copy-start | bytes 2359300
  3.1 5.5 %collective-permute-start = (f32[136,128]{1,0:T(8,128)}, f32[136,128]{1,0:T(8,128)S(1)}, u32[]{:S(2)}, u32[]{:S(2)}) collective-permute-start(f32[136,128]{1,0:T(8,128)} %shard_map.64), channel_id=1, source_target_pairs={{0,2},{1,3},{2,0},{3,1},{4,6},{5,7},{6,4},{7,5},{8,10},{9,11},{10,... | collective-permute-start | bytes 208904 | tf_op jit(solution)/shard_map/ppermute | solution.py:268
  9.5 12.1 %collective-permute-start.1 = (f32[2,136,128]{2,1,0:T(8,128)S(1)}, f32[2,136,128]{2,1,0:T(8,128)S(1)}, u32[]{:S(2)}, u32[]{:S(2)}) collective-permute-start(f32[2,136,128]{2,1,0:T(8,128)S(1)} %pad_maximum_fusion.near_ref), channel_id=1, source_target_pairs={{0,1},{1,0},{2,3},{3,2},{4,5},{5,4},{6,7},{7,6},{8,9},{9,8},{10,11... | collective-permute-start | bytes 417800 | tf_op jit(solution)/shard_map/ppermute | solution.py:268
  9.6 7.7 %collective-permute-start.2 = (f32[2,136,128]{2,1,0:T(8,128)S(1)}, f32[2,136,128]{2,1,0:T(8,128)S(1)}, u32[]{:S(2)}, u32[]{:S(2)}) collective-permute-start(f32[2,136,128]{2,1,0:T(8,128)S(1)} %pad_maximum_fusion.near_ref), channel_id=1, source_target_pairs={{0,12},{1,13},{2,14},{3,15},{4,0},{5,1},{6,2},{7,3},{8,4},{9,5},{1... | collective-permute-start | bytes 417800 | tf_op jit(solution)/shard_map/ppermute | solution.py:272
  16.5 17.8 %copy-start.14 = (bf16[6,2,256,256]{3,2,1,0:T(8,128)(2,1)}, bf16[6,2,256,256]{3,2,1,0:T(8,128)(2,1)S(1)}, u32[]{:S(2)}) copy-start(bf16[6,2,256,256]{3,2,1,0:T(8,128)(2,1)S(1)} %get-tuple-element.32.table_ref) | copy-start | bytes 4718596
  17.3 12.2 %collective-permute-start.3 = (f32[2,136,128]{2,1,0:T(8,128)S(1)}, f32[2,136,128]{2,1,0:T(8,128)S(1)}, u32[]{:S(2)}, u32[]{:S(2)}) collective-permute-start(f32[2,136,128]{2,1,0:T(8,128)S(1)} %collective-permute-done.2.near_ref), channel_id=1, source_target_pairs={{0,1},{1,0},{2,3},{3,2},{4,5},{5,4},{6,7},{7,6},{8,9},{9,8},{10,11... | collective-permute-start | bytes 417800 | tf_op jit(solution)/shard_map/ppermute | solution.py:268
  17.3 8.8 %collective-permute-start.4 = (f32[2,136,128]{2,1,0:T(8,128)S(1)}, f32[2,136,128]{2,1,0:T(8,128)S(1)}, u32[]{:S(2)}, u32[]{:S(2)}) collective-permute-start(f32[2,136,128]{2,1,0:T(8,128)S(1)} %collective-permute-done.2.near_ref), channel_id=1, source_target_pairs={{0,12},{1,13},{2,14},{3,15},{4,0},{5,1},{6,2},{7,3},{8,4},{9,5},{1... | collective-permute-start | bytes 417800 | tf_op jit(solution)/shard_map/ppermute | solution.py:272
  26.1 6.5 %copy-start.16 = (f32[4,2,128,128]{3,2,1,0:T(8,128)}, f32[4,2,128,128]{3,2,1,0:T(8,128)S(1)}, u32[]{:S(2)}) copy-start(f32[4,2,128,128]{3,2,1,0:T(8,128)S(1)} %get-tuple-element.34.cs_ref) | copy-start | bytes 1572868
  26.1 8.1 %collective-permute-start.5 = (f32[2,136,128]{2,1,0:T(8,128)S(1)}, f32[2,136,128]{2,1,0:T(8,128)S(1)}, u32[]{:S(2)}, u32[]{:S(2)}) collective-permute-start(f32[2,136,128]{2,1,0:T(8,128)S(1)} %collective-permute-done.4.near_ref), channel_id=1, source_target_pairs={{0,1},{1,0},{2,3},{3,2},{4,5},{5,4},{6,7},{7,6},{8,9},{9,8},{10,11... | collective-permute-start | bytes 417800 | tf_op jit(solution)/shard_map/ppermute | solution.py:268
  26.3 7.7 %collective-permute-start.6 = (f32[2,136,128]{2,1,0:T(8,128)S(1)}, f32[2,136,128]{2,1,0:T(8,128)S(1)}, u32[]{:S(2)}, u32[]{:S(2)}) collective-permute-start(f32[2,136,128]{2,1,0:T(8,128)S(1)} %collective-permute-done.4.near_ref), channel_id=1, source_target_pairs={{0,12},{1,13},{2,14},{3,15},{4,0},{5,1},{6,2},{7,3},{8,4},{9,5},{1... | collective-permute-start | bytes 417800 | tf_op jit(solution)/shard_map/ppermute | solution.py:272
  34.0 3.3 %copy-start.18 = (f32[4,2,128,128]{3,2,1,0:T(8,128)}, f32[4,2,128,128]{3,2,1,0:T(8,128)S(1)}, u32[]{:S(2)}) copy-start(f32[4,2,128,128]{3,2,1,0:T(8,128)S(1)} %get-tuple-element.37.cs_ref) | copy-start | bytes 1572868
  34.0 5.6 %collective-permute-start.7 = (f32[2,136,128]{2,1,0:T(8,128)S(1)}, f32[2,136,128]{2,1,0:T(8,128)S(1)}, u32[]{:S(2)}, u32[]{:S(2)}) collective-permute-start(f32[2,136,128]{2,1,0:T(8,128)S(1)} %collective-permute-done.6.near_ref), channel_id=1, source_target_pairs={{0,1},{1,0},{2,3},{3,2},{4,5},{5,4},{6,7},{7,6},{8,9},{9,8},{10,11... | collective-permute-start | bytes 417800 | tf_op jit(solution)/shard_map/ppermute | solution.py:268
  41.0 5.8 %copy-start.2 = (f32[1,128,128]{2,1,0:T(8,128)S(1)}, f32[1,128,128]{2,1,0:T(8,128)}, u32[]{:S(2)}) copy-start(f32[1,128,128]{2,1,0:T(8,128)} %refs_2_.1) | copy-start | bytes 196612
  45.5 1.3 %collective-permute-start.8 = (f32[128,128]{1,0:T(8,128)S(1)}, f32[128,128]{1,0:T(8,128)S(1)}, u32[]{:S(2)}, u32[]{:S(2)}) collective-permute-start(f32[128,128]{1,0:T(8,128)S(1)} %get-tuple-element.45.refs_0_), channel_id=1, source_target_pairs={{0,1},{1,0},{2,3},{3,2},{4,5},{5,4},{6,7},{7,6},{8,9},{9,8},{10,11... | collective-permute-start | bytes 196616 | tf_op jit(solution)/shard_map/ppermute | solution.py:268
  49.9 3.5 %copy-start.11 = (f32[3,6,128,256]{3,2,1,0:T(8,128)S(1)}, f32[3,6,128,256]{3,2,1,0:T(8,128)}, u32[]{:S(2)}) copy-start(f32[3,6,128,256]{3,2,1,0:T(8,128)} %copy-done.10) | copy-start | bytes 7077892
  49.9 3.5 %copy-start.21 = (f32[4,2,128,128]{3,2,1,0:T(8,128)S(1)}, f32[4,2,128,128]{3,2,1,0:T(8,128)}, u32[]{:S(2)}) copy-start(f32[4,2,128,128]{3,2,1,0:T(8,128)} %copy-done.20) | copy-start | bytes 1572868
  53.3 7.5 %collective-permute-start.9 = (f32[2,128,128]{2,1,0:T(8,128)S(1)}, f32[2,128,128]{2,1,0:T(8,128)S(1)}, u32[]{:S(2)}, u32[]{:S(2)}) collective-permute-start(f32[2,128,128]{2,1,0:T(8,128)S(1)} %pad_maximum_fusion.1), channel_id=1, source_target_pairs={{0,4},{1,5},{2,6},{3,7},{4,8},{5,9},{6,10},{7,11},{8,12},{9,13},{1... | collective-permute-start | bytes 393224 | tf_op jit(solution)/shard_map/ppermute | solution.py:272
  53.4 7.5 %copy-start.9 = (f32[3,6,128,256]{3,2,1,0:T(8,128)S(1)}, f32[3,6,128,256]{3,2,1,0:T(8,128)}, u32[]{:S(2)}) copy-start(f32[3,6,128,256]{3,2,1,0:T(8,128)} %copy-done.8) | copy-start | bytes 7077892
  53.4 7.5 %copy-start.19 = (f32[4,2,128,128]{3,2,1,0:T(8,128)S(1)}, f32[4,2,128,128]{3,2,1,0:T(8,128)}, u32[]{:S(2)}) copy-start(f32[4,2,128,128]{3,2,1,0:T(8,128)} %copy-done.18) | copy-start | bytes 1572868
  60.8 6.8 %collective-permute-start.10 = (f32[2,128,128]{2,1,0:T(8,128)S(1)}, f32[2,128,128]{2,1,0:T(8,128)S(1)}, u32[]{:S(2)}, u32[]{:S(2)}) collective-permute-start(f32[2,128,128]{2,1,0:T(8,128)S(1)} %maximum_select_fusion.1), channel_id=1, source_target_pairs={{0,4},{1,5},{2,6},{3,7},{4,8},{5,9},{6,10},{7,11},{8,12},{9,13},{1... | collective-permute-start | bytes 393224 | tf_op jit(solution)/shard_map/ppermute | solution.py:272
  60.9 6.8 %copy-start.7 = (f32[3,6,128,256]{3,2,1,0:T(8,128)S(1)}, f32[3,6,128,256]{3,2,1,0:T(8,128)}, u32[]{:S(2)}) copy-start(f32[3,6,128,256]{3,2,1,0:T(8,128)} %copy-done.6) | copy-start | bytes 7077892
  60.9 6.8 %copy-start.17 = (f32[4,2,128,128]{3,2,1,0:T(8,128)S(1)}, f32[4,2,128,128]{3,2,1,0:T(8,128)}, u32[]{:S(2)}) copy-start(f32[4,2,128,128]{3,2,1,0:T(8,128)} %copy-done.16) | copy-start | bytes 1572868
  67.7 6.8 %collective-permute-start.11 = (f32[2,128,128]{2,1,0:T(8,128)S(1)}, f32[2,128,128]{2,1,0:T(8,128)S(1)}, u32[]{:S(2)}, u32[]{:S(2)}) collective-permute-start(f32[2,128,128]{2,1,0:T(8,128)S(1)} %maximum_select_fusion), channel_id=1, source_target_pairs={{0,4},{1,5},{2,6},{3,7},{4,8},{5,9},{6,10},{7,11},{8,12},{9,13},{1... | collective-permute-start | bytes 393224 | tf_op jit(solution)/shard_map/ppermute | solution.py:272
  74.5 1.3 %collective-permute-start.12 = (f32[128,128]{1,0:T(8,128)S(1)}, f32[128,128]{1,0:T(8,128)S(1)}, u32[]{:S(2)}, u32[]{:S(2)}) collective-permute-start(f32[128,128]{1,0:T(8,128)S(1)} %fusion), channel_id=1, source_target_pairs={{0,1},{1,0},{2,3},{3,2},{4,5},{5,4},{6,7},{7,6},{8,9},{9,8},{10,11... | collective-permute-start | bytes 196616 | tf_op jit(solution)/shard_map/ppermute | solution.py:268
  (12 other events, 14.6 us)

commit v2 on v1

v2 whole, which is shorter than its diff:
```python
import functools
import math

import jax
import jax.numpy as jnp
from jax import lax
from jax.experimental import pallas as pl
from jax.experimental.pallas import tpu as pltpu
from jax.sharding import PartitionSpec as P

F32 = jnp.float32
BF16 = jnp.bfloat16
CLUSTER = 4
LIMIT = 12 * 2**20
VMEM = pl.BlockSpec(memory_space=pltpu.VMEM)
SMEM = pl.BlockSpec(memory_space=pltpu.SMEM)
HBM = pl.BlockSpec(memory_space=pltpu.HBM)
ANY = pl.BlockSpec(memory_space=pl.ANY)


def sincos(x):
    turns = jnp.floor(x * (2.0 / math.pi) + 0.5)
    r = x - turns * 1.5703125
    r = r - turns * 4.837512969970703125e-4
    r = r - turns * 7.549789948768648e-8
    r2 = r * r
    s = r + r * r2 * (-1.6666654611e-1 + r2 * (8.3321608736e-3 + r2 * -1.9515295891e-4))
    c = 1.0 - 0.5 * r2 + r2 * r2 * (
        4.166664568298827e-2 + r2 * (-1.388731625493765e-3 + r2 * 2.443315711809948e-5)
    )
    quadrant = turns.astype(jnp.int32)
    odd = (quadrant & 1) == 1
    sine = jnp.where(odd, c, s)
    cosine = jnp.where(odd, s, c)
    sine = jnp.where((quadrant & 2) == 2, -sine, sine)
    cosine = jnp.where(((quadrant + 1) & 2) == 2, -cosine, cosine)
    return cosine, sine


def split(x):
    high = x.astype(BF16)
    return high, (x - high.astype(F32)).astype(BF16)


def dot(a, b):
    return jnp.dot(a, b, preferred_element_type=F32)


def product(x, high, low):
    x_high, x_low = split(x)
    return dot(x_high, high) + dot(x_low, high) + dot(x_high, low)


def turned(x, size):
    return jnp.concatenate([x[:, :size].T, x[:, size:].T], axis=1)


def two_sided(x, high, low, size):
    return product(turned(product(x, high, low), size), high, low)


def window_of(offsets_ref, rows, columns, size):
    row, column = offsets_ref[0, 0], offsets_ref[0, 1]
    row_base = jnp.minimum(row // 8 * 8, rows - size - 8)
    column_base = jnp.minimum(column // 128 * 128, columns - 2 * size)
    return (
        pl.multiple_of(row_base, 8),
        pl.multiple_of(column_base, 128),
        row - row_base,
        column - column_base,
    )


def extract_kernel(offsets_hbm, thickness_hbm, potential_ref, out_ref, window, offsets_ref, thickness_ref, sems):
    size = out_ref.shape[1]
    corner = pltpu.make_async_copy(offsets_hbm, offsets_ref, sems.at[0])
    steps = pltpu.make_async_copy(thickness_hbm, thickness_ref, sems.at[1])
    corner.start()
    steps.start()
    corner.wait()
    row_base, column_base, down, across = window_of(
        offsets_ref, potential_ref.shape[1], potential_ref.shape[2], size
    )
    copy = pltpu.make_async_copy(
        potential_ref.at[0, pl.ds(row_base, size + 8), pl.ds(column_base, 2 * size)], window, sems.at[2]
    )
    copy.start()
    steps.wait()
    out_ref[size:, :] = jnp.full((8, size), thickness_ref[0].astype(F32))
    copy.wait()
    part = pltpu.roll(window[...], lax.rem(size + 8 - down, size + 8), 0)[:size]
    shift = lax.rem(size - across, size)
    left = pltpu.roll(part[:, :size], shift, 1)
    right = pltpu.roll(part[:, size:], shift, 1)
    lane = lax.broadcasted_iota(jnp.int32, (size, size), 1)
    out_ref[:size, :] = jnp.where(lane < size - across, left, right)


def place_kernel(offsets_ref, ours_ref, theirs_ref, zeros_ref, out_ref, window, sem):
    del zeros_ref
    size = theirs_ref.shape[1]
    row_base, column_base, down, across = window_of(
        offsets_ref, out_ref.shape[1], out_ref.shape[2], size
    )
    update = jnp.concatenate([ours_ref[...] + theirs_ref[...], jnp.zeros((8, size), F32)], axis=0)
    update = pltpu.roll(pltpu.roll(update, down, 0), lax.rem(across, size), 1)
    lane = lax.broadcasted_iota(jnp.int32, (size + 8, size), 1)
    window[:, :size] = jnp.where(lane < across, 0.0, update)
    window[:, size:] = jnp.where(lane < across, update, 0.0)
    copy = pltpu.make_async_copy(
        window, out_ref.at[0, pl.ds(row_base, size + 8), pl.ds(column_base, 2 * size)], sem
    )
    copy.start()
    copy.wait()


def table_kernel(phase_ref, forward_ref, backward_ref, zeros_ref, blank, sem):
    size = phase_ref.shape[1]
    blank[...] = jnp.zeros_like(blank)
    copies = [
        pltpu.make_async_copy(blank, zeros_ref.at[0, pl.ds(row, size)], sem.at[k])
        for k, row in enumerate(range(0, zeros_ref.shape[1], size))
    ]
    for copy in copies:
        copy.start()
    rows = lax.broadcasted_iota(jnp.int32, (size, size), 0)
    columns = lax.broadcasted_iota(jnp.int32, (size, size), 1)
    angle = ((rows * columns) % size).astype(F32) * (2.0 * math.pi / size)
    c, s = sincos(angle)
    whole = jnp.concatenate(
        [jnp.concatenate([c, s], axis=1), jnp.concatenate([-s, c], axis=1)], axis=0
    )

    def put(index, real, imag):
        real_turned, imag_turned = real.T, imag.T
        for ref, quarters in (
            (forward_ref, (real, imag, -imag, real)),
            (backward_ref, (real_turned, -imag_turned, imag_turned, real_turned)),
        ):
            for place, quarter in enumerate(quarters):
                r, k = place // 2 * size, place % 2 * size
                high, low = split(quarter)
                ref[index, 0, r : r + size, k : k + size] = high
                ref[index, 1, r : r + size, k : k + size] = low

    for steps in (1, 2, 3):
        h_real, h_imag = sincos(phase_ref[...] * float(steps))
        real = c * h_real + s * h_imag
        imag = c * h_imag - s * h_real
        put(2 + steps, real * (1.0 / math.sqrt(size)), imag * (1.0 / math.sqrt(size)))
        both = jnp.concatenate([real, imag], axis=1)
        k = jnp.dot(both, whole, precision=lax.Precision.HIGHEST, preferred_element_type=F32)
        put(steps - 1, k[:, :size] * (1.0 / size), k[:, size:] * (1.0 / size))
    for copy in copies:
        copy.wait()


def steps_of(ref, index, size):
    steps = ref[index, size, 0].astype(jnp.int32)
    return jnp.clip(steps, 1, 3) - 1


def position():
    rank = lax.axis_index("slc")
    return rank, rank // CLUSTER


def patch_of(near_ref, far_ref, at, size):
    block, half, crossed = at // CLUSTER, (at // 2) % 2, at % 2 == 1
    entry = 2 * block + half
    steps = jnp.where(crossed, far_ref[entry, size, 0], near_ref[entry, size, 0])
    kind = jnp.clip(steps.astype(jnp.int32), 1, 3) - 1
    cosine, sine = sincos(jnp.where(crossed, far_ref[entry, :size, :], near_ref[entry, :size, :]))
    return kind, cosine, sine


def first_waves(wave_ref, modes):
    if wave_ref.dtype == F32:
        return [wave_ref[m] for m in range(modes)]
    start = (lax.axis_index("slc") % 2) * modes
    return [
        jnp.concatenate(
            [wave_ref[0, start + m].astype(F32), wave_ref[1, start + m].astype(F32)], axis=1
        )
        for m in range(modes)
    ]


def forward_kernel(condition, chunks, last, near_ref, far_ref, table_ref, table_t_ref, wave_ref, *refs):
    del table_t_ref
    *_, out_ref, kept_ref, sum_ref = refs[-5:-2]
    rank, layer = position()

    @pl.when(condition(layer))
    def _():
        size = near_ref.shape[2]
        modes = out_ref.shape[0]
        waves = first_waves(wave_ref, modes)
        slices = range(CLUSTER * chunks[0], CLUSTER * chunks[1])
        for index in slices:
            at = index ^ rank
            kind, cosine, sine = patch_of(near_ref, far_ref, at, size)
            if last and index == slices[-1]:
                kind = kind + 3
            if index % 2 == 1:
                cosine, sine = cosine.T, sine.T
            high, low = table_ref[kind, 0], table_ref[kind, 1]
            slot = jnp.minimum(at, 2)
            after = []
            for m in range(modes):
                real, imag = waves[m][:, :size], waves[m][:, size:]
                u = jnp.concatenate(
                    [cosine * real - sine * imag, cosine * imag + sine * real], axis=1
                )
                kept_ref[slot, m] = u
                after.append(two_sided(u, high, low, size))
            waves = after
        total = None
        for m in range(modes):
            out_ref[m] = waves[m]
            if last:
                real, imag = waves[m][:, :size], waves[m][:, size:]
                power = real * real + imag * imag
                total = power if total is None else total + power
        if last:
            sum_ref[...] = total


def backward_kernel(chunk, last, near_ref, far_ref, table_ref, kept_ref, *refs):
    if last:
        mine_ref, theirs_ref, measured_ref, wave_ref, out_ref, ours_ref, _, update = refs
    else:
        _, wave_ref, out_ref, ours_ref, _, update = refs
    rank, layer = position()

    @pl.when(layer <= chunk)
    def _():
        size = near_ref.shape[2]
        modes = wave_ref.shape[0]
        waves = [wave_ref[m] for m in range(modes)]
        if last:
            misfit = mine_ref[...] + theirs_ref[...] - measured_ref[0]
            misfit = jnp.concatenate([misfit, misfit], axis=1)
            waves = [wave * misfit for wave in waves]
        slices = range(CLUSTER * chunk, CLUSTER * (chunk + 1))
        for index in reversed(slices):
            at = index ^ rank
            kind, cosine, sine = patch_of(near_ref, far_ref, at, size)
            if last and index == slices[-1]:
                kind = kind + 3
            if index % 2 == 1:
                cosine, sine = cosine.T, sine.T
            high, low = table_ref[kind, 0], table_ref[kind, 1]
            slot = jnp.minimum(at, 2)
            after = []
            gradient = None
            for m in range(modes):
                mu = two_sided(waves[m], high, low, size)
                real, imag = mu[:, :size], mu[:, size:]
                u = kept_ref[slot, m]
                term = imag * u[:, :size] - real * u[:, size:]
                gradient = term if gradient is None else gradient + term
                after.append(
                    jnp.concatenate(
                        [cosine * real + sine * imag, cosine * imag - sine * real], axis=1
                    )
                )
            update[slot] = gradient.T if index % 2 == 1 else gradient
            waves = after
        if chunk > 0:
            for m in range(modes):
                out_ref[m] = waves[m]
        ours_ref[0] = update[0]
        ours_ref[1] = update[1]


def choose_kernel(ours_ref, own_ref, other_ref):
    own_ref[...] = ours_ref[0]
    other_ref[...] = ours_ref[1]


def joined_kernel(*refs):
    del refs


def after(block, *others):
    return pl.pallas_call(
        joined_kernel,
        in_specs=[ANY] * (1 + len(others)),
        out_specs=ANY,
        out_shape=jax.ShapeDtypeStruct(block.shape, block.dtype),
        input_output_aliases={0: 0},
        compiler_params=pltpu.CompilerParams(vmem_limit_bytes=2**20),
    )(block, *others)


def shaped(*shape, dtype=F32):
    return jax.ShapeDtypeStruct(shape, dtype)


def call(kernel, ins, outs, out_specs=None, scratch=(), flops=0, limit=LIMIT, **more):
    return pl.pallas_call(
        kernel,
        in_specs=ins,
        out_specs=out_specs or [VMEM] * len(outs),
        out_shape=outs,
        scratch_shapes=list(scratch),
        compiler_params=pltpu.CompilerParams(vmem_limit_bytes=limit),
        cost_estimate=pl.CostEstimate(flops=flops, bytes_accessed=1024, transcendentals=0),
        **more,
    )


def local(potential, thickness, propagator_phase, probe, offsets, measured):
    size = probe.shape[2]
    modes = probe.shape[1] // 2
    length = lax.axis_size("slc")
    chunks = length // CLUSTER
    wave = shaped(modes, size, 2 * size)
    kept_shape = shaped(3, modes, size, 2 * size)
    panel = shaped(size, size)
    pair = shaped(2, size, size)
    table = shaped(6, 2, 2 * size, 2 * size, dtype=BF16)
    dma = pltpu.SemaphoreType.DMA
    window = pltpu.VMEM((size + 8, 2 * size), F32)

    def flipped(block, bit):
        return lax.ppermute(block, "slc", [(i, i ^ bit) for i in range(length)])

    (message,) = call(
        extract_kernel,
        [HBM, HBM, HBM],
        [shaped(size + 8, size)],
        None,
        [window, pltpu.SMEM((1, 2), jnp.int32), pltpu.SMEM((1,), jnp.int32), dma((3,))],
        limit=63 * 2**20,
    )(offsets, thickness, potential)
    received = flipped(message, 2)
    forward_table, backward_table, zeros = call(
        table_kernel,
        [VMEM],
        [table, table, shaped(*potential.shape)],
        [VMEM, VMEM, HBM],
        [pltpu.VMEM((size, potential.shape[2]), F32), dma((potential.shape[1] // size,))],
    )(propagator_phase.reshape(1, size))
    near = jnp.stack([message, after(received, forward_table)])
    far = flipped(near, 1)
    direct = [near] + [flipped(near, CLUSTER * k) for k in range(1, 2)]
    halves = [flipped(message, CLUSTER * k) for k in range(2, chunks)]

    def forward(condition, span, near, far, tables, waves, kept, power):
        last = span[1] == chunks
        ins = [near, far, *tables] + ([probe] if span[0] == 0 else [])
        aliases = {}
        if kept is not None:
            aliases = {len(ins) + k: k for k in range(3)}
            ins += [waves, kept, power]
        *results, first, second = call(
            functools.partial(forward_kernel, condition, span, last),
            [VMEM] * len(ins),
            [wave, kept_shape, panel, table, table],
            None,
            input_output_aliases=aliases | {2: 3, 3: 4},
        )(*ins)
        return (first, second), *results

    tables = (forward_table, backward_table)
    tables, waves, kept, power = forward(
        lambda layer: layer == 0, (0, 1), near, far, tables, None, None, None
    )
    halves = jnp.stack(halves)
    crossed = after(flipped(halves, 2), waves)
    late = [block for k in range(chunks - 2) for block in (halves[k], crossed[k])]
    blocks = jnp.concatenate([near, after(direct[1], waves), jnp.stack(late)])
    others = flipped(blocks, 1)
    tables, waves, kept, power = forward(
        lambda layer: layer > 0, (0, 1), blocks, others, tables, waves, kept, power
    )
    for start in range(1, chunks, 3):
        tables, waves, kept, power = forward(
            lambda layer: layer >= 0,
            (start, min(start + 3, chunks)),
            blocks,
            others,
            tables,
            waves,
            kept,
            power,
        )
    backward_table = tables[1]
    ours = None
    extra = (power, flipped(power, 1), measured)
    for chunk in reversed(range(chunks)):
        last = chunk == chunks - 1
        ins = [blocks, others, backward_table, kept, *(extra if last else (ours,)), waves]
        aliases = {2: 2, len(ins) - 1: 0}
        if not last:
            aliases[4] = 1
        waves, ours, backward_table = call(
            functools.partial(backward_kernel, chunk, last),
            [VMEM] * len(ins),
            [wave, pair, table],
            None,
            [pltpu.VMEM((3, size, size), F32)],
            input_output_aliases=aliases,
        )(*ins)
    own, other = call(choose_kernel, [VMEM], [panel, panel])(ours)
    (gradient,) = call(
        place_kernel,
        [SMEM, VMEM, VMEM, HBM],
        [shaped(*potential.shape)],
        [HBM],
        [window, dma],
        input_output_aliases={3: 0},
    )(offsets, own, flipped(other, 1), zeros)
    return gradient


def solution(mesh):
    placed = (
        P(("grp", "slc"), None, None),
        P(("grp", "slc")),
        P(),
        P("grp", None, None, None),
        P("grp", None),
        P("grp", None, None),
    )
    return jax.shard_map(
        local, mesh=mesh, in_specs=placed, out_specs=P(("grp", "slc"), None, None), check_vma=False
    )
```

time: 79.1 us -> 47.5 us (0.60)
  local copies, waits for them, and re-layouts: 15.2 us -> 1.64 us
  waiting for transfers between devices: 14.6 us -> 5.26 us
  starting transfers between devices: 15.6 us -> 9.63 us
  Pallas kernels: 31.2 us -> 29.8 us
  other arithmetic: 0.95 us -> 0.03 us
    unnamed x46 -> x16, local copies, waits for them, and re-layouts: 13.5 us -> 1.63 us
    ppermute x6 -> x0, starting transfers between devices: 11.7 us -> none  [moved(): return lax.ppermute(block, 'slc', route)]
    ppermute x6 -> x0, waiting for transfers between devices: 10.5 us -> none  [moved(): return lax.ppermute(block, 'slc', route)]
    ppermute x7 -> x9, starting transfers between devices: 3.9 us -> 9.63 us  [flipped(): return lax.ppermute(block, 'slc', [(i, i ^ bit) for i in range(length)])]
    pallas_call x11 -> x14, Pallas kernels: 31.2 us -> 29.8 us  [the longest x4 12.7 us: local(): call(functools.partial(backward_kernel, chunk, last), [VMEM] * len(ins),...]
    ppermute x7 -> x9, waiting for transfers between devices: 4.09 us -> 5.26 us  [flipped(): return lax.ppermute(block, 'slc', [(i, i ^ bit) for i in range(length)])]
    broadcast_in_dim x1 -> x0, local copies, waits for them, and re-layouts: 1.1 us -> none  [local(): jnp.zeros(potential.shape, F32)]
    another operation x2, other arithmetic: 0.91 us -> 0.03 us  [the longest x1 0.02 us: local(): halves = jnp.stack(halves)]
  transfers between devices with their start and end apart: 13 -> 9, of which waited for: 7 -> 6; matrix products, arithmetic and copies ran while one was open for 1% -> 2% of each run, Pallas kernels for 26% -> 10%
where the time goes in v2:
time: 47.5 us; the launch traced here: 47.3 us
  Pallas kernels  29.8 us (63%)
  starting transfers between devices  9.63 us (20%)
  waiting for transfers between devices  5.26 us (11%)
  local copies, waits for them, and re-layouts  1.64 us (3%)
  between operations  1.02 us (2%)
    pallas_call x4, Pallas kernels, local(): call(functools.partial(backward_kernel, chunk, last), [VMEM] * len(ins),...  12.7 us
    pallas_call x3, Pallas kernels, forward(): call(functools.partial(forward_kernel, condition, span, last), [VMEM] * l...  11.4 us
    ppermute x9, starting transfers between devices, flipped(): return lax.ppermute(block, 'slc', [(i, i ^ bit) for i in range(length)])  9.63 us
    ppermute x9, waiting for transfers between devices, flipped(): return lax.ppermute(block, 'slc', [(i, i ^ bit) for i in range(length)])  5.26 us
    pallas_call x1, Pallas kernels, local(): call(extract_kernel, [HBM, HBM, HBM], [shaped(size + 8, size)], None, [wi...  2.49 us
    pallas_call x1, Pallas kernels, local(): call(table_kernel, [VMEM], [table, table, shaped(*potential.shape)], [VME...  1.85 us
    unnamed x16, local copies, waits for them, and re-layouts  1.63 us
    pallas_call x1, Pallas kernels, local(): call(place_kernel, [SMEM, VMEM, VMEM, HBM], [shaped(*potential.shape)], [...  1.32 us
  transfers between devices with their start and end apart: 9, of which 6 were waited for; matrix products, arithmetic and copies ran while one was open for 2% of the time, Pallas kernels for 10%

profile of v2, /device:TPU:0, one launch (start us, length us, event | category | flops | bytes accessed | tf_op | source)
XLA Modules:
  0.0 47.3 jit_solution(1560071272845288859)
XLA Ops:
  0.7 2.5 %shard_map.64 = f32[136,128]{1,0:T(8,128)} custom-call(s32[1,2]{1,0:T(1,128)} %offsets_ref.1, s32[1]{0:T(128)S(6)} %copy.67.thickness_hbm, f32[1,512,512]{2,1,0:T(8,128)} %potential_ref.1), custom_call_target="tpu_custom_call" | custom-call | bytes 1024 | tf_op jit(solution)/shard_map/pallas_call | solution.py:330
  3.2 5.1 %collective-permute-start.4 = (f32[136,128]{1,0:T(8,128)}, f32[136,128]{1,0:T(8,128)S(1)}, u32[]{:S(2)}, u32[]{:S(2)}) collective-permute-start(f32[136,128]{1,0:T(8,128)} %shard_map.64), channel_id=1, source_target_pairs={{0,12},{1,13},{2,14},{3,15},{4,8},{5,9},{6,10},{7,11},{8,4},{9,5},... | collective-permute-start | bytes 208904 | tf_op jit(solution)/shard_map/ppermute | solution.py:328
  8.3 1.5 %collective-permute-start = (f32[136,128]{1,0:T(8,128)}, f32[136,128]{1,0:T(8,128)S(1)}, u32[]{:S(2)}, u32[]{:S(2)}) collective-permute-start(f32[136,128]{1,0:T(8,128)} %shard_map.64), channel_id=1, source_target_pairs={{0,2},{1,3},{2,0},{3,1},{4,6},{5,7},{6,4},{7,5},{8,10},{9,11},{10,... | collective-permute-start | bytes 208904 | tf_op jit(solution)/shard_map/ppermute | solution.py:328
  9.8 0.9 %constant_dynamic-update-slice_fusion.4 = f32[8,136,128]{2,1,0:T(8,128)S(1)} fusion(f32[136,128]{1,0:T(8,128)} %shard_map.64), kind=kLoop, calls=%fused_computation.8 | loop fusion | bytes 139264
  10.7 0.7 %copy-done.3 = f32[128]{0:T(128)S(1)} copy-done((f32[128]{0:T(128)S(1)}, f32[128]{0:T(128)}, u32[]{:S(2)}) %copy-start.3) | copy-done | bytes 536
  11.4 1.9 %shard_map.65 = (bf16[6,2,256,256]{3,2,1,0:T(8,128)(2,1)S(1)}, bf16[6,2,256,256]{3,2,1,0:T(8,128)(2,1)S(1)}, f32[1,512,512]{2,1,0:T(8,128)}) custom-call(f32[1,128]{1,0:T(1,128)S(1)} %bitcast.10), custom_call_target="tpu_custom_call" | custom-call | bytes 1024 | tf_op jit(solution)/shard_map/pallas_call | solution.py:339
  13.3 0.1 collective-permute-start.2
  13.4 0.8 %collective-permute-start.1 = (f32[2,136,128]{2,1,0:T(8,128)S(1)}, f32[2,136,128]{2,1,0:T(8,128)S(1)}, u32[]{:S(2)}, u32[]{:S(2)}) collective-permute-start(f32[2,136,128]{2,1,0:T(8,128)S(1)} %pad_maximum_fusion.near_ref), channel_id=1, source_target_pairs={{0,4},{1,5},{2,6},{3,7},{4,0},{5,1},{6,2},{7,3},{8,12},{9,13},{10,... | collective-permute-start | bytes 417800 | tf_op jit(solution)/shard_map/ppermute | solution.py:328
  14.2 0.2 collective-permute-done.3
  14.4 1.6 %collective-permute-start.5 = (f32[2,136,128]{2,1,0:T(8,128)S(1)}, f32[2,136,128]{2,1,0:T(8,128)S(1)}, u32[]{:S(2)}, u32[]{:S(2)}) collective-permute-start(f32[2,136,128]{2,1,0:T(8,128)S(1)} %pad_maximum_fusion.1), channel_id=1, source_target_pairs={{0,2},{1,3},{2,0},{3,1},{4,6},{5,7},{6,4},{7,5},{8,10},{9,11},{10,... | collective-permute-start | bytes 417800 | tf_op jit(solution)/shard_map/ppermute | solution.py:328
  16.0 3.1 %shard_map.67 = (f32[6,128,256]{2,1,0:T(8,128)S(1)}, f32[3,6,128,256]{3,2,1,0:T(8,128)S(1)}, f32[128,128]{1,0:T(8,128)S(1)}, bf16[6,2,256,256]{3,2,1,0:T(8,128)(2,1)S(1)}, bf16[6,2,256,256]{3,2,1,0:T(8,128)(2,1)S(1)}) custom-call(f32[2,136,128]{2,1,0:T(8,128)S(1)} %pad_maximum_fusion.near_ref, ...), custom_call_target="tpu_custom_call", output_to_operand_aliasing={{3}: (2, {}), {4}: (3, {})} | custom-call | bytes 1024 | tf_op jit(solution)/shard_map/pallas_call | solution.py:358
  19.1 0.3 collective-permute-done.1.refs_0_
  19.5 0.6 %collective-permute-done.5.refs_0_ = f32[2,136,128]{2,1,0:T(8,128)S(1)} collective-permute-done((f32[2,136,128]{2,1,0:T(8,128)S(1)}, f32[2,136,128]{2,1,0:T(8,128)S(1)}, u32[]{:S(2)}, u32[]{:S(2)}) %collective-permute-start.5) | collective-permute-done | bytes 139296 | tf_op jit(solution)/shard_map/ppermute | solution.py:328
  20.2 1.9 %collective-permute-done.6.far_ref = f32[8,136,128]{2,1,0:T(8,128)S(1)} collective-permute-done((f32[8,136,128]{2,1,0:T(8,128)S(1)}, f32[8,136,128]{2,1,0:T(8,128)S(1)}, u32[]{:S(2)}, u32[]{:S(2)}) %collective-permute-start.6) | collective-permute-done | bytes 557088 | tf_op jit(solution)/shard_map/ppermute | solution.py:328
  22.1 8.3 %shard_map.71 = (f32[6,128,256]{2,1,0:T(8,128)S(1)}, f32[3,6,128,256]{3,2,1,0:T(8,128)S(1)}, f32[128,128]{1,0:T(8,128)S(1)}, bf16[6,2,256,256]{3,2,1,0:T(8,128)(2,1)S(1)}, bf16[6,2,256,256]{3,2,1,0:T(8,128)(2,1)S(1)}) custom-call(f32[8,136,128]{2,1,0:T(8,128)S(1)} %slice_dynamic-update, ...), custom_call_target="tpu_custom_call", output_to_operand_aliasing={{0}: (4, {}), {1}: (5, {}), {2}: (6, {}), {3}: (2, {}), {4}... | custom-call | bytes 1024 | tf_op jit(solution)/shard_map/pallas_call | solution.py:358
  30.4 0.2 collective-permute-start.7
  30.6 1.1 %collective-permute-done.7.refs_1_ = f32[128,128]{1,0:T(8,128)S(1)} collective-permute-done((f32[128,128]{1,0:T(8,128)S(1)}, f32[128,128]{1,0:T(8,128)S(1)}, u32[]{:S(2)}, u32[]{:S(2)}) %collective-permute-start.7) | collective-permute-done | bytes 65568 | tf_op jit(solution)/shard_map/ppermute | solution.py:328
  31.7 3.1 %shard_map.72 = (f32[6,128,256]{2,1,0:T(8,128)S(1)}, f32[2,128,128]{2,1,0:T(8,128)S(1)}, bf16[6,2,256,256]{3,2,1,0:T(8,128)(2,1)S(1)}) custom-call(f32[8,136,128]{2,1,0:T(8,128)S(1)} %slice_dynamic-update-slice_fusion.near_ref, f32[8,136,128]{2,1,0:T(8,128)S(1)} %collective-permute-done.6.far_ref, ...), custom_call_target="tpu_custom_call", output_to_operand_aliasing={{2}: (2, {}), {0}: (7, {})} | custom-call | bytes 1024 | tf_op jit(solution)/shard_map/pallas_call | solution.py:399
  34.9 3.4 %shard_map.73 = (f32[6,128,256]{2,1,0:T(8,128)S(1)}, f32[2,128,128]{2,1,0:T(8,128)S(1)}, bf16[6,2,256,256]{3,2,1,0:T(8,128)(2,1)S(1)}) custom-call(f32[8,136,128]{2,1,0:T(8,128)S(1)} %slice_dynamic-update-slice_fusion.near_ref, f32[8,136,128]{2,1,0:T(8,128)S(1)} %collective-permute-done.6.far_ref, ...), custom_call_target="tpu_custom_call", output_to_operand_aliasing={{2}: (2, {}), {0}: (5, {}), {1}: (4, {})} | custom-call | bytes 1024 | tf_op jit(solution)/shard_map/pallas_call | solution.py:399
  38.2 3.1 %shard_map.74 = (f32[6,128,256]{2,1,0:T(8,128)S(1)}, f32[2,128,128]{2,1,0:T(8,128)S(1)}, bf16[6,2,256,256]{3,2,1,0:T(8,128)(2,1)S(1)}) custom-call(f32[8,136,128]{2,1,0:T(8,128)S(1)} %slice_dynamic-update-slice_fusion.near_ref, f32[8,136,128]{2,1,0:T(8,128)S(1)} %collective-permute-done.6.far_ref, ...), custom_call_target="tpu_custom_call", output_to_operand_aliasing={{2}: (2, {}), {0}: (5, {}), {1}: (4, {})} | custom-call | bytes 1024 | tf_op jit(solution)/shard_map/pallas_call | solution.py:399
  41.4 3.1 %shard_map.75 = (f32[6,128,256]{2,1,0:T(8,128)S(1)}, f32[2,128,128]{2,1,0:T(8,128)S(1)}, bf16[6,2,256,256]{3,2,1,0:T(8,128)(2,1)S(1)}) custom-call(f32[8,136,128]{2,1,0:T(8,128)S(1)} %slice_dynamic-update-slice_fusion.near_ref, f32[8,136,128]{2,1,0:T(8,128)S(1)} %collective-permute-done.6.far_ref, ...), custom_call_target="tpu_custom_call", output_to_operand_aliasing={{2}: (2, {}), {0}: (5, {}), {1}: (4, {})} | custom-call | bytes 1024 | tf_op jit(solution)/shard_map/pallas_call | solution.py:399
  44.5 0.2 collective-permute-start.8
  44.7 1.1 %collective-permute-done.8.theirs_ref = f32[128,128]{1,0:T(8,128)S(1)} collective-permute-done((f32[128,128]{1,0:T(8,128)S(1)}, f32[128,128]{1,0:T(8,128)S(1)}, u32[]{:S(2)}, u32[]{:S(2)}) %collective-permute-start.8) | collective-permute-done | bytes 65568 | tf_op jit(solution)/shard_map/ppermute | solution.py:328
  45.8 1.3 %shard_map.77 = f32[1,512,512]{2,1,0:T(8,128)} custom-call(s32[1,2]{1,0:T(1,128)S(1)} %copy-done.2, f32[128,128]{1,0:T(8,128)S(1)} %get-tuple-element.60.ours_ref, f32[128,128]{1,0:T(8,128)S(1)} %collective-permute-done.8.theirs_ref, f32[1,512,512]{2,1,0:T(8,128)} %get-tuple-element.62.zeros_ref), custom_call_target="tpu_custom_call", output_to_operand_aliasing={{}: (3, {})} | custom-call | bytes 1024 | tf_op jit(solution)/shard_map/pallas_call | solution.py:408
  (27 shorter events, 0.2 us)
Async XLA Ops:
  0.7 15.4 %copy-start = (bf16[2,12,128,128]{3,2,1,0:T(8,128)(2,1)S(1)}, bf16[2,12,128,128]{3,2,1,0:T(8,128)(2,1)}, u32[]{:S(2)}) copy-start(bf16[2,12,128,128]{3,2,1,0:T(8,128)(2,1)} %wave_ref.3) | copy-start | bytes 2359300
  3.2 10.1 %copy-start.4 = (f32[136,128]{1,0:T(8,128)S(1)}, f32[136,128]{1,0:T(8,128)}, u32[]{:S(2)}) copy-start(f32[136,128]{1,0:T(8,128)} %shard_map.64) | copy-start | bytes 208900
  3.2 11.1 %collective-permute-start.4 = (f32[136,128]{1,0:T(8,128)}, f32[136,128]{1,0:T(8,128)S(1)}, u32[]{:S(2)}, u32[]{:S(2)}) collective-permute-start(f32[136,128]{1,0:T(8,128)} %shard_map.64), channel_id=1, source_target_pairs={{0,12},{1,13},{2,14},{3,15},{4,8},{5,9},{6,10},{7,11},{8,4},{9,5},... | collective-permute-start | bytes 208904 | tf_op jit(solution)/shard_map/ppermute | solution.py:328
  8.3 6.1 %collective-permute-start.3 = (f32[136,128]{1,0:T(8,128)}, f32[136,128]{1,0:T(8,128)S(1)}, u32[]{:S(2)}, u32[]{:S(2)}) collective-permute-start(f32[136,128]{1,0:T(8,128)} %shard_map.64), channel_id=1, source_target_pairs={{0,8},{1,9},{2,10},{3,11},{4,12},{5,13},{6,14},{7,15},{8,0},{9,1},... | collective-permute-start | bytes 208904 | tf_op jit(solution)/shard_map/ppermute | solution.py:328
  8.3 5.0 %collective-permute-start = (f32[136,128]{1,0:T(8,128)}, f32[136,128]{1,0:T(8,128)S(1)}, u32[]{:S(2)}, u32[]{:S(2)}) collective-permute-start(f32[136,128]{1,0:T(8,128)} %shard_map.64), channel_id=1, source_target_pairs={{0,2},{1,3},{2,0},{3,1},{4,6},{5,7},{6,4},{7,5},{8,10},{9,11},{10,... | collective-permute-start | bytes 208904 | tf_op jit(solution)/shard_map/ppermute | solution.py:328
  10.7 0.7 %copy-start.3 = (f32[128]{0:T(128)S(1)}, f32[128]{0:T(128)}, u32[]{:S(2)}) copy-start(f32[128]{0:T(128)} %param.8) | copy-start | bytes 1540
  13.3 2.7 %collective-permute-start.2 = (f32[2,136,128]{2,1,0:T(8,128)S(1)}, f32[2,136,128]{2,1,0:T(8,128)S(1)}, u32[]{:S(2)}, u32[]{:S(2)}) collective-permute-start(f32[2,136,128]{2,1,0:T(8,128)S(1)} %pad_maximum_fusion.near_ref), channel_id=1, source_target_pairs={{0,1},{1,0},{2,3},{3,2},{4,5},{5,4},{6,7},{7,6},{8,9},{9,8},{10,11... | collective-permute-start | bytes 417800 | tf_op jit(solution)/shard_map/ppermute | solution.py:328
  13.4 6.1 %collective-permute-start.1 = (f32[2,136,128]{2,1,0:T(8,128)S(1)}, f32[2,136,128]{2,1,0:T(8,128)S(1)}, u32[]{:S(2)}, u32[]{:S(2)}) collective-permute-start(f32[2,136,128]{2,1,0:T(8,128)S(1)} %pad_maximum_fusion.near_ref), channel_id=1, source_target_pairs={{0,4},{1,5},{2,6},{3,7},{4,0},{5,1},{6,2},{7,3},{8,12},{9,13},{10,... | collective-permute-start | bytes 417800 | tf_op jit(solution)/shard_map/ppermute | solution.py:328
  14.4 5.6 %collective-permute-start.5 = (f32[2,136,128]{2,1,0:T(8,128)S(1)}, f32[2,136,128]{2,1,0:T(8,128)S(1)}, u32[]{:S(2)}, u32[]{:S(2)}) collective-permute-start(f32[2,136,128]{2,1,0:T(8,128)S(1)} %pad_maximum_fusion.1), channel_id=1, source_target_pairs={{0,2},{1,3},{2,0},{3,1},{4,6},{5,7},{6,4},{7,5},{8,10},{9,11},{10,... | collective-permute-start | bytes 417800 | tf_op jit(solution)/shard_map/ppermute | solution.py:328
  20.1 2.0 %collective-permute-start.6 = (f32[8,136,128]{2,1,0:T(8,128)S(1)}, f32[8,136,128]{2,1,0:T(8,128)S(1)}, u32[]{:S(2)}, u32[]{:S(2)}) collective-permute-start(f32[8,136,128]{2,1,0:T(8,128)S(1)} %slice_dynamic-update-slice_fusion.near_ref), channel_id=1, source_target_pairs={{0,1},{1,0},{2,3},{3,2},{4,5},{5,4},{6,7},{7,6},{8,9},{9,8},{10,11... | collective-permute-start | bytes 1671176 | tf_op jit(solution)/shard_map/ppermute | solution.py:328
  22.1 9.6 %copy-start.1 = (f32[1,128,128]{2,1,0:T(8,128)S(1)}, f32[1,128,128]{2,1,0:T(8,128)}, u32[]{:S(2)}) copy-start(f32[1,128,128]{2,1,0:T(8,128)} %refs_2_.1) | copy-start | bytes 196612
  30.4 1.3 %collective-permute-start.7 = (f32[128,128]{1,0:T(8,128)S(1)}, f32[128,128]{1,0:T(8,128)S(1)}, u32[]{:S(2)}, u32[]{:S(2)}) collective-permute-start(f32[128,128]{1,0:T(8,128)S(1)} %get-tuple-element.48.refs_0_), channel_id=1, source_target_pairs={{0,1},{1,0},{2,3},{3,2},{4,5},{5,4},{6,7},{7,6},{8,9},{9,8},{10,11... | collective-permute-start | bytes 196616 | tf_op jit(solution)/shard_map/ppermute | solution.py:328
  41.4 4.5 %copy-start.2 = (s32[1,2]{1,0:T(1,128)S(1)}, s32[1,2]{1,0:T(1,128)}, u32[]{:S(2)}) copy-start(s32[1,2]{1,0:T(1,128)} %offsets_ref.1) | copy-start | bytes 28
  44.5 1.3 %collective-permute-start.8 = (f32[128,128]{1,0:T(8,128)S(1)}, f32[128,128]{1,0:T(8,128)S(1)}, u32[]{:S(2)}, u32[]{:S(2)}) collective-permute-start(f32[128,128]{1,0:T(8,128)S(1)} %get-tuple-element.61), channel_id=1, source_target_pairs={{0,1},{1,0},{2,3},{3,2},{4,5},{5,4},{6,7},{7,6},{8,9},{9,8},{10,11... | collective-permute-start | bytes 196616 | tf_op jit(solution)/shard_map/ppermute | solution.py:328

commit v3 on v2

--- a/solution.py
+++ b/solution.py
@@ -191,10 +191,10 @@
     *_, out_ref, kept_ref, sum_ref = refs[-5:-2]
     rank, layer = position()
 
-    @pl.when(condition(layer))
-    def _():
-        size = near_ref.shape[2]
-        modes = out_ref.shape[0]
+    size = near_ref.shape[2]
+    modes = out_ref.shape[0]
+
+    def run():
         waves = first_waves(wave_ref, modes)
         slices = range(CLUSTER * chunks[0], CLUSTER * chunks[1])
         for index in slices:
@@ -225,18 +225,21 @@
         if last:
             sum_ref[...] = total
 
+    pl.when(condition(layer))(run)
+
 
 def backward_kernel(chunk, last, near_ref, far_ref, table_ref, kept_ref, *refs):
     if last:
-        mine_ref, theirs_ref, measured_ref, wave_ref, out_ref, ours_ref, _, update = refs
+        mine_ref, theirs_ref, measured_ref, *refs = refs
     else:
-        _, wave_ref, out_ref, ours_ref, _, update = refs
+        refs = refs[1:]
+    wave_ref, *outs, ours_ref, _, update = refs
     rank, layer = position()
 
-    @pl.when(layer <= chunk)
-    def _():
-        size = near_ref.shape[2]
-        modes = wave_ref.shape[0]
+    size = near_ref.shape[2]
+    modes = wave_ref.shape[0]
+
+    def run():
         waves = [wave_ref[m] for m in range(modes)]
         if last:
             misfit = mine_ref[...] + theirs_ref[...] - measured_ref[0]
@@ -260,18 +263,21 @@
                 u = kept_ref[slot, m]
                 term = imag * u[:, :size] - real * u[:, size:]
                 gradient = term if gradient is None else gradient + term
-                after.append(
-                    jnp.concatenate(
-                        [cosine * real + sine * imag, cosine * imag - sine * real], axis=1
+                if index > 0:
+                    after.append(
+                        jnp.concatenate(
+                            [cosine * real + sine * imag, cosine * imag - sine * real], axis=1
+                        )
                     )
-                )
             update[slot] = gradient.T if index % 2 == 1 else gradient
             waves = after
-        if chunk > 0:
-            for m in range(modes):
-                out_ref[m] = waves[m]
         ours_ref[0] = update[0]
         ours_ref[1] = update[1]
+        for out_ref in outs:
+            for m, wave in enumerate(waves):
+                out_ref[m] = wave
+
+    pl.when(layer <= chunk)(run)
 
 
 def choose_kernel(ours_ref, own_ref, other_ref):
@@ -345,8 +351,9 @@
     )(propagator_phase.reshape(1, size))
     near = jnp.stack([message, after(received, forward_table)])
     far = flipped(near, 1)
-    direct = [near] + [flipped(near, CLUSTER * k) for k in range(1, 2)]
+    beside = flipped(near, CLUSTER)
     halves = [flipped(message, CLUSTER * k) for k in range(2, chunks)]
+    crossed = [flipped(half, 2) for half in halves]
 
     def forward(condition, span, near, far, tables, waves, kept, power):
         last = span[1] == chunks
@@ -365,41 +372,37 @@
         return (first, second), *results
 
     tables = (forward_table, backward_table)
-    tables, waves, kept, power = forward(
-        lambda layer: layer == 0, (0, 1), near, far, tables, None, None, None
-    )
-    halves = jnp.stack(halves)
-    crossed = after(flipped(halves, 2), waves)
-    late = [block for k in range(chunks - 2) for block in (halves[k], crossed[k])]
-    blocks = jnp.concatenate([near, after(direct[1], waves), jnp.stack(late)])
-    others = flipped(blocks, 1)
-    tables, waves, kept, power = forward(
-        lambda layer: layer > 0, (0, 1), blocks, others, tables, waves, kept, power
-    )
-    for start in range(1, chunks, 3):
-        tables, waves, kept, power = forward(
-            lambda layer: layer >= 0,
-            (start, min(start + 3, chunks)),
-            blocks,
-            others,
-            tables,
-            waves,
-            kept,
-            power,
-        )
+    state = forward(lambda layer: layer == 0, (0, 1), near, far, tables, None, None, None)
+    beside = after(beside, state[1])
+    early = (jnp.concatenate([near, beside]), jnp.concatenate([far, flipped(beside, 1)]))
+    late = [block for half, cross in zip(halves, crossed) for block in (half, after(cross, state[1]))]
+    late = jnp.stack(late)
+    late_far = flipped(late, 1)
+    state = forward(lambda layer: layer == 1, (0, 1), *early, *state)
+    state = forward(lambda layer: layer <= 1, (1, 2), *early, *state)
+    blocks = jnp.concatenate([early[0], late])
+    others = jnp.concatenate([early[1], after(late_far, state[1])])
+    state = forward(lambda layer: layer > 1, (0, 2), blocks, others, *state)
+    for start in range(2, chunks, 2):
+        span = (start, min(start + 2, chunks))
+        state = forward(lambda layer: layer >= 0, span, blocks, others, *state)
+    tables, waves, kept, power = state
     backward_table = tables[1]
-    ours = None
+    ours, waves = None, [waves]
     extra = (power, flipped(power, 1), measured)
     for chunk in reversed(range(chunks)):
         last = chunk == chunks - 1
-        ins = [blocks, others, backward_table, kept, *(extra if last else (ours,)), waves]
-        aliases = {2: 2, len(ins) - 1: 0}
+        ins = [blocks, others, backward_table, kept, *(extra if last else (ours,)), *waves]
+        outs = [wave] if chunk > 0 else []
+        aliases = {2: len(outs) + 1}
         if not last:
-            aliases[4] = 1
-        waves, ours, backward_table = call(
+            aliases[4] = len(outs)
+        if outs:
+            aliases[len(ins) - 1] = 0
+        *waves, ours, backward_table = call(
             functools.partial(backward_kernel, chunk, last),
             [VMEM] * len(ins),
-            [wave, pair, table],
+            outs + [pair, table],
             None,
             [pltpu.VMEM((3, size, size), F32)],
             input_output_aliases=aliases,
@@ -407,7 +410,7 @@
     own, other = call(choose_kernel, [VMEM], [panel, panel])(ours)
     (gradient,) = call(
         place_kernel,
-        [SMEM, VMEM, VMEM, HBM],
+        [VMEM, VMEM, VMEM, HBM],
         [shaped(*potential.shape)],
         [HBM],
         [window, dma],

time: 47.5 us -> 47.1 us (level)
  waiting for transfers between devices: 5.26 us -> 4.11 us
    ppermute x9 -> x11, waiting for transfers between devices: 5.26 us -> 4.11 us  [flipped(): return lax.ppermute(block, 'slc', [(i, i ^ bit) for i in range(length)])]
    pallas_call x3 -> x5, Pallas kernels: 11.4 us -> 12.1 us  [forward(): call(functools.partial(forward_kernel, condition, span, last), [VMEM] * l...]
    ppermute x9 -> x11, starting transfers between devices: 9.63 us -> 9.72 us  [flipped(): return lax.ppermute(block, 'slc', [(i, i ^ bit) for i in range(length)])]
    unnamed x16 -> x17, local copies, waits for them, and re-layouts: 1.63 us -> 1.65 us
  transfers between devices with their start and end apart: 9 -> 11, of which waited for: 6 -> 5; matrix products, arithmetic and copies ran while one was open for 2% -> 2% of each run, Pallas kernels for 10% -> 17%
where the time goes in v3:
time: 47.1 us; the launch traced here: 46.9 us
  Pallas kernels  30.1 us (64%)
  starting transfers between devices  9.72 us (21%)
  waiting for transfers between devices  4.11 us (9%)
  local copies, waits for them, and re-layouts  1.66 us (4%)
  between operations  1.13 us (2%)
    pallas_call x4, Pallas kernels, local(): call(functools.partial(backward_kernel, chunk, last), [VMEM] * len(ins),...  12.7 us
    pallas_call x5, Pallas kernels, forward(): call(functools.partial(forward_kernel, condition, span, last), [VMEM] * l...  12.1 us
    ppermute x11, starting transfers between devices, flipped(): return lax.ppermute(block, 'slc', [(i, i ^ bit) for i in range(length)])  9.72 us
    ppermute x11, waiting for transfers between devices, flipped(): return lax.ppermute(block, 'slc', [(i, i ^ bit) for i in range(length)])  4.11 us
    pallas_call x1, Pallas kernels, local(): call(extract_kernel, [HBM, HBM, HBM], [shaped(size + 8, size)], None, [wi...  2.49 us
    pallas_call x1, Pallas kernels, local(): call(table_kernel, [VMEM], [table, table, shaped(*potential.shape)], [VME...  1.85 us
    unnamed x17, local copies, waits for them, and re-layouts  1.65 us
  transfers between devices with their start and end apart: 11, of which 5 were waited for; matrix products, arithmetic and copies ran while one was open for 2% of the time, Pallas kernels for 17%

profile of v3, /device:TPU:0, one launch (start us, length us, event | category | flops | bytes accessed | tf_op | source)
XLA Modules:
  0.0 46.9 jit_solution(3962016573942239554)
XLA Ops:
  0.7 2.5 %shard_map.64 = f32[136,128]{1,0:T(8,128)} custom-call(s32[1,2]{1,0:T(1,128)} %offsets_ref.1, s32[1]{0:T(128)S(6)} %copy.90.thickness_hbm, f32[1,512,512]{2,1,0:T(8,128)} %potential_ref.1), custom_call_target="tpu_custom_call" | custom-call | bytes 1024 | tf_op jit(solution)/shard_map/pallas_call | solution.py:336
  3.2 3.0 %collective-permute-start = (f32[136,128]{1,0:T(8,128)}, f32[136,128]{1,0:T(8,128)S(1)}, u32[]{:S(2)}, u32[]{:S(2)}) collective-permute-start(f32[136,128]{1,0:T(8,128)} %shard_map.64), channel_id=1, source_target_pairs={{0,2},{1,3},{2,0},{3,1},{4,6},{5,7},{6,4},{7,5},{8,10},{9,11},{10,... | collective-permute-start | bytes 208904 | tf_op jit(solution)/shard_map/ppermute | solution.py:334
  6.2 2.6 %collective-permute-start.3 = (f32[136,128]{1,0:T(8,128)}, f32[136,128]{1,0:T(8,128)S(1)}, u32[]{:S(2)}, u32[]{:S(2)}) collective-permute-start(f32[136,128]{1,0:T(8,128)} %shard_map.64), channel_id=1, source_target_pairs={{0,8},{1,9},{2,10},{3,11},{4,12},{5,13},{6,14},{7,15},{8,0},{9,1},... | collective-permute-start | bytes 208904 | tf_op jit(solution)/shard_map/ppermute | solution.py:334
  8.8 1.3 %collective-permute-start.5 = (f32[136,128]{1,0:T(8,128)}, f32[136,128]{1,0:T(8,128)S(1)}, u32[]{:S(2)}, u32[]{:S(2)}) collective-permute-start(f32[136,128]{1,0:T(8,128)} %shard_map.64), channel_id=1, source_target_pairs={{0,12},{1,13},{2,14},{3,15},{4,8},{5,9},{6,10},{7,11},{8,4},{9,5},... | collective-permute-start | bytes 208904 | tf_op jit(solution)/shard_map/ppermute | solution.py:334
  10.1 0.9 %constant_dynamic-update-slice_fusion.6 = f32[8,136,128]{2,1,0:T(8,128)S(1)} fusion(f32[136,128]{1,0:T(8,128)} %shard_map.64), kind=kLoop, calls=%fused_computation.10 | loop fusion | bytes 139264
  11.1 0.7 %copy-done.3 = f32[128]{0:T(128)S(1)} copy-done((f32[128]{0:T(128)S(1)}, f32[128]{0:T(128)}, u32[]{:S(2)}) %copy-start.3) | copy-done | bytes 536
  11.7 1.9 %shard_map.65 = (bf16[6,2,256,256]{3,2,1,0:T(8,128)(2,1)S(1)}, bf16[6,2,256,256]{3,2,1,0:T(8,128)(2,1)S(1)}, f32[1,512,512]{2,1,0:T(8,128)}) custom-call(f32[1,128]{1,0:T(1,128)S(1)} %bitcast.17), custom_call_target="tpu_custom_call" | custom-call | bytes 1024 | tf_op jit(solution)/shard_map/pallas_call | solution.py:345
  13.7 0.3 collective-permute-start.1
  14.0 0.5 %collective-permute-start.4 = (f32[136,128]{1,0:T(8,128)S(1)}, f32[136,128]{1,0:T(8,128)S(1)}, u32[]{:S(2)}, u32[]{:S(2)}) collective-permute-start(f32[136,128]{1,0:T(8,128)S(1)} %collective-permute-done.3), channel_id=1, source_target_pairs={{0,2},{1,3},{2,0},{3,1},{4,6},{5,7},{6,4},{7,5},{8,10},{9,11},{10,... | collective-permute-start | bytes 208904 | tf_op jit(solution)/shard_map/ppermute | solution.py:334
  14.5 0.7 %collective-permute-done.5 = f32[136,128]{1,0:T(8,128)S(1)} collective-permute-done((f32[136,128]{1,0:T(8,128)}, f32[136,128]{1,0:T(8,128)S(1)}, u32[]{:S(2)}, u32[]{:S(2)}) %collective-permute-start.5) | collective-permute-done | bytes 69664 | tf_op jit(solution)/shard_map/ppermute | solution.py:334
  15.2 0.8 %collective-permute-start.6 = (f32[136,128]{1,0:T(8,128)S(1)}, f32[136,128]{1,0:T(8,128)S(1)}, u32[]{:S(2)}, u32[]{:S(2)}) collective-permute-start(f32[136,128]{1,0:T(8,128)S(1)} %collective-permute-done.5), channel_id=1, source_target_pairs={{0,2},{1,3},{2,0},{3,1},{4,6},{5,7},{6,4},{7,5},{8,10},{9,11},{10,... | collective-permute-start | bytes 208904 | tf_op jit(solution)/shard_map/ppermute | solution.py:334
  16.1 3.1 %shard_map.67 = (f32[6,128,256]{2,1,0:T(8,128)S(1)}, f32[3,6,128,256]{3,2,1,0:T(8,128)S(1)}, f32[128,128]{1,0:T(8,128)S(1)}, bf16[6,2,256,256]{3,2,1,0:T(8,128)(2,1)S(1)}, bf16[6,2,256,256]{3,2,1,0:T(8,128)(2,1)S(1)}) custom-call(f32[2,136,128]{2,1,0:T(8,128)S(1)} %pad_maximum_fusion.3.near_ref, ...), custom_call_target="tpu_custom_call", output_to_operand_aliasing={{3}: (2, {}), {4}: (3, {})} | custom-call | bytes 1024 | tf_op jit(solution)/shard_map/pallas_call | solution.py:365
  19.2 0.6 %collective-permute-done.1.refs_0_ = f32[2,136,128]{2,1,0:T(8,128)S(1)} collective-permute-done((f32[2,136,128]{2,1,0:T(8,128)S(1)}, f32[2,136,128]{2,1,0:T(8,128)S(1)}, u32[]{:S(2)}, u32[]{:S(2)}) %collective-permute-start.1) | collective-permute-done | bytes 139296 | tf_op jit(solution)/shard_map/ppermute | solution.py:334
  19.9 0.6 %collective-permute-start.8 = (f32[4,136,128]{2,1,0:T(8,128)S(1)}, f32[4,136,128]{2,1,0:T(8,128)S(1)}, u32[]{:S(2)}, u32[]{:S(2)}) collective-permute-start(f32[4,136,128]{2,1,0:T(8,128)S(1)} %pad_maximum_fusion.1), channel_id=1, source_target_pairs={{0,1},{1,0},{2,3},{3,2},{4,5},{5,4},{6,7},{7,6},{8,9},{9,8},{10,11... | collective-permute-start | bytes 835592 | tf_op jit(solution)/shard_map/ppermute | solution.py:334
  20.5 0.6 %collective-permute-done.7 = f32[2,136,128]{2,1,0:T(8,128)S(1)} collective-permute-done((f32[2,136,128]{2,1,0:T(8,128)S(1)}, f32[2,136,128]{2,1,0:T(8,128)S(1)}, u32[]{:S(2)}, u32[]{:S(2)}) %collective-permute-start.7) | collective-permute-done | bytes 139296 | tf_op jit(solution)/shard_map/ppermute | solution.py:334
  21.2 3.1 %shard_map.72 = (f32[6,128,256]{2,1,0:T(8,128)S(1)}, f32[3,6,128,256]{3,2,1,0:T(8,128)S(1)}, f32[128,128]{1,0:T(8,128)S(1)}, bf16[6,2,256,256]{3,2,1,0:T(8,128)(2,1)S(1)}, bf16[6,2,256,256]{3,2,1,0:T(8,128)(2,1)S(1)}) custom-call(f32[4,136,128]{2,1,0:T(8,128)S(1)} %pad_maximum_fusion.2, ...), custom_call_target="tpu_custom_call", output_to_operand_aliasing={{0}: (4, {}), {1}: (5, {}), {2}: (6, {}), {3}: (2, {}), {4}... | custom-call | bytes 1024 | tf_op jit(solution)/shard_map/pallas_call | solution.py:365
  24.6 5.7 %shard_map.75 = (f32[6,128,256]{2,1,0:T(8,128)S(1)}, f32[3,6,128,256]{3,2,1,0:T(8,128)S(1)}, f32[128,128]{1,0:T(8,128)S(1)}, bf16[6,2,256,256]{3,2,1,0:T(8,128)(2,1)S(1)}, bf16[6,2,256,256]{3,2,1,0:T(8,128)(2,1)S(1)}) custom-call(f32[8,136,128]{2,1,0:T(8,128)S(1)} %constant_dynamic-upd, ...), custom_call_target="tpu_custom_call", output_to_operand_aliasing={{0}: (4, {}), {1}: (5, {}), {2}: (6, {}), {3}: (2, {}), {4}... | custom-call | bytes 1024 | tf_op jit(solution)/shard_map/pallas_call | solution.py:365
  30.5 1.1 %collective-permute-done.9.refs_1_ = f32[128,128]{1,0:T(8,128)S(1)} collective-permute-done((f32[128,128]{1,0:T(8,128)S(1)}, f32[128,128]{1,0:T(8,128)S(1)}, u32[]{:S(2)}, u32[]{:S(2)}) %collective-permute-start.9) | collective-permute-done | bytes 65568 | tf_op jit(solution)/shard_map/ppermute | solution.py:334
  31.7 3.1 %shard_map.76 = (f32[6,128,256]{2,1,0:T(8,128)S(1)}, f32[2,128,128]{2,1,0:T(8,128)S(1)}, bf16[6,2,256,256]{3,2,1,0:T(8,128)(2,1)S(1)}) custom-call(f32[8,136,128]{2,1,0:T(8,128)S(1)} %constant_dynamic-update-slice_fusion.near_ref, f32[8,136,128]{2,1,0:T(8,128)S(1)} %pad_maximum_fusion.far_ref, ...), custom_call_target="tpu_custom_call", output_to_operand_aliasing={{2}: (2, {}), {0}: (7, {})} | custom-call | bytes 1024 | tf_op jit(solution)/shard_map/pallas_call | solution.py:402
  34.8 3.1 %shard_map.77 = (f32[6,128,256]{2,1,0:T(8,128)S(1)}, f32[2,128,128]{2,1,0:T(8,128)S(1)}, bf16[6,2,256,256]{3,2,1,0:T(8,128)(2,1)S(1)}) custom-call(f32[8,136,128]{2,1,0:T(8,128)S(1)} %constant_dynamic-update-slice_fusion.near_ref, f32[8,136,128]{2,1,0:T(8,128)S(1)} %pad_maximum_fusion.far_ref, ...), custom_call_target="tpu_custom_call", output_to_operand_aliasing={{2}: (2, {}), {1}: (4, {}), {0}: (5, {})} | custom-call | bytes 1024 | tf_op jit(solution)/shard_map/pallas_call | solution.py:402
  37.9 3.1 %shard_map.78 = (f32[6,128,256]{2,1,0:T(8,128)S(1)}, f32[2,128,128]{2,1,0:T(8,128)S(1)}, bf16[6,2,256,256]{3,2,1,0:T(8,128)(2,1)S(1)}) custom-call(f32[8,136,128]{2,1,0:T(8,128)S(1)} %constant_dynamic-update-slice_fusion.near_ref, f32[8,136,128]{2,1,0:T(8,128)S(1)} %pad_maximum_fusion.far_ref, ...), custom_call_target="tpu_custom_call", output_to_operand_aliasing={{2}: (2, {}), {1}: (4, {}), {0}: (5, {})} | custom-call | bytes 1024 | tf_op jit(solution)/shard_map/pallas_call | solution.py:402
  41.1 3.4 %shard_map.79 = (f32[2,128,128]{2,1,0:T(8,128)S(1)}, bf16[6,2,256,256]{3,2,1,0:T(8,128)(2,1)S(1)}) custom-call(f32[8,136,128]{2,1,0:T(8,128)S(1)} %constant_dynamic-update-slice_fusion.near_ref, f32[8,136,128]{2,1,0:T(8,128)S(1)} %pad_maximum_fusion.far_ref, ...), custom_call_target="tpu_custom_call", output_to_operand_aliasing={{1}: (2, {}), {0}: (4, {})} | custom-call | bytes 1024 | tf_op jit(solution)/shard_map/pallas_call | solution.py:402
  44.7 1.1 %collective-permute-done.10.theirs_ref = f32[128,128]{1,0:T(8,128)S(1)} collective-permute-done((f32[128,128]{1,0:T(8,128)S(1)}, f32[128,128]{1,0:T(8,128)S(1)}, u32[]{:S(2)}, u32[]{:S(2)}) %collective-permute-start.10) | collective-permute-done | bytes 65568 | tf_op jit(solution)/shard_map/ppermute | solution.py:334
  45.8 0.9 %shard_map.81 = f32[1,512,512]{2,1,0:T(8,128)} custom-call(s32[1,2]{1,0:T(1,128)S(1)} %copy-done.2, f32[128,128]{1,0:T(8,128)S(1)} %get-tuple-element.80.ours_ref, f32[128,128]{1,0:T(8,128)S(1)} %collective-permute-done.10.theirs_ref, f32[1,512,512]{2,1,0:T(8,128)} %get-tuple-element.82.zeros_ref), custom_call_target="tpu_custom_call", output_to_operand_aliasing={{}: (3, {})} | custom-call | bytes 1024 | tf_op jit(solution)/shard_map/pallas_call | solution.py:411
  (39 shorter events, 1.0 us)
Async XLA Ops:
  0.7 15.4 %copy-start = (bf16[2,12,128,128]{3,2,1,0:T(8,128)(2,1)S(1)}, bf16[2,12,128,128]{3,2,1,0:T(8,128)(2,1)}, u32[]{:S(2)}) copy-start(bf16[2,12,128,128]{3,2,1,0:T(8,128)(2,1)} %wave_ref.5) | copy-start | bytes 2359300
  3.2 10.4 %copy-start.4 = (f32[136,128]{1,0:T(8,128)S(1)}, f32[136,128]{1,0:T(8,128)}, u32[]{:S(2)}) copy-start(f32[136,128]{1,0:T(8,128)} %shard_map.64) | copy-start | bytes 208900
  3.2 10.4 %collective-permute-start = (f32[136,128]{1,0:T(8,128)}, f32[136,128]{1,0:T(8,128)S(1)}, u32[]{:S(2)}, u32[]{:S(2)}) collective-permute-start(f32[136,128]{1,0:T(8,128)} %shard_map.64), channel_id=1, source_target_pairs={{0,2},{1,3},{2,0},{3,1},{4,6},{5,7},{6,4},{7,5},{8,10},{9,11},{10,... | collective-permute-start | bytes 208904 | tf_op jit(solution)/shard_map/ppermute | solution.py:334
  6.2 7.8 %collective-permute-start.3 = (f32[136,128]{1,0:T(8,128)}, f32[136,128]{1,0:T(8,128)S(1)}, u32[]{:S(2)}, u32[]{:S(2)}) collective-permute-start(f32[136,128]{1,0:T(8,128)} %shard_map.64), channel_id=1, source_target_pairs={{0,8},{1,9},{2,10},{3,11},{4,12},{5,13},{6,14},{7,15},{8,0},{9,1},... | collective-permute-start | bytes 208904 | tf_op jit(solution)/shard_map/ppermute | solution.py:334
  8.8 6.4 %collective-permute-start.5 = (f32[136,128]{1,0:T(8,128)}, f32[136,128]{1,0:T(8,128)S(1)}, u32[]{:S(2)}, u32[]{:S(2)}) collective-permute-start(f32[136,128]{1,0:T(8,128)} %shard_map.64), channel_id=1, source_target_pairs={{0,12},{1,13},{2,14},{3,15},{4,8},{5,9},{6,10},{7,11},{8,4},{9,5},... | collective-permute-start | bytes 208904 | tf_op jit(solution)/shard_map/ppermute | solution.py:334
  11.1 0.7 %copy-start.3 = (f32[128]{0:T(128)S(1)}, f32[128]{0:T(128)}, u32[]{:S(2)}) copy-start(f32[128]{0:T(128)} %param.8) | copy-start | bytes 1540
  13.6 2.5 %collective-permute-start.2 = (f32[2,136,128]{2,1,0:T(8,128)S(1)}, f32[2,136,128]{2,1,0:T(8,128)S(1)}, u32[]{:S(2)}, u32[]{:S(2)}) collective-permute-start(f32[2,136,128]{2,1,0:T(8,128)S(1)} %pad_maximum_fusion.3.near_ref), channel_id=1, source_target_pairs={{0,1},{1,0},{2,3},{3,2},{4,5},{5,4},{6,7},{7,6},{8,9},{9,8},{10,11... | collective-permute-start | bytes 417800 | tf_op jit(solution)/shard_map/ppermute | solution.py:334
  13.7 6.1 %collective-permute-start.1 = (f32[2,136,128]{2,1,0:T(8,128)S(1)}, f32[2,136,128]{2,1,0:T(8,128)S(1)}, u32[]{:S(2)}, u32[]{:S(2)}) collective-permute-start(f32[2,136,128]{2,1,0:T(8,128)S(1)} %pad_maximum_fusion.3.near_ref), channel_id=1, source_target_pairs={{0,4},{1,5},{2,6},{3,7},{4,0},{5,1},{6,2},{7,3},{8,12},{9,13},{10,... | collective-permute-start | bytes 417800 | tf_op jit(solution)/shard_map/ppermute | solution.py:334
  14.0 5.8 %collective-permute-start.4 = (f32[136,128]{1,0:T(8,128)S(1)}, f32[136,128]{1,0:T(8,128)S(1)}, u32[]{:S(2)}, u32[]{:S(2)}) collective-permute-start(f32[136,128]{1,0:T(8,128)S(1)} %collective-permute-done.3), channel_id=1, source_target_pairs={{0,2},{1,3},{2,0},{3,1},{4,6},{5,7},{6,4},{7,5},{8,10},{9,11},{10,... | collective-permute-start | bytes 208904 | tf_op jit(solution)/shard_map/ppermute | solution.py:334
  15.2 4.6 %collective-permute-start.6 = (f32[136,128]{1,0:T(8,128)S(1)}, f32[136,128]{1,0:T(8,128)S(1)}, u32[]{:S(2)}, u32[]{:S(2)}) collective-permute-start(f32[136,128]{1,0:T(8,128)S(1)} %collective-permute-done.5), channel_id=1, source_target_pairs={{0,2},{1,3},{2,0},{3,1},{4,6},{5,7},{6,4},{7,5},{8,10},{9,11},{10,... | collective-permute-start | bytes 208904 | tf_op jit(solution)/shard_map/ppermute | solution.py:334
  19.8 1.4 %collective-permute-start.7 = (f32[2,136,128]{2,1,0:T(8,128)S(1)}, f32[2,136,128]{2,1,0:T(8,128)S(1)}, u32[]{:S(2)}, u32[]{:S(2)}) collective-permute-start(f32[2,136,128]{2,1,0:T(8,128)S(1)} %shard_map.68), channel_id=1, source_target_pairs={{0,1},{1,0},{2,3},{3,2},{4,5},{5,4},{6,7},{7,6},{8,9},{9,8},{10,11... | collective-permute-start | bytes 417800 | tf_op jit(solution)/shard_map/ppermute | solution.py:334
  19.9 4.4 %collective-permute-start.8 = (f32[4,136,128]{2,1,0:T(8,128)S(1)}, f32[4,136,128]{2,1,0:T(8,128)S(1)}, u32[]{:S(2)}, u32[]{:S(2)}) collective-permute-start(f32[4,136,128]{2,1,0:T(8,128)S(1)} %pad_maximum_fusion.1), channel_id=1, source_target_pairs={{0,1},{1,0},{2,3},{3,2},{4,5},{5,4},{6,7},{7,6},{8,9},{9,8},{10,11... | collective-permute-start | bytes 835592 | tf_op jit(solution)/shard_map/ppermute | solution.py:334
  24.6 7.1 %copy-start.1 = (f32[1,128,128]{2,1,0:T(8,128)S(1)}, f32[1,128,128]{2,1,0:T(8,128)}, u32[]{:S(2)}) copy-start(f32[1,128,128]{2,1,0:T(8,128)} %refs_2_.1) | copy-start | bytes 196612
  30.3 1.3 %collective-permute-start.9 = (f32[128,128]{1,0:T(8,128)S(1)}, f32[128,128]{1,0:T(8,128)S(1)}, u32[]{:S(2)}, u32[]{:S(2)}) collective-permute-start(f32[128,128]{1,0:T(8,128)S(1)} %get-tuple-element.68.refs_0_), channel_id=1, source_target_pairs={{0,1},{1,0},{2,3},{3,2},{4,5},{5,4},{6,7},{7,6},{8,9},{9,8},{10,11... | collective-permute-start | bytes 196616 | tf_op jit(solution)/shard_map/ppermute | solution.py:334
  41.1 4.7 %copy-start.2 = (s32[1,2]{1,0:T(1,128)S(1)}, s32[1,2]{1,0:T(1,128)}, u32[]{:S(2)}) copy-start(s32[1,2]{1,0:T(1,128)} %offsets_ref.1) | copy-start | bytes 28
  44.5 1.3 %collective-permute-start.10 = (f32[128,128]{1,0:T(8,128)S(1)}, f32[128,128]{1,0:T(8,128)S(1)}, u32[]{:S(2)}, u32[]{:S(2)}) collective-permute-start(f32[128,128]{1,0:T(8,128)S(1)} %get-tuple-element.81), channel_id=1, source_target_pairs={{0,1},{1,0},{2,3},{3,2},{4,5},{5,4},{6,7},{7,6},{8,9},{9,8},{10,11... | collective-permute-start | bytes 196616 | tf_op jit(solution)/shard_map/ppermute | solution.py:334

commit v4 on v3

--- a/solution.py
+++ b/solution.py
@@ -71,8 +71,12 @@
     )
 
 
-def extract_kernel(offsets_hbm, thickness_hbm, potential_ref, out_ref, window, offsets_ref, thickness_ref, sems):
+def extract_kernel(
+    offsets_hbm, thickness_hbm, phase_hbm, potential_ref, out_ref, window, offsets_ref, thickness_ref, phase_ref, sems
+):
     size = out_ref.shape[1]
+    phases = pltpu.make_async_copy(phase_hbm, phase_ref, sems.at[3])
+    phases.start()
     corner = pltpu.make_async_copy(offsets_hbm, offsets_ref, sems.at[0])
     steps = pltpu.make_async_copy(thickness_hbm, thickness_ref, sems.at[1])
     corner.start()
@@ -86,7 +90,9 @@
     )
     copy.start()
     steps.wait()
-    out_ref[size:, :] = jnp.full((8, size), thickness_ref[0].astype(F32))
+    phases.wait()
+    row = lax.broadcasted_iota(jnp.int32, (8, size), 0)
+    out_ref[size:, :] = jnp.where(row == 1, phase_ref[...], thickness_ref[0].astype(F32))
     copy.wait()
     part = pltpu.roll(window[...], lax.rem(size + 8 - down, size + 8), 0)[:size]
     shift = lax.rem(size - across, size)
@@ -114,8 +120,8 @@
     copy.wait()
 
 
-def table_kernel(phase_ref, forward_ref, backward_ref, zeros_ref, blank, sem):
-    size = phase_ref.shape[1]
+def table_kernel(message_ref, forward_ref, backward_ref, zeros_ref, blank, sem):
+    size = message_ref.shape[1]
     blank[...] = jnp.zeros_like(blank)
     copies = [
         pltpu.make_async_copy(blank, zeros_ref.at[0, pl.ds(row, size)], sem.at[k])
@@ -144,7 +150,7 @@
                 ref[index, 1, r : r + size, k : k + size] = low
 
     for steps in (1, 2, 3):
-        h_real, h_imag = sincos(phase_ref[...] * float(steps))
+        h_real, h_imag = sincos(message_ref[size + 1 : size + 2, :] * float(steps))
         real = c * h_real + s * h_imag
         imag = c * h_imag - s * h_real
         put(2 + steps, real * (1.0 / math.sqrt(size)), imag * (1.0 / math.sqrt(size)))
@@ -335,12 +341,18 @@
 
     (message,) = call(
         extract_kernel,
-        [HBM, HBM, HBM],
+        [HBM, HBM, HBM, HBM],
         [shaped(size + 8, size)],
         None,
-        [window, pltpu.SMEM((1, 2), jnp.int32), pltpu.SMEM((1,), jnp.int32), dma((3,))],
+        [
+            window,
+            pltpu.SMEM((1, 2), jnp.int32),
+            pltpu.SMEM((1,), jnp.int32),
+            pltpu.VMEM((1, size), F32),
+            dma((4,)),
+        ],
         limit=63 * 2**20,
-    )(offsets, thickness, potential)
+    )(offsets, thickness, propagator_phase.reshape(1, size), potential)
     received = flipped(message, 2)
     forward_table, backward_table, zeros = call(
         table_kernel,
@@ -348,8 +360,8 @@
         [table, table, shaped(*potential.shape)],
         [VMEM, VMEM, HBM],
         [pltpu.VMEM((size, potential.shape[2]), F32), dma((potential.shape[1] // size,))],
-    )(propagator_phase.reshape(1, size))
-    near = jnp.stack([message, after(received, forward_table)])
+    )(message)
+    near = after(jnp.stack([message, received]), forward_table)
     far = flipped(near, 1)
     beside = flipped(near, CLUSTER)
     halves = [flipped(message, CLUSTER * k) for k in range(2, chunks)]

time: 47.1 us -> 46.4 us (0.985)
  waiting for transfers between devices: 4.11 us -> 4.88 us
  starting transfers between devices: 9.72 us -> 8.97 us
  local copies, waits for them, and re-layouts: 1.66 us -> 1 us
    ppermute x11, waiting for transfers between devices: 4.11 us -> 4.88 us  [flipped(): return lax.ppermute(block, 'slc', [(i, i ^ bit) for i in range(length)])]
    ppermute x11, starting transfers between devices: 9.72 us -> 8.97 us  [flipped(): return lax.ppermute(block, 'slc', [(i, i ^ bit) for i in range(length)])]
    unnamed x17 -> x14, local copies, waits for them, and re-layouts: 1.65 us -> 0.99 us
  transfers between devices with their start and end apart: 11 -> 11, of which waited for: 5 -> 7; matrix products, arithmetic and copies ran while one was open for 2% -> 0% of each run, Pallas kernels for 17% -> 17%
where the time goes in v4:
time: 46.4 us; the launch traced here: 46.2 us
  Pallas kernels  30.1 us (65%)
  starting transfers between devices  8.97 us (19%)
  waiting for transfers between devices  4.88 us (11%)
  between operations  1.1 us (2%)
  local copies, waits for them, and re-layouts  1 us (2%)
    pallas_call x4, Pallas kernels, local(): call(functools.partial(backward_kernel, chunk, last), [VMEM] * len(ins),...  12.7 us
    pallas_call x5, Pallas kernels, forward(): call(functools.partial(forward_kernel, condition, span, last), [VMEM] * l...  12.1 us
    ppermute x11, starting transfers between devices, flipped(): return lax.ppermute(block, 'slc', [(i, i ^ bit) for i in range(length)])  8.97 us
    ppermute x11, waiting for transfers between devices, flipped(): return lax.ppermute(block, 'slc', [(i, i ^ bit) for i in range(length)])  4.88 us
    pallas_call x1, Pallas kernels, local(): call(extract_kernel, [HBM, HBM, HBM, HBM], [shaped(size + 8, size)], None...  2.49 us
    pallas_call x1, Pallas kernels, local(): call(table_kernel, [VMEM], [table, table, shaped(*potential.shape)], [VME...  1.85 us
    unnamed x14, local copies, waits for them, and re-layouts  0.99 us
  transfers between devices with their start and end apart: 11, of which 7 were waited for; matrix products, arithmetic and copies ran while one was open for 0% of the time, Pallas kernels for 17%

profile of v4, /device:TPU:0, one launch (start us, length us, event | category | flops | bytes accessed | tf_op | source)
XLA Modules:
  0.0 46.2 jit_solution(6046078265531649654)
XLA Ops:
  0.7 2.5 %shard_map.64.message_ref = f32[136,128]{1,0:T(8,128)} custom-call(s32[1,2]{1,0:T(1,128)} %offsets_ref.1, s32[1]{0:T(128)S(6)} %copy.89.thickness_hbm, f32[1,128]{1,0:T(1,128)} %bitcast.17, f32[1,512,512]{2,1,0:T(8,128)} %potential_ref.1), custom_call_target="tpu_custom_call" | custom-call | bytes 1024 | tf_op jit(solution)/shard_map/pallas_call | solution.py:342
  3.2 3.0 %collective-permute-start = (f32[136,128]{1,0:T(8,128)}, f32[136,128]{1,0:T(8,128)S(1)}, u32[]{:S(2)}, u32[]{:S(2)}) collective-permute-start(f32[136,128]{1,0:T(8,128)} %shard_map.64.message_ref), channel_id=1, source_target_pairs={{0,2},{1,3},{2,0},{3,1},{4,6},{5,7},{6,4},{7,5},{8,10},{9,11},{10,... | collective-permute-start | bytes 208904 | tf_op jit(solution)/shard_map/ppermute | solution.py:340
  6.2 2.6 %collective-permute-start.3 = (f32[136,128]{1,0:T(8,128)}, f32[136,128]{1,0:T(8,128)S(1)}, u32[]{:S(2)}, u32[]{:S(2)}) collective-permute-start(f32[136,128]{1,0:T(8,128)} %shard_map.64.message_ref), channel_id=1, source_target_pairs={{0,8},{1,9},{2,10},{3,11},{4,12},{5,13},{6,14},{7,15},{8,0},{9,1},... | collective-permute-start | bytes 208904 | tf_op jit(solution)/shard_map/ppermute | solution.py:340
  8.8 1.3 %collective-permute-start.5 = (f32[136,128]{1,0:T(8,128)}, f32[136,128]{1,0:T(8,128)S(1)}, u32[]{:S(2)}, u32[]{:S(2)}) collective-permute-start(f32[136,128]{1,0:T(8,128)} %shard_map.64.message_ref), channel_id=1, source_target_pairs={{0,12},{1,13},{2,14},{3,15},{4,8},{5,9},{6,10},{7,11},{8,4},{9,5},... | collective-permute-start | bytes 208904 | tf_op jit(solution)/shard_map/ppermute | solution.py:340
  10.1 0.9 %copy-done.1 = f32[136,128]{1,0:T(8,128)S(1)} copy-done((f32[136,128]{1,0:T(8,128)S(1)}, f32[136,128]{1,0:T(8,128)}, u32[]{:S(2)}) %copy-start.1) | copy-done | bytes 69656
  11.0 1.9 %shard_map.65 = (bf16[6,2,256,256]{3,2,1,0:T(8,128)(2,1)S(1)}, bf16[6,2,256,256]{3,2,1,0:T(8,128)(2,1)S(1)}, f32[1,512,512]{2,1,0:T(8,128)}) custom-call(f32[136,128]{1,0:T(8,128)S(1)} %copy-done.1), custom_call_target="tpu_custom_call" | custom-call | bytes 1024 | tf_op jit(solution)/shard_map/pallas_call | solution.py:357
  13.0 0.3 collective-permute-start.1
  13.6 0.5 %collective-permute-start.4 = (f32[136,128]{1,0:T(8,128)S(1)}, f32[136,128]{1,0:T(8,128)S(1)}, u32[]{:S(2)}, u32[]{:S(2)}) collective-permute-start(f32[136,128]{1,0:T(8,128)S(1)} %collective-permute-done.3), channel_id=1, source_target_pairs={{0,2},{1,3},{2,0},{3,1},{4,6},{5,7},{6,4},{7,5},{8,10},{9,11},{10,... | collective-permute-start | bytes 208904 | tf_op jit(solution)/shard_map/ppermute | solution.py:340
  14.0 1.2 %collective-permute-done.5 = f32[136,128]{1,0:T(8,128)S(1)} collective-permute-done((f32[136,128]{1,0:T(8,128)}, f32[136,128]{1,0:T(8,128)S(1)}, u32[]{:S(2)}, u32[]{:S(2)}) %collective-permute-start.5) | collective-permute-done | bytes 69664 | tf_op jit(solution)/shard_map/ppermute | solution.py:340
  15.2 0.5 %collective-permute-start.6 = (f32[136,128]{1,0:T(8,128)S(1)}, f32[136,128]{1,0:T(8,128)S(1)}, u32[]{:S(2)}, u32[]{:S(2)}) collective-permute-start(f32[136,128]{1,0:T(8,128)S(1)} %collective-permute-done.5), channel_id=1, source_target_pairs={{0,2},{1,3},{2,0},{3,1},{4,6},{5,7},{6,4},{7,5},{8,10},{9,11},{10,... | collective-permute-start | bytes 208904 | tf_op jit(solution)/shard_map/ppermute | solution.py:340
  15.8 3.1 %shard_map.67 = (f32[6,128,256]{2,1,0:T(8,128)S(1)}, f32[3,6,128,256]{3,2,1,0:T(8,128)S(1)}, f32[128,128]{1,0:T(8,128)S(1)}, bf16[6,2,256,256]{3,2,1,0:T(8,128)(2,1)S(1)}, bf16[6,2,256,256]{3,2,1,0:T(8,128)(2,1)S(1)}) custom-call(f32[2,136,128]{2,1,0:T(8,128)S(1)} %shard_map.66.near_ref, ...), custom_call_target="tpu_custom_call", output_to_operand_aliasing={{3}: (2, {}), {4}: (3, {})} | custom-call | bytes 1024 | tf_op jit(solution)/shard_map/pallas_call | solution.py:377
  18.9 0.3 collective-permute-done.1.refs_0_
  19.1 0.4 collective-permute-done.6.refs_0_
  19.9 0.6 %collective-permute-done.7 = f32[2,136,128]{2,1,0:T(8,128)S(1)} collective-permute-done((f32[2,136,128]{2,1,0:T(8,128)S(1)}, f32[2,136,128]{2,1,0:T(8,128)S(1)}, u32[]{:S(2)}, u32[]{:S(2)}) %collective-permute-start.7) | collective-permute-done | bytes 139296 | tf_op jit(solution)/shard_map/ppermute | solution.py:340
  20.5 3.1 %shard_map.72 = (f32[6,128,256]{2,1,0:T(8,128)S(1)}, f32[3,6,128,256]{3,2,1,0:T(8,128)S(1)}, f32[128,128]{1,0:T(8,128)S(1)}, bf16[6,2,256,256]{3,2,1,0:T(8,128)(2,1)S(1)}, bf16[6,2,256,256]{3,2,1,0:T(8,128)(2,1)S(1)}) custom-call(f32[4,136,128]{2,1,0:T(8,128)S(1)} %pad_maximum_fusion.2, ...), custom_call_target="tpu_custom_call", output_to_operand_aliasing={{0}: (4, {}), {1}: (5, {}), {2}: (6, {}), {3}: (2, {}), {4}... | custom-call | bytes 1024 | tf_op jit(solution)/shard_map/pallas_call | solution.py:377
  23.9 5.7 %shard_map.75 = (f32[6,128,256]{2,1,0:T(8,128)S(1)}, f32[3,6,128,256]{3,2,1,0:T(8,128)S(1)}, f32[128,128]{1,0:T(8,128)S(1)}, bf16[6,2,256,256]{3,2,1,0:T(8,128)(2,1)S(1)}, bf16[6,2,256,256]{3,2,1,0:T(8,128)(2,1)S(1)}) custom-call(f32[8,136,128]{2,1,0:T(8,128)S(1)} %constant_dynamic-upd, ...), custom_call_target="tpu_custom_call", output_to_operand_aliasing={{0}: (4, {}), {1}: (5, {}), {2}: (6, {}), {3}: (2, {}), {4}... | custom-call | bytes 1024 | tf_op jit(solution)/shard_map/pallas_call | solution.py:377
  29.9 1.1 %collective-permute-done.9.refs_1_ = f32[128,128]{1,0:T(8,128)S(1)} collective-permute-done((f32[128,128]{1,0:T(8,128)S(1)}, f32[128,128]{1,0:T(8,128)S(1)}, u32[]{:S(2)}, u32[]{:S(2)}) %collective-permute-start.9) | collective-permute-done | bytes 65568 | tf_op jit(solution)/shard_map/ppermute | solution.py:340
  31.0 3.1 %shard_map.76 = (f32[6,128,256]{2,1,0:T(8,128)S(1)}, f32[2,128,128]{2,1,0:T(8,128)S(1)}, bf16[6,2,256,256]{3,2,1,0:T(8,128)(2,1)S(1)}) custom-call(f32[8,136,128]{2,1,0:T(8,128)S(1)} %constant_dynamic-update-slice_fusion.near_ref, f32[8,136,128]{2,1,0:T(8,128)S(1)} %pad_maximum_fusion.far_ref, ...), custom_call_target="tpu_custom_call", output_to_operand_aliasing={{2}: (2, {}), {0}: (7, {})} | custom-call | bytes 1024 | tf_op jit(solution)/shard_map/pallas_call | solution.py:414
  34.1 3.1 %shard_map.77 = (f32[6,128,256]{2,1,0:T(8,128)S(1)}, f32[2,128,128]{2,1,0:T(8,128)S(1)}, bf16[6,2,256,256]{3,2,1,0:T(8,128)(2,1)S(1)}) custom-call(f32[8,136,128]{2,1,0:T(8,128)S(1)} %constant_dynamic-update-slice_fusion.near_ref, f32[8,136,128]{2,1,0:T(8,128)S(1)} %pad_maximum_fusion.far_ref, ...), custom_call_target="tpu_custom_call", output_to_operand_aliasing={{2}: (2, {}), {1}: (4, {}), {0}: (5, {})} | custom-call | bytes 1024 | tf_op jit(solution)/shard_map/pallas_call | solution.py:414
  37.2 3.1 %shard_map.78 = (f32[6,128,256]{2,1,0:T(8,128)S(1)}, f32[2,128,128]{2,1,0:T(8,128)S(1)}, bf16[6,2,256,256]{3,2,1,0:T(8,128)(2,1)S(1)}) custom-call(f32[8,136,128]{2,1,0:T(8,128)S(1)} %constant_dynamic-update-slice_fusion.near_ref, f32[8,136,128]{2,1,0:T(8,128)S(1)} %pad_maximum_fusion.far_ref, ...), custom_call_target="tpu_custom_call", output_to_operand_aliasing={{2}: (2, {}), {1}: (4, {}), {0}: (5, {})} | custom-call | bytes 1024 | tf_op jit(solution)/shard_map/pallas_call | solution.py:414
  40.4 3.4 %shard_map.79 = (f32[2,128,128]{2,1,0:T(8,128)S(1)}, bf16[6,2,256,256]{3,2,1,0:T(8,128)(2,1)S(1)}) custom-call(f32[8,136,128]{2,1,0:T(8,128)S(1)} %constant_dynamic-update-slice_fusion.near_ref, f32[8,136,128]{2,1,0:T(8,128)S(1)} %pad_maximum_fusion.far_ref, ...), custom_call_target="tpu_custom_call", output_to_operand_aliasing={{1}: (2, {}), {0}: (4, {})} | custom-call | bytes 1024 | tf_op jit(solution)/shard_map/pallas_call | solution.py:414
  43.8 0.2 collective-permute-start.10
  44.0 1.1 %collective-permute-done.10.theirs_ref = f32[128,128]{1,0:T(8,128)S(1)} collective-permute-done((f32[128,128]{1,0:T(8,128)S(1)}, f32[128,128]{1,0:T(8,128)S(1)}, u32[]{:S(2)}, u32[]{:S(2)}) %collective-permute-start.10) | collective-permute-done | bytes 65568 | tf_op jit(solution)/shard_map/ppermute | solution.py:340
  45.1 0.9 %shard_map.81 = f32[1,512,512]{2,1,0:T(8,128)} custom-call(s32[1,2]{1,0:T(1,128)S(1)} %copy-done.3, f32[128,128]{1,0:T(8,128)S(1)} %get-tuple-element.80.ours_ref, f32[128,128]{1,0:T(8,128)S(1)} %collective-permute-done.10.theirs_ref, f32[1,512,512]{2,1,0:T(8,128)} %get-tuple-element.82.zeros_ref), custom_call_target="tpu_custom_call", output_to_operand_aliasing={{}: (3, {})} | custom-call | bytes 1024 | tf_op jit(solution)/shard_map/pallas_call | solution.py:423
  (36 shorter events, 1.1 us)
Async XLA Ops:
  0.7 15.1 %copy-start = (bf16[2,12,128,128]{3,2,1,0:T(8,128)(2,1)S(1)}, bf16[2,12,128,128]{3,2,1,0:T(8,128)(2,1)}, u32[]{:S(2)}) copy-start(bf16[2,12,128,128]{3,2,1,0:T(8,128)(2,1)} %wave_ref.5) | copy-start | bytes 2359300
  3.2 9.8 %collective-permute-start = (f32[136,128]{1,0:T(8,128)}, f32[136,128]{1,0:T(8,128)S(1)}, u32[]{:S(2)}, u32[]{:S(2)}) collective-permute-start(f32[136,128]{1,0:T(8,128)} %shard_map.64.message_ref), channel_id=1, source_target_pairs={{0,2},{1,3},{2,0},{3,1},{4,6},{5,7},{6,4},{7,5},{8,10},{9,11},{10,... | collective-permute-start | bytes 208904 | tf_op jit(solution)/shard_map/ppermute | solution.py:340
  6.2 7.4 %collective-permute-start.3 = (f32[136,128]{1,0:T(8,128)}, f32[136,128]{1,0:T(8,128)S(1)}, u32[]{:S(2)}, u32[]{:S(2)}) collective-permute-start(f32[136,128]{1,0:T(8,128)} %shard_map.64.message_ref), channel_id=1, source_target_pairs={{0,8},{1,9},{2,10},{3,11},{4,12},{5,13},{6,14},{7,15},{8,0},{9,1},... | collective-permute-start | bytes 208904 | tf_op jit(solution)/shard_map/ppermute | solution.py:340
  8.8 6.4 %collective-permute-start.5 = (f32[136,128]{1,0:T(8,128)}, f32[136,128]{1,0:T(8,128)S(1)}, u32[]{:S(2)}, u32[]{:S(2)}) collective-permute-start(f32[136,128]{1,0:T(8,128)} %shard_map.64.message_ref), channel_id=1, source_target_pairs={{0,12},{1,13},{2,14},{3,15},{4,8},{5,9},{6,10},{7,11},{8,4},{9,5},... | collective-permute-start | bytes 208904 | tf_op jit(solution)/shard_map/ppermute | solution.py:340
  10.1 0.9 %copy-start.1 = (f32[136,128]{1,0:T(8,128)S(1)}, f32[136,128]{1,0:T(8,128)}, u32[]{:S(2)}) copy-start(f32[136,128]{1,0:T(8,128)} %shard_map.64.message_ref) | copy-start | bytes 208900
  13.0 2.8 %collective-permute-start.2 = (f32[2,136,128]{2,1,0:T(8,128)S(1)}, f32[2,136,128]{2,1,0:T(8,128)S(1)}, u32[]{:S(2)}, u32[]{:S(2)}) collective-permute-start(f32[2,136,128]{2,1,0:T(8,128)S(1)} %shard_map.66.near_ref), channel_id=1, source_target_pairs={{0,1},{1,0},{2,3},{3,2},{4,5},{5,4},{6,7},{7,6},{8,9},{9,8},{10,11... | collective-permute-start | bytes 417800 | tf_op jit(solution)/shard_map/ppermute | solution.py:340
  13.0 6.1 %collective-permute-start.1 = (f32[2,136,128]{2,1,0:T(8,128)S(1)}, f32[2,136,128]{2,1,0:T(8,128)S(1)}, u32[]{:S(2)}, u32[]{:S(2)}) collective-permute-start(f32[2,136,128]{2,1,0:T(8,128)S(1)} %shard_map.66.near_ref), channel_id=1, source_target_pairs={{0,4},{1,5},{2,6},{3,7},{4,0},{5,1},{6,2},{7,3},{8,12},{9,13},{10,... | collective-permute-start | bytes 417800 | tf_op jit(solution)/shard_map/ppermute | solution.py:340
  13.6 5.6 %collective-permute-start.4 = (f32[136,128]{1,0:T(8,128)S(1)}, f32[136,128]{1,0:T(8,128)S(1)}, u32[]{:S(2)}, u32[]{:S(2)}) collective-permute-start(f32[136,128]{1,0:T(8,128)S(1)} %collective-permute-done.3), channel_id=1, source_target_pairs={{0,2},{1,3},{2,0},{3,1},{4,6},{5,7},{6,4},{7,5},{8,10},{9,11},{10,... | collective-permute-start | bytes 208904 | tf_op jit(solution)/shard_map/ppermute | solution.py:340
  15.2 4.3 %collective-permute-start.6 = (f32[136,128]{1,0:T(8,128)S(1)}, f32[136,128]{1,0:T(8,128)S(1)}, u32[]{:S(2)}, u32[]{:S(2)}) collective-permute-start(f32[136,128]{1,0:T(8,128)S(1)} %collective-permute-done.5), channel_id=1, source_target_pairs={{0,2},{1,3},{2,0},{3,1},{4,6},{5,7},{6,4},{7,5},{8,10},{9,11},{10,... | collective-permute-start | bytes 208904 | tf_op jit(solution)/shard_map/ppermute | solution.py:340
  19.1 1.4 %collective-permute-start.7 = (f32[2,136,128]{2,1,0:T(8,128)S(1)}, f32[2,136,128]{2,1,0:T(8,128)S(1)}, u32[]{:S(2)}, u32[]{:S(2)}) collective-permute-start(f32[2,136,128]{2,1,0:T(8,128)S(1)} %shard_map.68), channel_id=1, source_target_pairs={{0,1},{1,0},{2,3},{3,2},{4,5},{5,4},{6,7},{7,6},{8,9},{9,8},{10,11... | collective-permute-start | bytes 417800 | tf_op jit(solution)/shard_map/ppermute | solution.py:340
  19.5 4.1 %collective-permute-start.8 = (f32[4,136,128]{2,1,0:T(8,128)S(1)}, f32[4,136,128]{2,1,0:T(8,128)S(1)}, u32[]{:S(2)}, u32[]{:S(2)}) collective-permute-start(f32[4,136,128]{2,1,0:T(8,128)S(1)} %pad_maximum_fusion.1), channel_id=1, source_target_pairs={{0,1},{1,0},{2,3},{3,2},{4,5},{5,4},{6,7},{7,6},{8,9},{9,8},{10,11... | collective-permute-start | bytes 835592 | tf_op jit(solution)/shard_map/ppermute | solution.py:340
  23.9 7.1 %copy-start.2 = (f32[1,128,128]{2,1,0:T(8,128)S(1)}, f32[1,128,128]{2,1,0:T(8,128)}, u32[]{:S(2)}) copy-start(f32[1,128,128]{2,1,0:T(8,128)} %refs_2_.1) | copy-start | bytes 196612
  29.6 1.3 %collective-permute-start.9 = (f32[128,128]{1,0:T(8,128)S(1)}, f32[128,128]{1,0:T(8,128)S(1)}, u32[]{:S(2)}, u32[]{:S(2)}) collective-permute-start(f32[128,128]{1,0:T(8,128)S(1)} %get-tuple-element.68.refs_0_), channel_id=1, source_target_pairs={{0,1},{1,0},{2,3},{3,2},{4,5},{5,4},{6,7},{7,6},{8,9},{9,8},{10,11... | collective-permute-start | bytes 196616 | tf_op jit(solution)/shard_map/ppermute | solution.py:340
  40.4 4.7 %copy-start.3 = (s32[1,2]{1,0:T(1,128)S(1)}, s32[1,2]{1,0:T(1,128)}, u32[]{:S(2)}) copy-start(s32[1,2]{1,0:T(1,128)} %offsets_ref.1) | copy-start | bytes 28
  43.8 1.3 %collective-permute-start.10 = (f32[128,128]{1,0:T(8,128)S(1)}, f32[128,128]{1,0:T(8,128)S(1)}, u32[]{:S(2)}, u32[]{:S(2)}) collective-permute-start(f32[128,128]{1,0:T(8,128)S(1)} %get-tuple-element.81), channel_id=1, source_target_pairs={{0,1},{1,0},{2,3},{3,2},{4,5},{5,4},{6,7},{7,6},{8,9},{9,8},{10,11... | collective-permute-start | bytes 196616 | tf_op jit(solution)/shard_map/ppermute | solution.py:340

commit v5 on v4

--- a/solution.py
+++ b/solution.py
@@ -234,12 +234,12 @@
     pl.when(condition(layer))(run)
 
 
-def backward_kernel(chunk, last, near_ref, far_ref, table_ref, kept_ref, *refs):
+def backward_kernel(low_end, high_end, last, near_ref, far_ref, table_ref, kept_ref, *refs):
     if last:
         mine_ref, theirs_ref, measured_ref, *refs = refs
     else:
         refs = refs[1:]
-    wave_ref, *outs, ours_ref, _, update = refs
+    wave_ref, *outs, ours_ref, _, pulled = refs
     rank, layer = position()
 
     size = near_ref.shape[2]
@@ -251,7 +251,7 @@
             misfit = mine_ref[...] + theirs_ref[...] - measured_ref[0]
             misfit = jnp.concatenate([misfit, misfit], axis=1)
             waves = [wave * misfit for wave in waves]
-        slices = range(CLUSTER * chunk, CLUSTER * (chunk + 1))
+        slices = range(CLUSTER * low_end, CLUSTER * high_end)
         for index in reversed(slices):
             at = index ^ rank
             kind, cosine, sine = patch_of(near_ref, far_ref, at, size)
@@ -260,30 +260,37 @@
             if index % 2 == 1:
                 cosine, sine = cosine.T, sine.T
             high, low = table_ref[kind, 0], table_ref[kind, 1]
-            slot = jnp.minimum(at, 2)
             after = []
-            gradient = None
             for m in range(modes):
                 mu = two_sided(waves[m], high, low, size)
+                pulled[index - slices[0], m] = mu
                 real, imag = mu[:, :size], mu[:, size:]
-                u = kept_ref[slot, m]
-                term = imag * u[:, :size] - real * u[:, size:]
-                gradient = term if gradient is None else gradient + term
                 if index > 0:
                     after.append(
                         jnp.concatenate(
                             [cosine * real + sine * imag, cosine * imag - sine * real], axis=1
                         )
                     )
-            update[slot] = gradient.T if index % 2 == 1 else gradient
             waves = after
-        ours_ref[0] = update[0]
-        ours_ref[1] = update[1]
         for out_ref in outs:
             for m, wave in enumerate(waves):
                 out_ref[m] = wave
 
-    pl.when(layer <= chunk)(run)
+    def finish():
+        place = rank % CLUSTER
+        for odd in range(2):
+            index = place // 2 * 2 + odd
+            slot = index ^ place
+            index = index + CLUSTER * (layer - low_end)
+            gradient = None
+            for m in range(modes):
+                mu, u = pulled[index, m], kept_ref[slot, m]
+                term = mu[:, size:] * u[:, :size] - mu[:, :size] * u[:, size:]
+                gradient = term if gradient is None else gradient + term
+            ours_ref[slot] = gradient.T if odd else gradient
+
+    pl.when(layer < high_end)(run)
+    pl.when(jnp.logical_and(layer >= low_end, layer < high_end))(finish)
 
 
 def choose_kernel(ours_ref, own_ref, other_ref):
@@ -402,21 +409,22 @@
     backward_table = tables[1]
     ours, waves = None, [waves]
     extra = (power, flipped(power, 1), measured)
-    for chunk in reversed(range(chunks)):
-        last = chunk == chunks - 1
+    spans = [(chunks - 2, chunks)] + [(k, k + 1) for k in reversed(range(chunks - 2))]
+    for low_end, high_end in spans:
+        last = high_end == chunks
         ins = [blocks, others, backward_table, kept, *(extra if last else (ours,)), *waves]
-        outs = [wave] if chunk > 0 else []
+        outs = [wave] if low_end > 0 else []
         aliases = {2: len(outs) + 1}
         if not last:
             aliases[4] = len(outs)
         if outs:
             aliases[len(ins) - 1] = 0
         *waves, ours, backward_table = call(
-            functools.partial(backward_kernel, chunk, last),
+            functools.partial(backward_kernel, low_end, high_end, last),
             [VMEM] * len(ins),
             outs + [pair, table],
             None,
-            [pltpu.VMEM((3, size, size), F32)],
+            [pltpu.VMEM((CLUSTER * (high_end - low_end), *wave.shape), F32)],
             input_output_aliases=aliases,
         )(*ins)
     own, other = call(choose_kernel, [VMEM], [panel, panel])(ours)

time: 46.4 us -> 45.6 us (0.983)
  Pallas kernels: 30.1 us -> 29.3 us
    pallas_call x4 -> x3, Pallas kernels: 12.7 us -> 12 us  [local(): call(functools.partial(backward_kernel, low_end, high_end, last), [VMEM]...]
  transfers between devices with their start and end apart: 11 -> 11, of which waited for: 7 -> 7; matrix products, arithmetic and copies ran while one was open for 0% -> 0% of each run, Pallas kernels for 17% -> 18%
where the time goes in v5:
time: 45.6 us; the launch traced here: 45.4 us
  Pallas kernels  29.3 us (64%)
  starting transfers between devices  8.97 us (20%)
  waiting for transfers between devices  4.88 us (11%)
  between operations  1.07 us (2%)
  local copies, waits for them, and re-layouts  1 us (2%)
    pallas_call x5, Pallas kernels, forward(): call(functools.partial(forward_kernel, condition, span, last), [VMEM] * l...  12.1 us
    pallas_call x3, Pallas kernels, local(): call(functools.partial(backward_kernel, low_end, high_end, last), [VMEM]...  12 us
    ppermute x11, starting transfers between devices, flipped(): return lax.ppermute(block, 'slc', [(i, i ^ bit) for i in range(length)])  8.97 us
    ppermute x11, waiting for transfers between devices, flipped(): return lax.ppermute(block, 'slc', [(i, i ^ bit) for i in range(length)])  4.88 us
    pallas_call x1, Pallas kernels, local(): call(extract_kernel, [HBM, HBM, HBM, HBM], [shaped(size + 8, size)], None...  2.5 us
    pallas_call x1, Pallas kernels, local(): call(table_kernel, [VMEM], [table, table, shaped(*potential.shape)], [VME...  1.85 us
    unnamed x14, local copies, waits for them, and re-layouts  0.99 us
  transfers between devices with their start and end apart: 11, of which 7 were waited for; matrix products, arithmetic and copies ran while one was open for 0% of the time, Pallas kernels for 18%

profile of v5, /device:TPU:0, one launch (start us, length us, event | category | flops | bytes accessed | tf_op | source)
XLA Modules:
  0.0 45.4 jit_solution(1268197751229763811)
XLA Ops:
  0.7 2.5 %shard_map.64.message_ref = f32[136,128]{1,0:T(8,128)} custom-call(s32[1,2]{1,0:T(1,128)} %offsets_ref.1, s32[1]{0:T(128)S(6)} %copy.83.thickness_hbm, f32[1,128]{1,0:T(1,128)} %bitcast.17, f32[1,512,512]{2,1,0:T(8,128)} %potential_ref.1), custom_call_target="tpu_custom_call" | custom-call | bytes 1024 | tf_op jit(solution)/shard_map/pallas_call | solution.py:349
  3.2 3.0 %collective-permute-start = (f32[136,128]{1,0:T(8,128)}, f32[136,128]{1,0:T(8,128)S(1)}, u32[]{:S(2)}, u32[]{:S(2)}) collective-permute-start(f32[136,128]{1,0:T(8,128)} %shard_map.64.message_ref), channel_id=1, source_target_pairs={{0,2},{1,3},{2,0},{3,1},{4,6},{5,7},{6,4},{7,5},{8,10},{9,11},{10,... | collective-permute-start | bytes 208904 | tf_op jit(solution)/shard_map/ppermute | solution.py:347
  6.2 2.6 %collective-permute-start.3 = (f32[136,128]{1,0:T(8,128)}, f32[136,128]{1,0:T(8,128)S(1)}, u32[]{:S(2)}, u32[]{:S(2)}) collective-permute-start(f32[136,128]{1,0:T(8,128)} %shard_map.64.message_ref), channel_id=1, source_target_pairs={{0,8},{1,9},{2,10},{3,11},{4,12},{5,13},{6,14},{7,15},{8,0},{9,1},... | collective-permute-start | bytes 208904 | tf_op jit(solution)/shard_map/ppermute | solution.py:347
  8.8 1.3 %collective-permute-start.5 = (f32[136,128]{1,0:T(8,128)}, f32[136,128]{1,0:T(8,128)S(1)}, u32[]{:S(2)}, u32[]{:S(2)}) collective-permute-start(f32[136,128]{1,0:T(8,128)} %shard_map.64.message_ref), channel_id=1, source_target_pairs={{0,12},{1,13},{2,14},{3,15},{4,8},{5,9},{6,10},{7,11},{8,4},{9,5},... | collective-permute-start | bytes 208904 | tf_op jit(solution)/shard_map/ppermute | solution.py:347
  10.1 0.9 %copy-done.1 = f32[136,128]{1,0:T(8,128)S(1)} copy-done((f32[136,128]{1,0:T(8,128)S(1)}, f32[136,128]{1,0:T(8,128)}, u32[]{:S(2)}) %copy-start.1) | copy-done | bytes 69656
  11.1 1.9 %shard_map.65 = (bf16[6,2,256,256]{3,2,1,0:T(8,128)(2,1)S(1)}, bf16[6,2,256,256]{3,2,1,0:T(8,128)(2,1)S(1)}, f32[1,512,512]{2,1,0:T(8,128)}) custom-call(f32[136,128]{1,0:T(8,128)S(1)} %copy-done.1), custom_call_target="tpu_custom_call" | custom-call | bytes 1024 | tf_op jit(solution)/shard_map/pallas_call | solution.py:364
  13.0 0.3 collective-permute-start.1
  13.6 0.5 %collective-permute-start.4 = (f32[136,128]{1,0:T(8,128)S(1)}, f32[136,128]{1,0:T(8,128)S(1)}, u32[]{:S(2)}, u32[]{:S(2)}) collective-permute-start(f32[136,128]{1,0:T(8,128)S(1)} %collective-permute-done.3), channel_id=1, source_target_pairs={{0,2},{1,3},{2,0},{3,1},{4,6},{5,7},{6,4},{7,5},{8,10},{9,11},{10,... | collective-permute-start | bytes 208904 | tf_op jit(solution)/shard_map/ppermute | solution.py:347
  14.0 1.2 %collective-permute-done.5 = f32[136,128]{1,0:T(8,128)S(1)} collective-permute-done((f32[136,128]{1,0:T(8,128)}, f32[136,128]{1,0:T(8,128)S(1)}, u32[]{:S(2)}, u32[]{:S(2)}) %collective-permute-start.5) | collective-permute-done | bytes 69664 | tf_op jit(solution)/shard_map/ppermute | solution.py:347
  15.2 0.5 %collective-permute-start.6 = (f32[136,128]{1,0:T(8,128)S(1)}, f32[136,128]{1,0:T(8,128)S(1)}, u32[]{:S(2)}, u32[]{:S(2)}) collective-permute-start(f32[136,128]{1,0:T(8,128)S(1)} %collective-permute-done.5), channel_id=1, source_target_pairs={{0,2},{1,3},{2,0},{3,1},{4,6},{5,7},{6,4},{7,5},{8,10},{9,11},{10,... | collective-permute-start | bytes 208904 | tf_op jit(solution)/shard_map/ppermute | solution.py:347
  15.8 3.1 %shard_map.67 = (f32[6,128,256]{2,1,0:T(8,128)S(1)}, f32[3,6,128,256]{3,2,1,0:T(8,128)S(1)}, f32[128,128]{1,0:T(8,128)S(1)}, bf16[6,2,256,256]{3,2,1,0:T(8,128)(2,1)S(1)}, bf16[6,2,256,256]{3,2,1,0:T(8,128)(2,1)S(1)}) custom-call(f32[2,136,128]{2,1,0:T(8,128)S(1)} %shard_map.66.near_ref, ...), custom_call_target="tpu_custom_call", output_to_operand_aliasing={{3}: (2, {}), {4}: (3, {})} | custom-call | bytes 1024 | tf_op jit(solution)/shard_map/pallas_call | solution.py:384
  18.9 0.3 collective-permute-done.1.refs_0_
  19.1 0.4 collective-permute-done.6.refs_0_
  19.9 0.6 %collective-permute-done.7 = f32[2,136,128]{2,1,0:T(8,128)S(1)} collective-permute-done((f32[2,136,128]{2,1,0:T(8,128)S(1)}, f32[2,136,128]{2,1,0:T(8,128)S(1)}, u32[]{:S(2)}, u32[]{:S(2)}) %collective-permute-start.7) | collective-permute-done | bytes 139296 | tf_op jit(solution)/shard_map/ppermute | solution.py:347
  20.5 3.1 %shard_map.72 = (f32[6,128,256]{2,1,0:T(8,128)S(1)}, f32[3,6,128,256]{3,2,1,0:T(8,128)S(1)}, f32[128,128]{1,0:T(8,128)S(1)}, bf16[6,2,256,256]{3,2,1,0:T(8,128)(2,1)S(1)}, bf16[6,2,256,256]{3,2,1,0:T(8,128)(2,1)S(1)}) custom-call(f32[4,136,128]{2,1,0:T(8,128)S(1)} %pad_maximum_fusion.2, ...), custom_call_target="tpu_custom_call", output_to_operand_aliasing={{0}: (4, {}), {1}: (5, {}), {2}: (6, {}), {3}: (2, {}), {4}... | custom-call | bytes 1024 | tf_op jit(solution)/shard_map/pallas_call | solution.py:384
  23.9 5.7 %shard_map.75 = (f32[6,128,256]{2,1,0:T(8,128)S(1)}, f32[3,6,128,256]{3,2,1,0:T(8,128)S(1)}, f32[128,128]{1,0:T(8,128)S(1)}, bf16[6,2,256,256]{3,2,1,0:T(8,128)(2,1)S(1)}, bf16[6,2,256,256]{3,2,1,0:T(8,128)(2,1)S(1)}) custom-call(f32[8,136,128]{2,1,0:T(8,128)S(1)} %constant_dynamic-upd, ...), custom_call_target="tpu_custom_call", output_to_operand_aliasing={{0}: (4, {}), {1}: (5, {}), {2}: (6, {}), {3}: (2, {}), {4}... | custom-call | bytes 1024 | tf_op jit(solution)/shard_map/pallas_call | solution.py:384
  29.6 0.2 collective-permute-start.9
  29.9 1.1 %collective-permute-done.9.refs_1_ = f32[128,128]{1,0:T(8,128)S(1)} collective-permute-done((f32[128,128]{1,0:T(8,128)S(1)}, f32[128,128]{1,0:T(8,128)S(1)}, u32[]{:S(2)}, u32[]{:S(2)}) %collective-permute-start.9) | collective-permute-done | bytes 65568 | tf_op jit(solution)/shard_map/ppermute | solution.py:347
  31.0 5.7 %shard_map.76 = (f32[6,128,256]{2,1,0:T(8,128)S(1)}, f32[2,128,128]{2,1,0:T(8,128)S(1)}, bf16[6,2,256,256]{3,2,1,0:T(8,128)(2,1)S(1)}) custom-call(f32[8,136,128]{2,1,0:T(8,128)S(1)} %constant_dynamic-update-slice_fusion.near_ref, f32[8,136,128]{2,1,0:T(8,128)S(1)} %pad_maximum_fusion.far_ref, ...), custom_call_target="tpu_custom_call", output_to_operand_aliasing={{2}: (2, {}), {0}: (7, {})} | custom-call | bytes 1024 | tf_op jit(solution)/shard_map/pallas_call | solution.py:422
  36.6 3.1 %shard_map.77 = (f32[6,128,256]{2,1,0:T(8,128)S(1)}, f32[2,128,128]{2,1,0:T(8,128)S(1)}, bf16[6,2,256,256]{3,2,1,0:T(8,128)(2,1)S(1)}) custom-call(f32[8,136,128]{2,1,0:T(8,128)S(1)} %constant_dynamic-update-slice_fusion.near_ref, f32[8,136,128]{2,1,0:T(8,128)S(1)} %pad_maximum_fusion.far_ref, ...), custom_call_target="tpu_custom_call", output_to_operand_aliasing={{2}: (2, {}), {1}: (4, {}), {0}: (5, {})} | custom-call | bytes 1024 | tf_op jit(solution)/shard_map/pallas_call | solution.py:422
  39.7 3.2 %shard_map.78 = (f32[2,128,128]{2,1,0:T(8,128)S(1)}, bf16[6,2,256,256]{3,2,1,0:T(8,128)(2,1)S(1)}) custom-call(f32[8,136,128]{2,1,0:T(8,128)S(1)} %constant_dynamic-update-slice_fusion.near_ref, f32[8,136,128]{2,1,0:T(8,128)S(1)} %pad_maximum_fusion.far_ref, ...), custom_call_target="tpu_custom_call", output_to_operand_aliasing={{1}: (2, {}), {0}: (4, {})} | custom-call | bytes 1024 | tf_op jit(solution)/shard_map/pallas_call | solution.py:422
  43.0 0.2 collective-permute-start.10
  43.2 1.1 %collective-permute-done.10.theirs_ref = f32[128,128]{1,0:T(8,128)S(1)} collective-permute-done((f32[128,128]{1,0:T(8,128)S(1)}, f32[128,128]{1,0:T(8,128)S(1)}, u32[]{:S(2)}, u32[]{:S(2)}) %collective-permute-start.10) | collective-permute-done | bytes 65568 | tf_op jit(solution)/shard_map/ppermute | solution.py:347
  44.3 0.9 %shard_map.80 = f32[1,512,512]{2,1,0:T(8,128)} custom-call(s32[1,2]{1,0:T(1,128)S(1)} %copy-done.3, f32[128,128]{1,0:T(8,128)S(1)} %get-tuple-element.74.ours_ref, f32[128,128]{1,0:T(8,128)S(1)} %collective-permute-done.10.theirs_ref, f32[1,512,512]{2,1,0:T(8,128)} %get-tuple-element.76.zeros_ref), custom_call_target="tpu_custom_call", output_to_operand_aliasing={{}: (3, {})} | custom-call | bytes 1024 | tf_op jit(solution)/shard_map/pallas_call | solution.py:431
  (35 shorter events, 0.9 us)
Async XLA Ops:
  0.7 15.1 %copy-start = (bf16[2,12,128,128]{3,2,1,0:T(8,128)(2,1)S(1)}, bf16[2,12,128,128]{3,2,1,0:T(8,128)(2,1)}, u32[]{:S(2)}) copy-start(bf16[2,12,128,128]{3,2,1,0:T(8,128)(2,1)} %wave_ref.5) | copy-start | bytes 2359300
  3.2 9.8 %collective-permute-start = (f32[136,128]{1,0:T(8,128)}, f32[136,128]{1,0:T(8,128)S(1)}, u32[]{:S(2)}, u32[]{:S(2)}) collective-permute-start(f32[136,128]{1,0:T(8,128)} %shard_map.64.message_ref), channel_id=1, source_target_pairs={{0,2},{1,3},{2,0},{3,1},{4,6},{5,7},{6,4},{7,5},{8,10},{9,11},{10,... | collective-permute-start | bytes 208904 | tf_op jit(solution)/shard_map/ppermute | solution.py:347
  6.2 7.4 %collective-permute-start.3 = (f32[136,128]{1,0:T(8,128)}, f32[136,128]{1,0:T(8,128)S(1)}, u32[]{:S(2)}, u32[]{:S(2)}) collective-permute-start(f32[136,128]{1,0:T(8,128)} %shard_map.64.message_ref), channel_id=1, source_target_pairs={{0,8},{1,9},{2,10},{3,11},{4,12},{5,13},{6,14},{7,15},{8,0},{9,1},... | collective-permute-start | bytes 208904 | tf_op jit(solution)/shard_map/ppermute | solution.py:347
  8.8 6.4 %collective-permute-start.5 = (f32[136,128]{1,0:T(8,128)}, f32[136,128]{1,0:T(8,128)S(1)}, u32[]{:S(2)}, u32[]{:S(2)}) collective-permute-start(f32[136,128]{1,0:T(8,128)} %shard_map.64.message_ref), channel_id=1, source_target_pairs={{0,12},{1,13},{2,14},{3,15},{4,8},{5,9},{6,10},{7,11},{8,4},{9,5},... | collective-permute-start | bytes 208904 | tf_op jit(solution)/shard_map/ppermute | solution.py:347
  10.1 0.9 %copy-start.1 = (f32[136,128]{1,0:T(8,128)S(1)}, f32[136,128]{1,0:T(8,128)}, u32[]{:S(2)}) copy-start(f32[136,128]{1,0:T(8,128)} %shard_map.64.message_ref) | copy-start | bytes 208900
  13.0 2.8 %collective-permute-start.2 = (f32[2,136,128]{2,1,0:T(8,128)S(1)}, f32[2,136,128]{2,1,0:T(8,128)S(1)}, u32[]{:S(2)}, u32[]{:S(2)}) collective-permute-start(f32[2,136,128]{2,1,0:T(8,128)S(1)} %shard_map.66.near_ref), channel_id=1, source_target_pairs={{0,1},{1,0},{2,3},{3,2},{4,5},{5,4},{6,7},{7,6},{8,9},{9,8},{10,11... | collective-permute-start | bytes 417800 | tf_op jit(solution)/shard_map/ppermute | solution.py:347
  13.0 6.1 %collective-permute-start.1 = (f32[2,136,128]{2,1,0:T(8,128)S(1)}, f32[2,136,128]{2,1,0:T(8,128)S(1)}, u32[]{:S(2)}, u32[]{:S(2)}) collective-permute-start(f32[2,136,128]{2,1,0:T(8,128)S(1)} %shard_map.66.near_ref), channel_id=1, source_target_pairs={{0,4},{1,5},{2,6},{3,7},{4,0},{5,1},{6,2},{7,3},{8,12},{9,13},{10,... | collective-permute-start | bytes 417800 | tf_op jit(solution)/shard_map/ppermute | solution.py:347
  13.6 5.6 %collective-permute-start.4 = (f32[136,128]{1,0:T(8,128)S(1)}, f32[136,128]{1,0:T(8,128)S(1)}, u32[]{:S(2)}, u32[]{:S(2)}) collective-permute-start(f32[136,128]{1,0:T(8,128)S(1)} %collective-permute-done.3), channel_id=1, source_target_pairs={{0,2},{1,3},{2,0},{3,1},{4,6},{5,7},{6,4},{7,5},{8,10},{9,11},{10,... | collective-permute-start | bytes 208904 | tf_op jit(solution)/shard_map/ppermute | solution.py:347
  15.2 4.3 %collective-permute-start.6 = (f32[136,128]{1,0:T(8,128)S(1)}, f32[136,128]{1,0:T(8,128)S(1)}, u32[]{:S(2)}, u32[]{:S(2)}) collective-permute-start(f32[136,128]{1,0:T(8,128)S(1)} %collective-permute-done.5), channel_id=1, source_target_pairs={{0,2},{1,3},{2,0},{3,1},{4,6},{5,7},{6,4},{7,5},{8,10},{9,11},{10,... | collective-permute-start | bytes 208904 | tf_op jit(solution)/shard_map/ppermute | solution.py:347
  19.1 1.4 %collective-permute-start.7 = (f32[2,136,128]{2,1,0:T(8,128)S(1)}, f32[2,136,128]{2,1,0:T(8,128)S(1)}, u32[]{:S(2)}, u32[]{:S(2)}) collective-permute-start(f32[2,136,128]{2,1,0:T(8,128)S(1)} %shard_map.68), channel_id=1, source_target_pairs={{0,1},{1,0},{2,3},{3,2},{4,5},{5,4},{6,7},{7,6},{8,9},{9,8},{10,11... | collective-permute-start | bytes 417800 | tf_op jit(solution)/shard_map/ppermute | solution.py:347
  19.6 4.1 %collective-permute-start.8 = (f32[4,136,128]{2,1,0:T(8,128)S(1)}, f32[4,136,128]{2,1,0:T(8,128)S(1)}, u32[]{:S(2)}, u32[]{:S(2)}) collective-permute-start(f32[4,136,128]{2,1,0:T(8,128)S(1)} %pad_maximum_fusion.1), channel_id=1, source_target_pairs={{0,1},{1,0},{2,3},{3,2},{4,5},{5,4},{6,7},{7,6},{8,9},{9,8},{10,11... | collective-permute-start | bytes 835592 | tf_op jit(solution)/shard_map/ppermute | solution.py:347
  23.9 7.1 %copy-start.2 = (f32[1,128,128]{2,1,0:T(8,128)S(1)}, f32[1,128,128]{2,1,0:T(8,128)}, u32[]{:S(2)}) copy-start(f32[1,128,128]{2,1,0:T(8,128)} %refs_2_.1) | copy-start | bytes 196612
  29.6 1.3 %collective-permute-start.9 = (f32[128,128]{1,0:T(8,128)S(1)}, f32[128,128]{1,0:T(8,128)S(1)}, u32[]{:S(2)}, u32[]{:S(2)}) collective-permute-start(f32[128,128]{1,0:T(8,128)S(1)} %get-tuple-element.65.refs_0_), channel_id=1, source_target_pairs={{0,1},{1,0},{2,3},{3,2},{4,5},{5,4},{6,7},{7,6},{8,9},{9,8},{10,11... | collective-permute-start | bytes 196616 | tf_op jit(solution)/shard_map/ppermute | solution.py:347
  39.7 4.6 %copy-start.3 = (s32[1,2]{1,0:T(1,128)S(1)}, s32[1,2]{1,0:T(1,128)}, u32[]{:S(2)}) copy-start(s32[1,2]{1,0:T(1,128)} %offsets_ref.1) | copy-start | bytes 28
  43.0 1.3 %collective-permute-start.10 = (f32[128,128]{1,0:T(8,128)S(1)}, f32[128,128]{1,0:T(8,128)S(1)}, u32[]{:S(2)}, u32[]{:S(2)}) collective-permute-start(f32[128,128]{1,0:T(8,128)S(1)} %get-tuple-element.75), channel_id=1, source_target_pairs={{0,1},{1,0},{2,3},{3,2},{4,5},{5,4},{6,7},{7,6},{8,9},{9,8},{10,11... | collective-permute-start | bytes 196616 | tf_op jit(solution)/shard_map/ppermute | solution.py:347

commit v6 on v5

--- a/solution.py
+++ b/solution.py
@@ -409,7 +409,7 @@
     backward_table = tables[1]
     ours, waves = None, [waves]
     extra = (power, flipped(power, 1), measured)
-    spans = [(chunks - 2, chunks)] + [(k, k + 1) for k in reversed(range(chunks - 2))]
+    spans = [(chunks - 3, chunks)] + [(k, k + 1) for k in reversed(range(chunks - 3))]
     for low_end, high_end in spans:
         last = high_end == chunks
         ins = [blocks, others, backward_table, kept, *(extra if last else (ours,)), *waves]

time: 45.6 us -> 45.1 us (0.989)
    pallas_call x3 -> x2, Pallas kernels: 12 us -> 11.5 us  [local(): call(functools.partial(backward_kernel, low_end, high_end, last), [VMEM]...]
where the time goes in v6:
time: 45.1 us; the launch traced here: 44.9 us
  Pallas kernels  28.9 us (64%)
  starting transfers between devices  8.97 us (20%)
  waiting for transfers between devices  4.88 us (11%)
  between operations  1.06 us (2%)
  local copies, waits for them, and re-layouts  1 us (2%)
    pallas_call x5, Pallas kernels, forward(): call(functools.partial(forward_kernel, condition, span, last), [VMEM] * l...  12.1 us
    pallas_call x2, Pallas kernels, local(): call(functools.partial(backward_kernel, low_end, high_end, last), [VMEM]...  11.5 us
    ppermute x11, starting transfers between devices, flipped(): return lax.ppermute(block, 'slc', [(i, i ^ bit) for i in range(length)])  8.97 us
    ppermute x11, waiting for transfers between devices, flipped(): return lax.ppermute(block, 'slc', [(i, i ^ bit) for i in range(length)])  4.88 us
    pallas_call x1, Pallas kernels, local(): call(extract_kernel, [HBM, HBM, HBM, HBM], [shaped(size + 8, size)], None...  2.49 us
    pallas_call x1, Pallas kernels, local(): call(table_kernel, [VMEM], [table, table, shaped(*potential.shape)], [VME...  1.85 us
    unnamed x14, local copies, waits for them, and re-layouts  0.99 us
  transfers between devices with their start and end apart: 11, of which 7 were waited for; matrix products, arithmetic and copies ran while one was open for 0% of the time, Pallas kernels for 18%

profile of v6, /device:TPU:0, one launch (start us, length us, event | category | flops | bytes accessed | tf_op | source)
XLA Modules:
  0.0 44.9 jit_solution(16226086911829760187)
XLA Ops:
  0.7 2.5 %shard_map.64.message_ref = f32[136,128]{1,0:T(8,128)} custom-call(s32[1,2]{1,0:T(1,128)} %offsets_ref.1, s32[1]{0:T(128)S(6)} %copy.77.thickness_hbm, f32[1,128]{1,0:T(1,128)} %bitcast.17, f32[1,512,512]{2,1,0:T(8,128)} %potential_ref.1), custom_call_target="tpu_custom_call" | custom-call | bytes 1024 | tf_op jit(solution)/shard_map/pallas_call | solution.py:349
  3.2 3.0 %collective-permute-start = (f32[136,128]{1,0:T(8,128)}, f32[136,128]{1,0:T(8,128)S(1)}, u32[]{:S(2)}, u32[]{:S(2)}) collective-permute-start(f32[136,128]{1,0:T(8,128)} %shard_map.64.message_ref), channel_id=1, source_target_pairs={{0,2},{1,3},{2,0},{3,1},{4,6},{5,7},{6,4},{7,5},{8,10},{9,11},{10,... | collective-permute-start | bytes 208904 | tf_op jit(solution)/shard_map/ppermute | solution.py:347
  6.2 2.6 %collective-permute-start.3 = (f32[136,128]{1,0:T(8,128)}, f32[136,128]{1,0:T(8,128)S(1)}, u32[]{:S(2)}, u32[]{:S(2)}) collective-permute-start(f32[136,128]{1,0:T(8,128)} %shard_map.64.message_ref), channel_id=1, source_target_pairs={{0,8},{1,9},{2,10},{3,11},{4,12},{5,13},{6,14},{7,15},{8,0},{9,1},... | collective-permute-start | bytes 208904 | tf_op jit(solution)/shard_map/ppermute | solution.py:347
  8.8 1.3 %collective-permute-start.5 = (f32[136,128]{1,0:T(8,128)}, f32[136,128]{1,0:T(8,128)S(1)}, u32[]{:S(2)}, u32[]{:S(2)}) collective-permute-start(f32[136,128]{1,0:T(8,128)} %shard_map.64.message_ref), channel_id=1, source_target_pairs={{0,12},{1,13},{2,14},{3,15},{4,8},{5,9},{6,10},{7,11},{8,4},{9,5},... | collective-permute-start | bytes 208904 | tf_op jit(solution)/shard_map/ppermute | solution.py:347
  10.1 0.9 %copy-done.1 = f32[136,128]{1,0:T(8,128)S(1)} copy-done((f32[136,128]{1,0:T(8,128)S(1)}, f32[136,128]{1,0:T(8,128)}, u32[]{:S(2)}) %copy-start.1) | copy-done | bytes 69656
  11.0 1.9 %shard_map.65 = (bf16[6,2,256,256]{3,2,1,0:T(8,128)(2,1)S(1)}, bf16[6,2,256,256]{3,2,1,0:T(8,128)(2,1)S(1)}, f32[1,512,512]{2,1,0:T(8,128)}) custom-call(f32[136,128]{1,0:T(8,128)S(1)} %copy-done.1), custom_call_target="tpu_custom_call" | custom-call | bytes 1024 | tf_op jit(solution)/shard_map/pallas_call | solution.py:364
  13.0 0.3 collective-permute-start.1
  13.4 0.2 collective-permute-done.3
  13.6 0.5 %collective-permute-start.4 = (f32[136,128]{1,0:T(8,128)S(1)}, f32[136,128]{1,0:T(8,128)S(1)}, u32[]{:S(2)}, u32[]{:S(2)}) collective-permute-start(f32[136,128]{1,0:T(8,128)S(1)} %collective-permute-done.3), channel_id=1, source_target_pairs={{0,2},{1,3},{2,0},{3,1},{4,6},{5,7},{6,4},{7,5},{8,10},{9,11},{10,... | collective-permute-start | bytes 208904 | tf_op jit(solution)/shard_map/ppermute | solution.py:347
  14.0 1.2 %collective-permute-done.5 = f32[136,128]{1,0:T(8,128)S(1)} collective-permute-done((f32[136,128]{1,0:T(8,128)}, f32[136,128]{1,0:T(8,128)S(1)}, u32[]{:S(2)}, u32[]{:S(2)}) %collective-permute-start.5) | collective-permute-done | bytes 69664 | tf_op jit(solution)/shard_map/ppermute | solution.py:347
  15.2 0.5 %collective-permute-start.6 = (f32[136,128]{1,0:T(8,128)S(1)}, f32[136,128]{1,0:T(8,128)S(1)}, u32[]{:S(2)}, u32[]{:S(2)}) collective-permute-start(f32[136,128]{1,0:T(8,128)S(1)} %collective-permute-done.5), channel_id=1, source_target_pairs={{0,2},{1,3},{2,0},{3,1},{4,6},{5,7},{6,4},{7,5},{8,10},{9,11},{10,... | collective-permute-start | bytes 208904 | tf_op jit(solution)/shard_map/ppermute | solution.py:347
  15.8 3.1 %shard_map.67 = (f32[6,128,256]{2,1,0:T(8,128)S(1)}, f32[3,6,128,256]{3,2,1,0:T(8,128)S(1)}, f32[128,128]{1,0:T(8,128)S(1)}, bf16[6,2,256,256]{3,2,1,0:T(8,128)(2,1)S(1)}, bf16[6,2,256,256]{3,2,1,0:T(8,128)(2,1)S(1)}) custom-call(f32[2,136,128]{2,1,0:T(8,128)S(1)} %shard_map.66.near_ref, ...), custom_call_target="tpu_custom_call", output_to_operand_aliasing={{3}: (2, {}), {4}: (3, {})} | custom-call | bytes 1024 | tf_op jit(solution)/shard_map/pallas_call | solution.py:384
  18.8 0.3 collective-permute-done.1.refs_0_
  19.1 0.4 collective-permute-done.6.refs_0_
  19.9 0.6 %collective-permute-done.7 = f32[2,136,128]{2,1,0:T(8,128)S(1)} collective-permute-done((f32[2,136,128]{2,1,0:T(8,128)S(1)}, f32[2,136,128]{2,1,0:T(8,128)S(1)}, u32[]{:S(2)}, u32[]{:S(2)}) %collective-permute-start.7) | collective-permute-done | bytes 139296 | tf_op jit(solution)/shard_map/ppermute | solution.py:347
  20.5 3.1 %shard_map.72 = (f32[6,128,256]{2,1,0:T(8,128)S(1)}, f32[3,6,128,256]{3,2,1,0:T(8,128)S(1)}, f32[128,128]{1,0:T(8,128)S(1)}, bf16[6,2,256,256]{3,2,1,0:T(8,128)(2,1)S(1)}, bf16[6,2,256,256]{3,2,1,0:T(8,128)(2,1)S(1)}) custom-call(f32[4,136,128]{2,1,0:T(8,128)S(1)} %pad_maximum_fusion.2, ...), custom_call_target="tpu_custom_call", output_to_operand_aliasing={{0}: (4, {}), {1}: (5, {}), {2}: (6, {}), {3}: (2, {}), {4}... | custom-call | bytes 1024 | tf_op jit(solution)/shard_map/pallas_call | solution.py:384
  23.9 5.7 %shard_map.75 = (f32[6,128,256]{2,1,0:T(8,128)S(1)}, f32[3,6,128,256]{3,2,1,0:T(8,128)S(1)}, f32[128,128]{1,0:T(8,128)S(1)}, bf16[6,2,256,256]{3,2,1,0:T(8,128)(2,1)S(1)}, bf16[6,2,256,256]{3,2,1,0:T(8,128)(2,1)S(1)}) custom-call(f32[8,136,128]{2,1,0:T(8,128)S(1)} %constant_dynamic-upd, ...), custom_call_target="tpu_custom_call", output_to_operand_aliasing={{0}: (4, {}), {1}: (5, {}), {2}: (6, {}), {3}: (2, {}), {4}... | custom-call | bytes 1024 | tf_op jit(solution)/shard_map/pallas_call | solution.py:384
  29.6 0.2 collective-permute-start.9
  29.9 1.1 %collective-permute-done.9.refs_1_ = f32[128,128]{1,0:T(8,128)S(1)} collective-permute-done((f32[128,128]{1,0:T(8,128)S(1)}, f32[128,128]{1,0:T(8,128)S(1)}, u32[]{:S(2)}, u32[]{:S(2)}) %collective-permute-start.9) | collective-permute-done | bytes 65568 | tf_op jit(solution)/shard_map/ppermute | solution.py:347
  31.0 8.3 %shard_map.76 = (f32[6,128,256]{2,1,0:T(8,128)S(1)}, f32[2,128,128]{2,1,0:T(8,128)S(1)}, bf16[6,2,256,256]{3,2,1,0:T(8,128)(2,1)S(1)}) custom-call(f32[8,136,128]{2,1,0:T(8,128)S(1)} %constant_dynamic-update-slice_fusion.near_ref, f32[8,136,128]{2,1,0:T(8,128)S(1)} %pad_maximum_fusion.far_ref, ...), custom_call_target="tpu_custom_call", output_to_operand_aliasing={{2}: (2, {}), {0}: (7, {})} | custom-call | bytes 1024 | tf_op jit(solution)/shard_map/pallas_call | solution.py:422
  39.3 3.2 %shard_map.77 = (f32[2,128,128]{2,1,0:T(8,128)S(1)}, bf16[6,2,256,256]{3,2,1,0:T(8,128)(2,1)S(1)}) custom-call(f32[8,136,128]{2,1,0:T(8,128)S(1)} %constant_dynamic-update-slice_fusion.near_ref, f32[8,136,128]{2,1,0:T(8,128)S(1)} %pad_maximum_fusion.far_ref, ...), custom_call_target="tpu_custom_call", output_to_operand_aliasing={{1}: (2, {}), {0}: (4, {})} | custom-call | bytes 1024 | tf_op jit(solution)/shard_map/pallas_call | solution.py:422
  42.5 0.2 collective-permute-start.10
  42.7 1.1 %collective-permute-done.10.theirs_ref = f32[128,128]{1,0:T(8,128)S(1)} collective-permute-done((f32[128,128]{1,0:T(8,128)S(1)}, f32[128,128]{1,0:T(8,128)S(1)}, u32[]{:S(2)}, u32[]{:S(2)}) %collective-permute-start.10) | collective-permute-done | bytes 65568 | tf_op jit(solution)/shard_map/ppermute | solution.py:347
  43.8 0.9 %shard_map.79 = f32[1,512,512]{2,1,0:T(8,128)} custom-call(s32[1,2]{1,0:T(1,128)S(1)} %copy-done.3, f32[128,128]{1,0:T(8,128)S(1)} %get-tuple-element.68.ours_ref, f32[128,128]{1,0:T(8,128)S(1)} %collective-permute-done.10.theirs_ref, f32[1,512,512]{2,1,0:T(8,128)} %get-tuple-element.70.zeros_ref), custom_call_target="tpu_custom_call", output_to_operand_aliasing={{}: (3, {})} | custom-call | bytes 1024 | tf_op jit(solution)/shard_map/pallas_call | solution.py:431
  (34 shorter events, 0.7 us)
Async XLA Ops:
  0.7 15.1 %copy-start = (bf16[2,12,128,128]{3,2,1,0:T(8,128)(2,1)S(1)}, bf16[2,12,128,128]{3,2,1,0:T(8,128)(2,1)}, u32[]{:S(2)}) copy-start(bf16[2,12,128,128]{3,2,1,0:T(8,128)(2,1)} %wave_ref.5) | copy-start | bytes 2359300
  3.2 9.8 %collective-permute-start = (f32[136,128]{1,0:T(8,128)}, f32[136,128]{1,0:T(8,128)S(1)}, u32[]{:S(2)}, u32[]{:S(2)}) collective-permute-start(f32[136,128]{1,0:T(8,128)} %shard_map.64.message_ref), channel_id=1, source_target_pairs={{0,2},{1,3},{2,0},{3,1},{4,6},{5,7},{6,4},{7,5},{8,10},{9,11},{10,... | collective-permute-start | bytes 208904 | tf_op jit(solution)/shard_map/ppermute | solution.py:347
  6.2 7.4 %collective-permute-start.3 = (f32[136,128]{1,0:T(8,128)}, f32[136,128]{1,0:T(8,128)S(1)}, u32[]{:S(2)}, u32[]{:S(2)}) collective-permute-start(f32[136,128]{1,0:T(8,128)} %shard_map.64.message_ref), channel_id=1, source_target_pairs={{0,8},{1,9},{2,10},{3,11},{4,12},{5,13},{6,14},{7,15},{8,0},{9,1},... | collective-permute-start | bytes 208904 | tf_op jit(solution)/shard_map/ppermute | solution.py:347
  8.8 6.4 %collective-permute-start.5 = (f32[136,128]{1,0:T(8,128)}, f32[136,128]{1,0:T(8,128)S(1)}, u32[]{:S(2)}, u32[]{:S(2)}) collective-permute-start(f32[136,128]{1,0:T(8,128)} %shard_map.64.message_ref), channel_id=1, source_target_pairs={{0,12},{1,13},{2,14},{3,15},{4,8},{5,9},{6,10},{7,11},{8,4},{9,5},... | collective-permute-start | bytes 208904 | tf_op jit(solution)/shard_map/ppermute | solution.py:347
  10.1 0.9 %copy-start.1 = (f32[136,128]{1,0:T(8,128)S(1)}, f32[136,128]{1,0:T(8,128)}, u32[]{:S(2)}) copy-start(f32[136,128]{1,0:T(8,128)} %shard_map.64.message_ref) | copy-start | bytes 208900
  12.9 2.8 %collective-permute-start.2 = (f32[2,136,128]{2,1,0:T(8,128)S(1)}, f32[2,136,128]{2,1,0:T(8,128)S(1)}, u32[]{:S(2)}, u32[]{:S(2)}) collective-permute-start(f32[2,136,128]{2,1,0:T(8,128)S(1)} %shard_map.66.near_ref), channel_id=1, source_target_pairs={{0,1},{1,0},{2,3},{3,2},{4,5},{5,4},{6,7},{7,6},{8,9},{9,8},{10,11... | collective-permute-start | bytes 417800 | tf_op jit(solution)/shard_map/ppermute | solution.py:347
  13.0 6.1 %collective-permute-start.1 = (f32[2,136,128]{2,1,0:T(8,128)S(1)}, f32[2,136,128]{2,1,0:T(8,128)S(1)}, u32[]{:S(2)}, u32[]{:S(2)}) collective-permute-start(f32[2,136,128]{2,1,0:T(8,128)S(1)} %shard_map.66.near_ref), channel_id=1, source_target_pairs={{0,4},{1,5},{2,6},{3,7},{4,0},{5,1},{6,2},{7,3},{8,12},{9,13},{10,... | collective-permute-start | bytes 417800 | tf_op jit(solution)/shard_map/ppermute | solution.py:347
  13.6 5.6 %collective-permute-start.4 = (f32[136,128]{1,0:T(8,128)S(1)}, f32[136,128]{1,0:T(8,128)S(1)}, u32[]{:S(2)}, u32[]{:S(2)}) collective-permute-start(f32[136,128]{1,0:T(8,128)S(1)} %collective-permute-done.3), channel_id=1, source_target_pairs={{0,2},{1,3},{2,0},{3,1},{4,6},{5,7},{6,4},{7,5},{8,10},{9,11},{10,... | collective-permute-start | bytes 208904 | tf_op jit(solution)/shard_map/ppermute | solution.py:347
  15.2 4.3 %collective-permute-start.6 = (f32[136,128]{1,0:T(8,128)S(1)}, f32[136,128]{1,0:T(8,128)S(1)}, u32[]{:S(2)}, u32[]{:S(2)}) collective-permute-start(f32[136,128]{1,0:T(8,128)S(1)} %collective-permute-done.5), channel_id=1, source_target_pairs={{0,2},{1,3},{2,0},{3,1},{4,6},{5,7},{6,4},{7,5},{8,10},{9,11},{10,... | collective-permute-start | bytes 208904 | tf_op jit(solution)/shard_map/ppermute | solution.py:347
  19.1 1.4 %collective-permute-start.7 = (f32[2,136,128]{2,1,0:T(8,128)S(1)}, f32[2,136,128]{2,1,0:T(8,128)S(1)}, u32[]{:S(2)}, u32[]{:S(2)}) collective-permute-start(f32[2,136,128]{2,1,0:T(8,128)S(1)} %shard_map.68), channel_id=1, source_target_pairs={{0,1},{1,0},{2,3},{3,2},{4,5},{5,4},{6,7},{7,6},{8,9},{9,8},{10,11... | collective-permute-start | bytes 417800 | tf_op jit(solution)/shard_map/ppermute | solution.py:347
  19.5 4.1 %collective-permute-start.8 = (f32[4,136,128]{2,1,0:T(8,128)S(1)}, f32[4,136,128]{2,1,0:T(8,128)S(1)}, u32[]{:S(2)}, u32[]{:S(2)}) collective-permute-start(f32[4,136,128]{2,1,0:T(8,128)S(1)} %pad_maximum_fusion.1), channel_id=1, source_target_pairs={{0,1},{1,0},{2,3},{3,2},{4,5},{5,4},{6,7},{7,6},{8,9},{9,8},{10,11... | collective-permute-start | bytes 835592 | tf_op jit(solution)/shard_map/ppermute | solution.py:347
  23.9 7.1 %copy-start.2 = (f32[1,128,128]{2,1,0:T(8,128)S(1)}, f32[1,128,128]{2,1,0:T(8,128)}, u32[]{:S(2)}) copy-start(f32[1,128,128]{2,1,0:T(8,128)} %refs_2_.1) | copy-start | bytes 196612
  29.6 1.3 %collective-permute-start.9 = (f32[128,128]{1,0:T(8,128)S(1)}, f32[128,128]{1,0:T(8,128)S(1)}, u32[]{:S(2)}, u32[]{:S(2)}) collective-permute-start(f32[128,128]{1,0:T(8,128)S(1)} %get-tuple-element.62.refs_0_), channel_id=1, source_target_pairs={{0,1},{1,0},{2,3},{3,2},{4,5},{5,4},{6,7},{7,6},{8,9},{9,8},{10,11... | collective-permute-start | bytes 196616 | tf_op jit(solution)/shard_map/ppermute | solution.py:347
  39.2 4.6 %copy-start.3 = (s32[1,2]{1,0:T(1,128)S(1)}, s32[1,2]{1,0:T(1,128)}, u32[]{:S(2)}) copy-start(s32[1,2]{1,0:T(1,128)} %offsets_ref.1) | copy-start | bytes 28
  42.5 1.3 %collective-permute-start.10 = (f32[128,128]{1,0:T(8,128)S(1)}, f32[128,128]{1,0:T(8,128)S(1)}, u32[]{:S(2)}, u32[]{:S(2)}) collective-permute-start(f32[128,128]{1,0:T(8,128)S(1)} %get-tuple-element.69), channel_id=1, source_target_pairs={{0,1},{1,0},{2,3},{3,2},{4,5},{5,4},{6,7},{7,6},{8,9},{9,8},{10,11... | collective-permute-start | bytes 196616 | tf_op jit(solution)/shard_map/ppermute | solution.py:347

commit v7 on v6

--- a/solution.py
+++ b/solution.py
@@ -401,7 +401,8 @@
     state = forward(lambda layer: layer <= 1, (1, 2), *early, *state)
     blocks = jnp.concatenate([early[0], late])
     others = jnp.concatenate([early[1], after(late_far, state[1])])
-    state = forward(lambda layer: layer > 1, (0, 2), blocks, others, *state)
+    for span in ((0, 1), (1, 2)):
+        state = forward(lambda layer: layer > 1, span, blocks, others, *state)
     for start in range(2, chunks, 2):
         span = (start, min(start + 2, chunks))
         state = forward(lambda layer: layer >= 0, span, blocks, others, *state)

time: 45.1 us -> 45.1 us (level)
    pallas_call x5 -> x6, Pallas kernels: 12.1 us -> 12.2 us  [forward(): call(functools.partial(forward_kernel, condition, span, last), [VMEM] * l...]
where the time goes in v7:
time: 45.1 us; the launch traced here: 44.9 us
  Pallas kernels  28.9 us (64%)
  starting transfers between devices  8.97 us (20%)
  waiting for transfers between devices  4.88 us (11%)
  between operations  1.07 us (2%)
  local copies, waits for them, and re-layouts  1 us (2%)
    pallas_call x6, Pallas kernels, forward(): call(functools.partial(forward_kernel, condition, span, last), [VMEM] * l...  12.2 us
    pallas_call x2, Pallas kernels, local(): call(functools.partial(backward_kernel, low_end, high_end, last), [VMEM]...  11.5 us
    ppermute x11, starting transfers between devices, flipped(): return lax.ppermute(block, 'slc', [(i, i ^ bit) for i in range(length)])  8.97 us
    ppermute x11, waiting for transfers between devices, flipped(): return lax.ppermute(block, 'slc', [(i, i ^ bit) for i in range(length)])  4.88 us
    pallas_call x1, Pallas kernels, local(): call(extract_kernel, [HBM, HBM, HBM, HBM], [shaped(size + 8, size)], None...  2.5 us
    pallas_call x1, Pallas kernels, local(): call(table_kernel, [VMEM], [table, table, shaped(*potential.shape)], [VME...  1.85 us
    unnamed x14, local copies, waits for them, and re-layouts  0.99 us
  transfers between devices with their start and end apart: 11, of which 7 were waited for; matrix products, arithmetic and copies ran while one was open for 0% of the time, Pallas kernels for 18%

profile of v7, /device:TPU:0, one launch (start us, length us, event | category | flops | bytes accessed | tf_op | source)
XLA Modules:
  0.0 44.9 jit_solution(6757830079064524600)
XLA Ops:
  0.7 2.5 %shard_map.64.message_ref = f32[136,128]{1,0:T(8,128)} custom-call(s32[1,2]{1,0:T(1,128)} %offsets_ref.1, s32[1]{0:T(128)S(6)} %copy.87.thickness_hbm, f32[1,128]{1,0:T(1,128)} %bitcast.17, f32[1,512,512]{2,1,0:T(8,128)} %potential_ref.1), custom_call_target="tpu_custom_call" | custom-call | bytes 1024 | tf_op jit(solution)/shard_map/pallas_call | solution.py:349
  3.2 3.0 %collective-permute-start = (f32[136,128]{1,0:T(8,128)}, f32[136,128]{1,0:T(8,128)S(1)}, u32[]{:S(2)}, u32[]{:S(2)}) collective-permute-start(f32[136,128]{1,0:T(8,128)} %shard_map.64.message_ref), channel_id=1, source_target_pairs={{0,2},{1,3},{2,0},{3,1},{4,6},{5,7},{6,4},{7,5},{8,10},{9,11},{10,... | collective-permute-start | bytes 208904 | tf_op jit(solution)/shard_map/ppermute | solution.py:347
  6.2 2.6 %collective-permute-start.3 = (f32[136,128]{1,0:T(8,128)}, f32[136,128]{1,0:T(8,128)S(1)}, u32[]{:S(2)}, u32[]{:S(2)}) collective-permute-start(f32[136,128]{1,0:T(8,128)} %shard_map.64.message_ref), channel_id=1, source_target_pairs={{0,8},{1,9},{2,10},{3,11},{4,12},{5,13},{6,14},{7,15},{8,0},{9,1},... | collective-permute-start | bytes 208904 | tf_op jit(solution)/shard_map/ppermute | solution.py:347
  8.8 1.3 %collective-permute-start.5 = (f32[136,128]{1,0:T(8,128)}, f32[136,128]{1,0:T(8,128)S(1)}, u32[]{:S(2)}, u32[]{:S(2)}) collective-permute-start(f32[136,128]{1,0:T(8,128)} %shard_map.64.message_ref), channel_id=1, source_target_pairs={{0,12},{1,13},{2,14},{3,15},{4,8},{5,9},{6,10},{7,11},{8,4},{9,5},... | collective-permute-start | bytes 208904 | tf_op jit(solution)/shard_map/ppermute | solution.py:347
  10.1 0.9 %copy-done.1 = f32[136,128]{1,0:T(8,128)S(1)} copy-done((f32[136,128]{1,0:T(8,128)S(1)}, f32[136,128]{1,0:T(8,128)}, u32[]{:S(2)}) %copy-start.1) | copy-done | bytes 69656
  11.1 1.9 %shard_map.65 = (bf16[6,2,256,256]{3,2,1,0:T(8,128)(2,1)S(1)}, bf16[6,2,256,256]{3,2,1,0:T(8,128)(2,1)S(1)}, f32[1,512,512]{2,1,0:T(8,128)}) custom-call(f32[136,128]{1,0:T(8,128)S(1)} %copy-done.1), custom_call_target="tpu_custom_call" | custom-call | bytes 1024 | tf_op jit(solution)/shard_map/pallas_call | solution.py:364
  13.0 0.3 collective-permute-start.1
  13.4 0.2 collective-permute-done.3
  13.6 0.5 %collective-permute-start.4 = (f32[136,128]{1,0:T(8,128)S(1)}, f32[136,128]{1,0:T(8,128)S(1)}, u32[]{:S(2)}, u32[]{:S(2)}) collective-permute-start(f32[136,128]{1,0:T(8,128)S(1)} %collective-permute-done.3), channel_id=1, source_target_pairs={{0,2},{1,3},{2,0},{3,1},{4,6},{5,7},{6,4},{7,5},{8,10},{9,11},{10,... | collective-permute-start | bytes 208904 | tf_op jit(solution)/shard_map/ppermute | solution.py:347
  14.0 1.2 %collective-permute-done.5 = f32[136,128]{1,0:T(8,128)S(1)} collective-permute-done((f32[136,128]{1,0:T(8,128)}, f32[136,128]{1,0:T(8,128)S(1)}, u32[]{:S(2)}, u32[]{:S(2)}) %collective-permute-start.5) | collective-permute-done | bytes 69664 | tf_op jit(solution)/shard_map/ppermute | solution.py:347
  15.2 0.5 %collective-permute-start.6 = (f32[136,128]{1,0:T(8,128)S(1)}, f32[136,128]{1,0:T(8,128)S(1)}, u32[]{:S(2)}, u32[]{:S(2)}) collective-permute-start(f32[136,128]{1,0:T(8,128)S(1)} %collective-permute-done.5), channel_id=1, source_target_pairs={{0,2},{1,3},{2,0},{3,1},{4,6},{5,7},{6,4},{7,5},{8,10},{9,11},{10,... | collective-permute-start | bytes 208904 | tf_op jit(solution)/shard_map/ppermute | solution.py:347
  15.8 3.1 %shard_map.67 = (f32[6,128,256]{2,1,0:T(8,128)S(1)}, f32[3,6,128,256]{3,2,1,0:T(8,128)S(1)}, f32[128,128]{1,0:T(8,128)S(1)}, bf16[6,2,256,256]{3,2,1,0:T(8,128)(2,1)S(1)}, bf16[6,2,256,256]{3,2,1,0:T(8,128)(2,1)S(1)}) custom-call(f32[2,136,128]{2,1,0:T(8,128)S(1)} %shard_map.66.near_ref, ...), custom_call_target="tpu_custom_call", output_to_operand_aliasing={{3}: (2, {}), {4}: (3, {})} | custom-call | bytes 1024 | tf_op jit(solution)/shard_map/pallas_call | solution.py:384
  18.9 0.3 collective-permute-done.1.refs_0_
  19.1 0.4 collective-permute-done.6.refs_0_
  19.9 0.6 %collective-permute-done.7 = f32[2,136,128]{2,1,0:T(8,128)S(1)} collective-permute-done((f32[2,136,128]{2,1,0:T(8,128)S(1)}, f32[2,136,128]{2,1,0:T(8,128)S(1)}, u32[]{:S(2)}, u32[]{:S(2)}) %collective-permute-start.7) | collective-permute-done | bytes 139296 | tf_op jit(solution)/shard_map/ppermute | solution.py:347
  20.5 3.1 %shard_map.72 = (f32[6,128,256]{2,1,0:T(8,128)S(1)}, f32[3,6,128,256]{3,2,1,0:T(8,128)S(1)}, f32[128,128]{1,0:T(8,128)S(1)}, bf16[6,2,256,256]{3,2,1,0:T(8,128)(2,1)S(1)}, bf16[6,2,256,256]{3,2,1,0:T(8,128)(2,1)S(1)}) custom-call(f32[4,136,128]{2,1,0:T(8,128)S(1)} %pad_maximum_fusion.2, ...), custom_call_target="tpu_custom_call", output_to_operand_aliasing={{0}: (4, {}), {1}: (5, {}), {2}: (6, {}), {3}: (2, {}), {4}... | custom-call | bytes 1024 | tf_op jit(solution)/shard_map/pallas_call | solution.py:384
  24.0 5.7 %shard_map.76 = (f32[6,128,256]{2,1,0:T(8,128)S(1)}, f32[3,6,128,256]{3,2,1,0:T(8,128)S(1)}, f32[128,128]{1,0:T(8,128)S(1)}, bf16[6,2,256,256]{3,2,1,0:T(8,128)(2,1)S(1)}, bf16[6,2,256,256]{3,2,1,0:T(8,128)(2,1)S(1)}) custom-call(f32[8,136,128]{2,1,0:T(8,128)S(1)} %constant_dynamic-upd, ...), custom_call_target="tpu_custom_call", output_to_operand_aliasing={{0}: (4, {}), {1}: (5, {}), {2}: (6, {}), {3}: (2, {}), {4}... | custom-call | bytes 1024 | tf_op jit(solution)/shard_map/pallas_call | solution.py:384
  29.7 0.2 collective-permute-start.9
  29.9 1.1 %collective-permute-done.9.refs_1_ = f32[128,128]{1,0:T(8,128)S(1)} collective-permute-done((f32[128,128]{1,0:T(8,128)S(1)}, f32[128,128]{1,0:T(8,128)S(1)}, u32[]{:S(2)}, u32[]{:S(2)}) %collective-permute-start.9) | collective-permute-done | bytes 65568 | tf_op jit(solution)/shard_map/ppermute | solution.py:347
  31.0 8.3 %shard_map.77 = (f32[6,128,256]{2,1,0:T(8,128)S(1)}, f32[2,128,128]{2,1,0:T(8,128)S(1)}, bf16[6,2,256,256]{3,2,1,0:T(8,128)(2,1)S(1)}) custom-call(f32[8,136,128]{2,1,0:T(8,128)S(1)} %constant_dynamic-update-slice_fusion.near_ref, f32[8,136,128]{2,1,0:T(8,128)S(1)} %pad_maximum_fusion.far_ref, ...), custom_call_target="tpu_custom_call", output_to_operand_aliasing={{2}: (2, {}), {0}: (7, {})} | custom-call | bytes 1024 | tf_op jit(solution)/shard_map/pallas_call | solution.py:423
  39.3 3.2 %shard_map.78 = (f32[2,128,128]{2,1,0:T(8,128)S(1)}, bf16[6,2,256,256]{3,2,1,0:T(8,128)(2,1)S(1)}) custom-call(f32[8,136,128]{2,1,0:T(8,128)S(1)} %constant_dynamic-update-slice_fusion.near_ref, f32[8,136,128]{2,1,0:T(8,128)S(1)} %pad_maximum_fusion.far_ref, ...), custom_call_target="tpu_custom_call", output_to_operand_aliasing={{1}: (2, {}), {0}: (4, {})} | custom-call | bytes 1024 | tf_op jit(solution)/shard_map/pallas_call | solution.py:423
  42.5 0.2 collective-permute-start.10
  42.8 1.1 %collective-permute-done.10.theirs_ref = f32[128,128]{1,0:T(8,128)S(1)} collective-permute-done((f32[128,128]{1,0:T(8,128)S(1)}, f32[128,128]{1,0:T(8,128)S(1)}, u32[]{:S(2)}, u32[]{:S(2)}) %collective-permute-start.10) | collective-permute-done | bytes 65568 | tf_op jit(solution)/shard_map/ppermute | solution.py:347
  43.9 0.9 %shard_map.80 = f32[1,512,512]{2,1,0:T(8,128)} custom-call(s32[1,2]{1,0:T(1,128)S(1)} %copy-done.3, f32[128,128]{1,0:T(8,128)S(1)} %get-tuple-element.78.ours_ref, f32[128,128]{1,0:T(8,128)S(1)} %collective-permute-done.10.theirs_ref, f32[1,512,512]{2,1,0:T(8,128)} %get-tuple-element.80.zeros_ref), custom_call_target="tpu_custom_call", output_to_operand_aliasing={{}: (3, {})} | custom-call | bytes 1024 | tf_op jit(solution)/shard_map/pallas_call | solution.py:432
  (35 shorter events, 0.7 us)
Async XLA Ops:
  0.7 15.1 %copy-start = (bf16[2,12,128,128]{3,2,1,0:T(8,128)(2,1)S(1)}, bf16[2,12,128,128]{3,2,1,0:T(8,128)(2,1)}, u32[]{:S(2)}) copy-start(bf16[2,12,128,128]{3,2,1,0:T(8,128)(2,1)} %wave_ref.5) | copy-start | bytes 2359300
  3.2 9.8 %collective-permute-start = (f32[136,128]{1,0:T(8,128)}, f32[136,128]{1,0:T(8,128)S(1)}, u32[]{:S(2)}, u32[]{:S(2)}) collective-permute-start(f32[136,128]{1,0:T(8,128)} %shard_map.64.message_ref), channel_id=1, source_target_pairs={{0,2},{1,3},{2,0},{3,1},{4,6},{5,7},{6,4},{7,5},{8,10},{9,11},{10,... | collective-permute-start | bytes 208904 | tf_op jit(solution)/shard_map/ppermute | solution.py:347
  6.2 7.4 %collective-permute-start.3 = (f32[136,128]{1,0:T(8,128)}, f32[136,128]{1,0:T(8,128)S(1)}, u32[]{:S(2)}, u32[]{:S(2)}) collective-permute-start(f32[136,128]{1,0:T(8,128)} %shard_map.64.message_ref), channel_id=1, source_target_pairs={{0,8},{1,9},{2,10},{3,11},{4,12},{5,13},{6,14},{7,15},{8,0},{9,1},... | collective-permute-start | bytes 208904 | tf_op jit(solution)/shard_map/ppermute | solution.py:347
  8.8 6.4 %collective-permute-start.5 = (f32[136,128]{1,0:T(8,128)}, f32[136,128]{1,0:T(8,128)S(1)}, u32[]{:S(2)}, u32[]{:S(2)}) collective-permute-start(f32[136,128]{1,0:T(8,128)} %shard_map.64.message_ref), channel_id=1, source_target_pairs={{0,12},{1,13},{2,14},{3,15},{4,8},{5,9},{6,10},{7,11},{8,4},{9,5},... | collective-permute-start | bytes 208904 | tf_op jit(solution)/shard_map/ppermute | solution.py:347
  10.1 0.9 %copy-start.1 = (f32[136,128]{1,0:T(8,128)S(1)}, f32[136,128]{1,0:T(8,128)}, u32[]{:S(2)}) copy-start(f32[136,128]{1,0:T(8,128)} %shard_map.64.message_ref) | copy-start | bytes 208900
  13.0 2.8 %collective-permute-start.2 = (f32[2,136,128]{2,1,0:T(8,128)S(1)}, f32[2,136,128]{2,1,0:T(8,128)S(1)}, u32[]{:S(2)}, u32[]{:S(2)}) collective-permute-start(f32[2,136,128]{2,1,0:T(8,128)S(1)} %shard_map.66.near_ref), channel_id=1, source_target_pairs={{0,1},{1,0},{2,3},{3,2},{4,5},{5,4},{6,7},{7,6},{8,9},{9,8},{10,11... | collective-permute-start | bytes 417800 | tf_op jit(solution)/shard_map/ppermute | solution.py:347
  13.0 6.1 %collective-permute-start.1 = (f32[2,136,128]{2,1,0:T(8,128)S(1)}, f32[2,136,128]{2,1,0:T(8,128)S(1)}, u32[]{:S(2)}, u32[]{:S(2)}) collective-permute-start(f32[2,136,128]{2,1,0:T(8,128)S(1)} %shard_map.66.near_ref), channel_id=1, source_target_pairs={{0,4},{1,5},{2,6},{3,7},{4,0},{5,1},{6,2},{7,3},{8,12},{9,13},{10,... | collective-permute-start | bytes 417800 | tf_op jit(solution)/shard_map/ppermute | solution.py:347
  13.6 5.6 %collective-permute-start.4 = (f32[136,128]{1,0:T(8,128)S(1)}, f32[136,128]{1,0:T(8,128)S(1)}, u32[]{:S(2)}, u32[]{:S(2)}) collective-permute-start(f32[136,128]{1,0:T(8,128)S(1)} %collective-permute-done.3), channel_id=1, source_target_pairs={{0,2},{1,3},{2,0},{3,1},{4,6},{5,7},{6,4},{7,5},{8,10},{9,11},{10,... | collective-permute-start | bytes 208904 | tf_op jit(solution)/shard_map/ppermute | solution.py:347
  15.2 4.3 %collective-permute-start.6 = (f32[136,128]{1,0:T(8,128)S(1)}, f32[136,128]{1,0:T(8,128)S(1)}, u32[]{:S(2)}, u32[]{:S(2)}) collective-permute-start(f32[136,128]{1,0:T(8,128)S(1)} %collective-permute-done.5), channel_id=1, source_target_pairs={{0,2},{1,3},{2,0},{3,1},{4,6},{5,7},{6,4},{7,5},{8,10},{9,11},{10,... | collective-permute-start | bytes 208904 | tf_op jit(solution)/shard_map/ppermute | solution.py:347
  19.1 1.4 %collective-permute-start.7 = (f32[2,136,128]{2,1,0:T(8,128)S(1)}, f32[2,136,128]{2,1,0:T(8,128)S(1)}, u32[]{:S(2)}, u32[]{:S(2)}) collective-permute-start(f32[2,136,128]{2,1,0:T(8,128)S(1)} %shard_map.68), channel_id=1, source_target_pairs={{0,1},{1,0},{2,3},{3,2},{4,5},{5,4},{6,7},{7,6},{8,9},{9,8},{10,11... | collective-permute-start | bytes 417800 | tf_op jit(solution)/shard_map/ppermute | solution.py:347
  19.6 4.1 %collective-permute-start.8 = (f32[4,136,128]{2,1,0:T(8,128)S(1)}, f32[4,136,128]{2,1,0:T(8,128)S(1)}, u32[]{:S(2)}, u32[]{:S(2)}) collective-permute-start(f32[4,136,128]{2,1,0:T(8,128)S(1)} %pad_maximum_fusion.1), channel_id=1, source_target_pairs={{0,1},{1,0},{2,3},{3,2},{4,5},{5,4},{6,7},{7,6},{8,9},{9,8},{10,11... | collective-permute-start | bytes 835592 | tf_op jit(solution)/shard_map/ppermute | solution.py:347
  23.9 7.1 %copy-start.2 = (f32[1,128,128]{2,1,0:T(8,128)S(1)}, f32[1,128,128]{2,1,0:T(8,128)}, u32[]{:S(2)}) copy-start(f32[1,128,128]{2,1,0:T(8,128)} %refs_2_.1) | copy-start | bytes 196612
  29.7 1.3 %collective-permute-start.9 = (f32[128,128]{1,0:T(8,128)S(1)}, f32[128,128]{1,0:T(8,128)S(1)}, u32[]{:S(2)}, u32[]{:S(2)}) collective-permute-start(f32[128,128]{1,0:T(8,128)S(1)} %get-tuple-element.72.refs_0_), channel_id=1, source_target_pairs={{0,1},{1,0},{2,3},{3,2},{4,5},{5,4},{6,7},{7,6},{8,9},{9,8},{10,11... | collective-permute-start | bytes 196616 | tf_op jit(solution)/shard_map/ppermute | solution.py:347
  39.3 4.6 %copy-start.3 = (s32[1,2]{1,0:T(1,128)S(1)}, s32[1,2]{1,0:T(1,128)}, u32[]{:S(2)}) copy-start(s32[1,2]{1,0:T(1,128)} %offsets_ref.1) | copy-start | bytes 28
  42.5 1.3 %collective-permute-start.10 = (f32[128,128]{1,0:T(8,128)S(1)}, f32[128,128]{1,0:T(8,128)S(1)}, u32[]{:S(2)}, u32[]{:S(2)}) collective-permute-start(f32[128,128]{1,0:T(8,128)S(1)} %get-tuple-element.79), channel_id=1, source_target_pairs={{0,1},{1,0},{2,3},{3,2},{4,5},{5,4},{6,7},{7,6},{8,9},{9,8},{10,11... | collective-permute-start | bytes 196616 | tf_op jit(solution)/shard_map/ppermute | solution.py:347
